TPU v7x, 32 devices: a whole 2x2x4 slice. The times are simulated.
32 devices in a mesh: heads: 4 (over y, core), blk: 8 (over z, x).
Axes of the slice: x: 2, y: 2, z: 4, core: 2. Of those that a mesh axis runs over, the one named last changes fastest.
Arguments:
- tokens: bfloat16 [4096, 2304], P(('blk', 'heads')), may hold values from -6 to 6
- cotangent: bfloat16 [4096, 2304], P(('blk', 'heads')), may hold values from -6 to 6
- norm_attn_in: float32 [2304], replicated, may hold values from -0.5 to 0.5
- w_query: bfloat16 [2304, 2048], P('blk', 'heads'), may hold values from -0.125 to 0.125
- w_key: bfloat16 [2304, 1024], P('blk', 'heads'), may hold values from -0.125 to 0.125
- w_value: bfloat16 [2304, 1024], P('blk', 'heads'), may hold values from -0.125 to 0.125
- w_out: bfloat16 [2048, 2304], P('heads', 'blk'), may hold values from -0.125 to 0.125
- norm_attn_out: float32 [2304], replicated, may hold values from -0.5 to 0.5
- norm_ff_in: float32 [2304], replicated, may hold values from -0.5 to 0.5
- w_gate: bfloat16 [2304, 9216], P('blk', 'heads'), may hold values from -0.125 to 0.125
- w_up: bfloat16 [2304, 9216], P('blk', 'heads'), may hold values from -0.125 to 0.125
- w_down: bfloat16 [9216, 2304], P('heads', 'blk'), may hold values from -0.0625 to 0.0625
- norm_ff_out: float32 [2304], replicated, may hold values from -0.5 to 0.5
- block_group: int32 [8], replicated, may hold values from 0 to 1, as said below
- block_role: int32 [8], replicated, may hold values from 0 to 3, as said below
Outputs:
- layer_out: bfloat16 [4096, 2304], P(('blk', 'heads'))
- input_grad: bfloat16 [4096, 2304], P(('blk', 'heads'))
- grad_norm_attn_in: float32 [2304], replicated
- grad_w_query: float32 [2304, 2048], P('blk', 'heads')
- grad_w_key: float32 [2304, 1024], P('blk', 'heads')
- grad_w_value: float32 [2304, 1024], P('blk', 'heads')
- grad_w_out: float32 [2048, 2304], P('heads', 'blk')
- grad_norm_attn_out: float32 [2304], replicated
- grad_norm_ff_in: float32 [2304], replicated
- grad_w_gate: float32 [2304, 9216], P('blk', 'heads')
- grad_w_up: float32 [2304, 9216], P('blk', 'heads')
- grad_w_down: float32 [9216, 2304], P('heads', 'blk')
- grad_norm_ff_out: float32 [2304], replicated
Inputs may be any that keep to these rules, and one draw needn't show every extreme that they name: `block_group`: two groups of 4 blocks each; the first and the last block belong to the same group. `block_role`: within each group the roles are a permutation of 0 to 3; roles under 2 are the group's prompt blocks in order, the others its continuations.
All inputs are finite; a program needn't handle non-finite values.
Results may differ from a plain program's by a relative error of at most 0.03.
Values may be sent and summed in bfloat16 or wider, within the bound.
A program may use at most 192 MiB of HBM per device.

v0:
```python
import math

import jax
import jax.numpy as jnp
from jax import lax
from jax.sharding import PartitionSpec as P

HEAD_DIM = 256


softcap = 50.0
epsilon = 1e-06
masked_low = -1e30


def normalize(values, weight_gain):
    factor = lax.rsqrt(jnp.mean(values * values, axis=-1, keepdims=True) + epsilon)
    return values * factor * (1.0 + weight_gain)


def rope_tables(positions):
    half_dim = HEAD_DIM // 2
    frequency = jnp.exp(
        jnp.arange(half_dim, dtype=jnp.float32) * (-2.0 * math.log(10000.0) / HEAD_DIM)
    )
    angles = positions.astype(jnp.float32)[:, None] * frequency[None, :]
    return (jnp.cos(angles), jnp.sin(angles))


def rotate(tensor, cosine, sine_table):
    half_dim = tensor.shape[-1] // 2
    first_half = tensor[..., :half_dim]
    second_half = tensor[..., half_dim:]
    cos_wide = cosine[:, None, :]
    sin_wide = sine_table[:, None, :]
    return jnp.concatenate(
        [
            first_half * cos_wide - second_half * sin_wide,
            second_half * cos_wide + first_half * sin_wide,
        ],
        axis=-1,
    )


def contract(left_side, right_side, left_dim, right_dim):
    return lax.dot_general(
        left_side,
        right_side,
        (((left_dim,), (right_dim,)), ((), ())),
        preferred_element_type=jnp.float32,
    )


def to_block(row_part):
    return lax.all_gather(row_part, "heads", axis=0, tiled=True)


def from_block(partial_sum):
    return lax.psum_scatter(
        partial_sum.astype(jnp.bfloat16), "heads", scatter_dimension=0, tiled=True
    ).astype(jnp.float32)


def on_device(
    tokens,
    cotangent,
    norm_attn_in,
    w_query,
    w_key,
    w_value,
    w_out,
    norm_attn_out,
    norm_ff_in,
    w_gate,
    w_up,
    w_down,
    norm_ff_out,
    block_group,
    block_role,
):
    own_rows = tokens.shape[0]
    block_len = own_rows * lax.axis_size("heads")
    blocks = lax.axis_size("blk")
    prompt_len = blocks // 4
    score_scale = HEAD_DIM ** (-0.5)
    my_block = lax.axis_index("blk")
    block_ids = jnp.arange(blocks, dtype=jnp.int32)
    my_group = jnp.sum(jnp.where(block_ids == my_block, block_group, 0))
    my_role = jnp.sum(jnp.where(block_ids == my_block, block_role, 0))
    offsets = jnp.arange(block_len, dtype=jnp.int32)
    positions = (
        jnp.where(my_role < prompt_len, my_role * block_len, prompt_len * block_len) + offsets
    )
    cosine, sine_table = rope_tables(positions)

    def key_allowed(index_rows):
        block_of = index_rows // block_len
        matches = block_of[:, None] == block_ids[None, :]
        key_group = jnp.sum(jnp.where(matches, block_group[None, :], 0), axis=1)
        key_role = jnp.sum(jnp.where(matches, block_role[None, :], 0), axis=1)
        key_offset = index_rows % block_len
        prompt_part = (key_role[None, :] < prompt_len) & (key_role[None, :] < my_role)
        own_part = (key_role[None, :] == my_role) & (key_offset[None, :] <= offsets[:, None])
        return (key_group[None, :] == my_group) & (prompt_part | own_part)

    token_f32 = tokens.astype(jnp.float32)
    normed_one = to_block(normalize(token_f32, norm_attn_in).astype(jnp.bfloat16))
    shards = (w_query, w_key, w_value, w_out, w_gate, w_up, w_down)
    query_full, key_full, value_full, out_full, gate_full, up_full, down_full = (
        lax.all_gather(shards[0], "blk", axis=0, tiled=True),
        lax.all_gather(shards[1], "blk", axis=0, tiled=True),
        lax.all_gather(shards[2], "blk", axis=0, tiled=True),
        lax.all_gather(shards[3], "blk", axis=1, tiled=True),
        lax.all_gather(shards[4], "blk", axis=0, tiled=True),
        lax.all_gather(shards[5], "blk", axis=0, tiled=True),
        lax.all_gather(shards[6], "blk", axis=1, tiled=True),
    )
    head_count = query_full.shape[1] // HEAD_DIM
    query_lin = jnp.dot(normed_one, query_full, preferred_element_type=jnp.float32)
    key_lin = jnp.dot(normed_one, key_full, preferred_element_type=jnp.float32)
    value_rows = jnp.dot(normed_one, value_full, preferred_element_type=jnp.float32).astype(
        jnp.bfloat16
    )
    queries = rotate(query_lin.reshape(block_len, head_count, HEAD_DIM), cosine, sine_table).astype(
        jnp.bfloat16
    )
    key_rows = (
        rotate(key_lin.reshape(block_len, 1, HEAD_DIM), cosine, sine_table)
        .reshape(block_len, HEAD_DIM)
        .astype(jnp.bfloat16)
    )
    start_state = (
        jnp.full((block_len, head_count), masked_low, jnp.float32),
        jnp.zeros((block_len, head_count), jnp.float32),
        jnp.zeros((block_len, head_count, HEAD_DIM), jnp.float32),
    )
    running = start_state
    piece_keys = lax.all_gather(key_rows, "blk", axis=0, tiled=True)
    piece_values = lax.all_gather(value_rows, "blk", axis=0, tiled=True)
    piece_rows = piece_keys.shape[0]
    part_rows = math.gcd(piece_rows, block_len)
    part_count = piece_rows // part_rows
    split_keys = piece_keys.reshape(part_count, part_rows, HEAD_DIM)
    split_values = piece_values.reshape(part_count, part_rows, HEAD_DIM)
    starts = jnp.arange(part_count, dtype=jnp.int32) * part_rows

    def one_part(state_now, packed):
        part_keys, part_values, part_start = packed
        allowed = key_allowed(part_start + jnp.arange(part_rows, dtype=jnp.int32))[:, None, :]

        def update(state_old):
            top_old, total_old, accum_old = state_old
            raw_scores = jnp.einsum(
                "qhd,kd->qhk", queries, part_keys, preferred_element_type=jnp.float32
            )
            capped = softcap * jnp.tanh(raw_scores * score_scale / softcap)
            top_new = jnp.maximum(top_old, jnp.max(jnp.where(allowed, capped, masked_low), axis=-1))
            shrink = jnp.exp(top_old - top_new)
            weights = jnp.where(allowed, jnp.exp(capped - top_new[..., None]), 0.0)
            total_new = total_old * shrink + jnp.sum(weights, axis=-1)
            accum_new = accum_old * shrink[..., None] + jnp.einsum(
                "qhk,kd->qhd",
                weights.astype(jnp.bfloat16),
                part_values,
                preferred_element_type=jnp.float32,
            )
            return (top_new, total_new, accum_new)

        return (lax.cond(jnp.any(allowed), update, lambda state_old: state_old, state_now), None)

    running, _ = lax.scan(one_part, running, (split_keys, split_values, starts))
    top_final, total_final, accum_final = running
    attended = accum_final / total_final[..., None]
    log_total = top_final + jnp.log(total_final)
    attn_rows = attended.reshape(block_len, head_count * HEAD_DIM).astype(jnp.bfloat16)
    attn_proj = from_block(jnp.dot(attn_rows, out_full, preferred_element_type=jnp.float32))
    middle = token_f32 + normalize(attn_proj, norm_attn_out)
    normed_two = to_block(normalize(middle, norm_ff_in).astype(jnp.bfloat16))
    gate_lin = jnp.dot(normed_two, gate_full, preferred_element_type=jnp.float32)
    up_lin = jnp.dot(normed_two, up_full, preferred_element_type=jnp.float32)
    hidden = (jax.nn.gelu(gate_lin, approximate=True) * up_lin).astype(jnp.bfloat16)
    ff_proj = from_block(jnp.dot(hidden, down_full, preferred_element_type=jnp.float32))
    layer_out = middle + normalize(ff_proj, norm_ff_out)
    upstream = cotangent.astype(jnp.float32)
    _, last_back = jax.vjp(normalize, ff_proj, norm_ff_out)
    d_ff, grad_ff_out = last_back(upstream)
    d_ff_rows = to_block(d_ff.astype(jnp.bfloat16))
    query_full, key_full, value_full, out_full, gate_full, up_full, down_full = (
        lax.all_gather(shards[0], "blk", axis=0, tiled=True),
        lax.all_gather(shards[1], "blk", axis=0, tiled=True),
        lax.all_gather(shards[2], "blk", axis=0, tiled=True),
        lax.all_gather(shards[3], "blk", axis=1, tiled=True),
        lax.all_gather(shards[4], "blk", axis=0, tiled=True),
        lax.all_gather(shards[5], "blk", axis=0, tiled=True),
        lax.all_gather(shards[6], "blk", axis=1, tiled=True),
    )
    d_hidden = contract(d_ff_rows, down_full, 1, 1)
    grad_down = contract(hidden, d_ff_rows, 0, 0)
    _, glu_back = jax.vjp(
        lambda gate_in, up_in: jax.nn.gelu(gate_in, approximate=True) * up_in, gate_lin, up_lin
    )
    d_gate, d_up = glu_back(d_hidden)
    d_gate = d_gate.astype(jnp.bfloat16)
    d_up = d_up.astype(jnp.bfloat16)
    grad_gate = contract(normed_two, d_gate, 0, 0)
    grad_up = contract(normed_two, d_up, 0, 0)
    d_normed_two = from_block(contract(d_gate, gate_full, 1, 1) + contract(d_up, up_full, 1, 1))
    _, middle_back = jax.vjp(normalize, middle, norm_ff_in)
    d_middle_part, grad_ff_in = middle_back(d_normed_two)
    d_middle = upstream + d_middle_part
    _, proj_back = jax.vjp(normalize, attn_proj, norm_attn_out)
    d_proj, grad_attn_out = proj_back(d_middle)
    d_proj_rows = to_block(d_proj.astype(jnp.bfloat16))
    d_attended = (
        contract(d_proj_rows, out_full, 1, 1)
        .astype(jnp.bfloat16)
        .reshape(block_len, head_count, HEAD_DIM)
    )
    grad_out = contract(attn_rows, d_proj_rows, 0, 0)
    row_delta = jnp.sum(d_attended.astype(jnp.float32) * attended, axis=-1)
    all_keys, all_values = (
        lax.all_gather(key_rows, "blk", axis=0, tiled=True),
        lax.all_gather(value_rows, "blk", axis=0, tiled=True),
    )
    key_span = 2 * block_len
    turn_count = blocks // 2
    split_keys = all_keys.reshape(turn_count, key_span, HEAD_DIM)
    split_values = all_values.reshape(turn_count, key_span, HEAD_DIM)
    firsts = jnp.arange(turn_count, dtype=jnp.int32) * key_span

    def back_part(query_acc, packed):
        part_keys, part_values, part_start = packed
        allowed = key_allowed(part_start + jnp.arange(key_span, dtype=jnp.int32))[:, None, :]

        def work_part(acc_in):
            raw_scores = jnp.einsum(
                "qhd,kd->qhk", queries, part_keys, preferred_element_type=jnp.float32
            )
            bounded = jnp.tanh(raw_scores * score_scale / softcap)
            capped = softcap * bounded
            probabilities = jnp.where(allowed, jnp.exp(capped - log_total[..., None]), 0.0)
            d_probs = jnp.einsum(
                "qhd,kd->qhk", d_attended, part_values, preferred_element_type=jnp.float32
            )
            d_capped = probabilities * (d_probs - row_delta[..., None])
            d_raw = (d_capped * (1.0 - bounded * bounded) * score_scale).astype(jnp.bfloat16)
            acc_out = acc_in + jnp.einsum(
                "qhk,kd->qhd", d_raw, part_keys, preferred_element_type=jnp.float32
            )
            d_key_part = jnp.einsum(
                "qhk,qhd->kd", d_raw, queries, preferred_element_type=jnp.float32
            )
            d_value_part = jnp.einsum(
                "qhk,qhd->kd",
                probabilities.astype(jnp.bfloat16),
                d_attended,
                preferred_element_type=jnp.float32,
            )
            return (acc_out, d_key_part, d_value_part)

        def skip_part(acc_in):
            empty_rows = jnp.zeros((key_span, HEAD_DIM), jnp.float32)
            return (acc_in, empty_rows, empty_rows)

        acc_out, d_key_part, d_value_part = lax.cond(
            jnp.any(allowed), work_part, skip_part, query_acc
        )
        return (acc_out, (d_key_part, d_value_part))

    d_query, (d_key_parts, d_value_parts) = lax.scan(
        back_part,
        jnp.zeros((block_len, head_count, HEAD_DIM), jnp.float32),
        (split_keys, split_values, firsts),
    )
    d_key_mine, d_value_mine = (
        lax.psum_scatter(
            d_key_parts.reshape(blocks * block_len, HEAD_DIM).astype(jnp.bfloat16),
            "blk",
            scatter_dimension=0,
            tiled=True,
        ).astype(jnp.float32),
        lax.psum_scatter(
            d_value_parts.reshape(blocks * block_len, HEAD_DIM).astype(jnp.bfloat16),
            "blk",
            scatter_dimension=0,
            tiled=True,
        ).astype(jnp.float32),
    )
    d_query_lin = (
        rotate(d_query, cosine, -sine_table)
        .reshape(block_len, head_count * HEAD_DIM)
        .astype(jnp.bfloat16)
    )
    d_key_lin = (
        rotate(d_key_mine.reshape(block_len, 1, HEAD_DIM), cosine, -sine_table)
        .reshape(block_len, HEAD_DIM)
        .astype(jnp.bfloat16)
    )
    d_value_lin = d_value_mine.astype(jnp.bfloat16)
    grad_query = contract(normed_one, d_query_lin, 0, 0)
    grad_key = contract(normed_one, d_key_lin, 0, 0)
    grad_value = contract(normed_one, d_value_lin, 0, 0)
    d_normed_one = from_block(
        contract(d_query_lin, query_full, 1, 1)
        + contract(d_key_lin, key_full, 1, 1)
        + contract(d_value_lin, value_full, 1, 1)
    )
    _, first_back = jax.vjp(normalize, token_f32, norm_attn_in)
    d_token_part, grad_attn_in = first_back(d_normed_one)
    input_grad = (d_middle + d_token_part).astype(jnp.bfloat16)
    row_sums = (
        lax.psum_scatter(
            grad_query.astype(jnp.bfloat16), "blk", scatter_dimension=0, tiled=True
        ).astype(jnp.float32),
        lax.psum_scatter(
            grad_key.astype(jnp.bfloat16), "blk", scatter_dimension=0, tiled=True
        ).astype(jnp.float32),
        lax.psum_scatter(
            grad_value.astype(jnp.bfloat16), "blk", scatter_dimension=0, tiled=True
        ).astype(jnp.float32),
        lax.psum_scatter(
            grad_gate.astype(jnp.bfloat16), "blk", scatter_dimension=0, tiled=True
        ).astype(jnp.float32),
        lax.psum_scatter(
            grad_up.astype(jnp.bfloat16), "blk", scatter_dimension=0, tiled=True
        ).astype(jnp.float32),
    )
    column_sums = (
        lax.psum_scatter(
            grad_out.astype(jnp.bfloat16), "blk", scatter_dimension=1, tiled=True
        ).astype(jnp.float32),
        lax.psum_scatter(
            grad_down.astype(jnp.bfloat16), "blk", scatter_dimension=1, tiled=True
        ).astype(jnp.float32),
    )
    gain_sums = lax.psum((grad_attn_in, grad_attn_out, grad_ff_in, grad_ff_out), ("heads", "blk"))
    return (
        layer_out.astype(jnp.bfloat16),
        input_grad,
        gain_sums[0],
        row_sums[0],
        row_sums[1],
        row_sums[2],
        column_sums[0],
        gain_sums[1],
        gain_sums[2],
        row_sums[3],
        row_sums[4],
        column_sums[1],
        gain_sums[3],
    )


def solution(mesh):
    return jax.shard_map(
        on_device,
        mesh=mesh,
        in_specs=(
            P(("blk", "heads"), None),
            P(("blk", "heads"), None),
            P(),
            P("blk", "heads"),
            P("blk", "heads"),
            P("blk", "heads"),
            P("heads", "blk"),
            P(),
            P(),
            P("blk", "heads"),
            P("blk", "heads"),
            P("heads", "blk"),
            P(),
            P(),
            P(),
        ),
        out_specs=(
            P(("blk", "heads"), None),
            P(("blk", "heads"), None),
            P(),
            P("blk", "heads"),
            P("blk", "heads"),
            P("blk", "heads"),
            P("heads", "blk"),
            P(),
            P(),
            P("blk", "heads"),
            P("blk", "heads"),
            P("heads", "blk"),
            P(),
        ),
        check_vma=False,
    )
```

profile of v0, /device:TPU:2, one launch (start us, length us, event | category | flops | bytes accessed | tf_op | source)
XLA Modules:
  0.0 2119.9 jit_solution(11596717691491346607)
XLA Ops:
  16.0 35.6 %all-gather.17.cloned.1.call-done = bf16[2304,256]{1,0:T(8,128)(2,1)} async-done(((bf16[288,256]{1,0:T(8,128)(2,1)}), bf16[2304,256]{1,0:T(8,128)(2,1)}) %all-gather.17.cloned.1.call-update) | async-done | bytes 1179664 | tf_op jit(solution)/shard_map/all_gather | solution.py:111
  51.6 25.9 %all-gather.15.cloned.1.call-done = bf16[512,2304]{1,0:T(8,128)(2,1)} async-done(((bf16[128,2304]{1,0:T(8,128)(2,1)}), bf16[512,2304]{1,0:T(8,128)(2,1)}) %all-gather.15.cloned.1.call-update) | async-done | bytes 2359312 | tf_op jit(solution)/shard_map/all_gather | solution.py:55
  77.5 2.8 convolution_bitcast_fusion.1
  82.3 37.6 %all-gather.21.cloned.1.call-done = bf16[2304,256]{1,0:T(8,128)(2,1)} async-done(((bf16[288,256]{1,0:T(8,128)(2,1)}), bf16[2304,256]{1,0:T(8,128)(2,1)}) %all-gather.21.cloned.1.call-update) | async-done | bytes 1179664 | tf_op jit(solution)/shard_map/all_gather | solution.py:112
  119.9 3.5 convolution_convert_fusion.10
  126.7 46.1 %all-gather.19.cloned.1.call-done = bf16[2304,512]{1,0:T(8,128)(2,1)} async-done(((bf16[288,512]{1,0:T(8,128)(2,1)}), bf16[2304,512]{1,0:T(8,128)(2,1)}) %all-gather.19.cloned.1.call-update) | async-done | bytes 2359312 | tf_op jit(solution)/shard_map/all_gather | solution.py:110
  172.8 3.8 fusion.140
  177.1 48.7 %all-gather.39.cloned.1.call-done = bf16[4096,1,256]{0,2,1:T(8,128)(2,1)} async-done(((bf16[512,1,256]{0,2,1:T(8,128)(2,1)}), bf16[4096,1,256]{0,2,1:T(8,128)(2,1)}) %all-gather.39.cloned.1.call-update) | async-done | bytes 2097168 | tf_op jit(solution)/shard_map/all_gather | solution.py:138
  225.8 3.3 copy.61
  229.1 45.9 %all-gather.23.cloned.1.call-done = bf16[4096,256]{1,0:T(8,128)(2,1)} async-done(((bf16[512,256]{1,0:T(8,128)(2,1)}), bf16[4096,256]{1,0:T(8,128)(2,1)}) %all-gather.23.cloned.1.call-update) | async-done | bytes 2097168 | tf_op jit(solution)/shard_map/all_gather | solution.py:139
  276.0 45.5 %while.37 = (s32[]{:T(128)}, f32[512,2]{0,1:T(2,128)S(1)}, f32[512,2]{0,1:T(2,128)S(1)}, f32[512,2,256]{2,0,1:T(8,128)}, s32[8]{0:T(128)S(1)}, /*index=5*/s32[8]...) while((s32[]{:T(128)}, f32[512,2]{0,1:T(2,128)S(1)}, ...), condition=%wide.region_11.12_spmd.clone, body=%wide.region_3.11_spmd.clone.sunk | while | flops 546084352 | bytes 18960276 | solution.py:171
  286.3 4.4 conditional.6
  321.5 3.3 copy.52
  327.6 4.5 convolution_convert_fusion.6
  332.9 40.1 %reduce-scatter.14.cloned.1.call-done = bf16[128,2304]{1,0:T(8,128)(2,1)} async-done(((bf16[512,2304]{1,0:T(8,128)(2,1)}), bf16[128,2304]{1,0:T(8,128)(2,1)}) %reduce-scatter.14.cloned.1.call-update) | async-done | bytes 589840 | tf_op jit(solution)/shard_map/reduce_scatter | solution.py:59
  375.7 2.3 multiply_convert_fusion.2
  380.2 22.1 %all-gather.27.cloned.1.call-done = bf16[512,2304]{1,0:T(8,128)(2,1)} async-done(((bf16[128,2304]{1,0:T(8,128)(2,1)}), bf16[512,2304]{1,0:T(8,128)(2,1)}) %all-gather.27.cloned.1.call-update) | async-done | bytes 2359312 | tf_op jit(solution)/shard_map/all_gather | solution.py:55
  402.2 153.8 %all-gather.29.cloned.1.call-done = bf16[2304,2304]{1,0:T(8,128)(2,1)} async-done(((bf16[288,2304]{1,0:T(8,128)(2,1)}), bf16[2304,2304]{1,0:T(8,128)(2,1)}) %all-gather.29.cloned.1.call-update) | async-done | bytes 10616848 | tf_op jit(solution)/shard_map/all_gather | solution.py:114
  556.1 11.6 fusion.141
  567.7 141.5 %all-gather.31.cloned.1.call-done = bf16[2304,2304]{1,0:T(8,128)(2,1)} async-done(((bf16[288,2304]{1,0:T(8,128)(2,1)}), bf16[2304,2304]{1,0:T(8,128)(2,1)}) %all-gather.31.cloned.1.call-update) | async-done | bytes 10616848 | tf_op jit(solution)/shard_map/all_gather | solution.py:115
  709.2 12.8 multiply_convert_fusion.1
  722.0 140.1 %all-gather.33.cloned.1.call-done = bf16[2304,2304]{0,1:T(8,128)(2,1)} async-done(((bf16[2304,288]{0,1:T(8,128)(2,1)}), bf16[2304,2304]{0,1:T(8,128)(2,1)}) %all-gather.33.cloned.1.call-update) | async-done | bytes 10616848 | tf_op jit(solution)/shard_map/all_gather | solution.py:116
  862.1 11.3 convolution_convert_fusion.5
  874.1 31.6 %reduce-scatter.16.cloned.1.call-done = bf16[128,2304]{1,0:T(8,128)(2,1)} async-done(((bf16[512,2304]{1,0:T(8,128)(2,1)}), bf16[128,2304]{1,0:T(8,128)(2,1)}) %reduce-scatter.16.cloned.1.call-update) | async-done | bytes 589840 | tf_op jit(solution)/shard_map/reduce_scatter | solution.py:59
  907.0 2.3 fusion.97
  912.1 23.8 %all-gather.35.cloned.1.call-done = bf16[512,2304]{1,0:T(8,128)(2,1)} async-done(((bf16[128,2304]{1,0:T(8,128)(2,1)}), bf16[512,2304]{1,0:T(8,128)(2,1)}) %all-gather.35.cloned.1.call-update) | async-done | bytes 2359312 | tf_op jit(solution)/shard_map/all_gather | solution.py:55
  935.9 15.3 multiply_convert_fusion
  951.2 12.3 fusion.142
  963.6 9.2 fusion.81
  972.8 33.2 %reduce-scatter.18.cloned.1.call-done = bf16[128,2304]{1,0:T(8,128)(2,1)} async-done(((bf16[512,2304]{1,0:T(8,128)(2,1)}), bf16[128,2304]{1,0:T(8,128)(2,1)}) %reduce-scatter.18.cloned.1.call-update) | async-done | bytes 589840 | tf_op jit(solution)/shard_map/reduce_scatter | solution.py:59
  1007.7 3.1 fusion.93
  1013.3 24.0 %all-gather.37.cloned.1.call-done = bf16[512,2304]{1,0:T(8,128)(2,1)} async-done(((bf16[128,2304]{1,0:T(8,128)(2,1)}), bf16[512,2304]{1,0:T(8,128)(2,1)}) %all-gather.37.cloned.1.call-update) | async-done | bytes 2359312 | tf_op jit(solution)/shard_map/all_gather | solution.py:55
  1037.2 3.8 multiply_reduce_fusion.1
  1042.1 42.8 %while.38 = (s32[]{:T(128)}, f32[512,2,256]{2,0,1:T(8,128)S(1)}, bf16[4,1024,256]{2,1,0:T(8,128)(2,1)}, bf16[4,1024,256]{2,1,0:T(8,128)(2,1)}, s32[4]{0:T(128)S(...) while((s32[]{:T(128)}, f32[512,2,256]{2,0,1:T(8,128)S(1)}, ...), condition=%wide.region_28.29_spmd.clone, body=%wide.region_22.28_spmd.clone.sunk | while | flops 2704088064 | bytes 33608592 | solution.py:270
  1045.4 2.7 fusion.197
  1048.7 9.4 conditional.7
  1050.7 3.6 fusion.30
  1063.1 2.7 fusion.197
  1071.5 2.7 fusion.197
  1079.8 2.7 fusion.197
  1084.9 4.1 copy.63
  1091.7 2.9 convolution_convert_fusion.4
  1096.3 3.9 convolution_convert_fusion.3
  1100.4 73.9 %reduce-scatter.20.cloned.1.call-done = bf16[512,256]{0,1:T(8,128)(2,1)} async-done(((bf16[4096,256]{0,1:T(8,128)(2,1)}), bf16[512,256]{0,1:T(8,128)(2,1)}) %reduce-scatter.20.cloned.1.call-update) | async-done | bytes 262160 | tf_op jit(solution)/shard_map/reduce_scatter | solution.py:276
  1177.2 3.7 convolution_convert_fusion.8
  1181.0 64.0 %reduce-scatter.22.cloned.1.call-done = bf16[512,256]{1,0:T(8,128)(2,1)} async-done(((bf16[4096,256]{1,0:T(8,128)(2,1)}), bf16[512,256]{1,0:T(8,128)(2,1)}) %reduce-scatter.22.cloned.1.call-update) | async-done | bytes 262160 | tf_op jit(solution)/shard_map/reduce_scatter | solution.py:282
  1245.0 2.8 convolution_convert_fusion.7
  1247.9 2.4 fusion.126
  1255.6 10.1 convolution_convert_fusion
  1267.4 10.0 convolution_convert_fusion.2
  1277.7 10.0 convolution_convert_fusion.1
  1287.9 29.0 %reduce-scatter.26.cloned.1.call-done = bf16[288,512]{1,0:T(8,128)(2,1)} async-done(((bf16[2304,512]{1,0:T(8,128)(2,1)}), bf16[288,512]{1,0:T(8,128)(2,1)}) %reduce-scatter.26.cloned.1.call-update) | async-done | bytes 294928 | tf_op jit(solution)/shard_map/reduce_scatter | solution.py:312
  1318.7 70.1 %reduce-scatter.32.cloned.1.call-done = bf16[512,288]{0,1:T(8,128)(2,1)} async-done(((bf16[512,2304]{0,1:T(8,128)(2,1)}), bf16[512,288]{0,1:T(8,128)(2,1)}) %reduce-scatter.32.cloned.1.call-update) | async-done | bytes 294928 | tf_op jit(solution)/shard_map/reduce_scatter | solution.py:329
  1390.6 65.6 %reduce-scatter.28.cloned.1.call-done = bf16[288,256]{1,0:T(8,128)(2,1)} async-done(((bf16[2304,256]{1,0:T(8,128)(2,1)}), bf16[288,256]{1,0:T(8,128)(2,1)}) %reduce-scatter.28.cloned.1.call-update) | async-done | bytes 147472 | tf_op jit(solution)/shard_map/reduce_scatter | solution.py:315
  1457.8 65.2 %reduce-scatter.30.cloned.1.call-done = bf16[288,256]{1,0:T(8,128)(2,1)} async-done(((bf16[2304,256]{1,0:T(8,128)(2,1)}), bf16[288,256]{1,0:T(8,128)(2,1)}) %reduce-scatter.30.cloned.1.call-update) | async-done | bytes 147472 | tf_op jit(solution)/shard_map/reduce_scatter | solution.py:318
  1524.7 34.1 %reduce-scatter.24.cloned.1.call-done = bf16[128,2304]{1,0:T(8,128)(2,1)} async-done(((bf16[512,2304]{1,0:T(8,128)(2,1)}), bf16[128,2304]{1,0:T(8,128)(2,1)}) %reduce-scatter.24.cloned.1.call-update) | async-done | bytes 589840 | tf_op jit(solution)/shard_map/reduce_scatter | solution.py:59
  1560.5 46.0 %all-reduce = (f32[2304]{0:T(1024)}, f32[2304]{0:T(1024)}, f32[2304]{0:T(1024)}, f32[2304]{0:T(1024)}) all-reduce(f32[2304]{0:T(1024)S(1)} %get-tuple-element.736, f32[2304]{0:T(1024)S(1)} %get-tuple-element.732, f32[2304]{0:T(1024)S(1)} %get-tuple-element.730, ...), channel_id=1, replica_groups=mesh['heads'=4,'blk'=8] {'heads','blk'}, use_global_device_ids=true, to_apply=%region_34.35 | all-reduce | flops 9216 | bytes 73728 | tf_op jit(solution)/shard_map/psum | solution.py:336
  1606.5 2.3 fusion.101
  1608.8 135.4 %reduce-scatter.38.cloned.1.call-done = bf16[2304,288]{0,1:T(8,128)(2,1)} async-done(((bf16[2304,2304]{0,1:T(8,128)(2,1)}), bf16[2304,288]{0,1:T(8,128)(2,1)}) %reduce-scatter.38.cloned.1.call-update) | async-done | bytes 1327120 | tf_op jit(solution)/shard_map/reduce_scatter | solution.py:332
  1744.3 3.0 convert_element_type.221
  1747.3 180.1 %reduce-scatter.34.cloned.1.call-done = bf16[288,2304]{1,0:T(8,128)(2,1)} async-done(((bf16[2304,2304]{1,0:T(8,128)(2,1)}), bf16[288,2304]{1,0:T(8,128)(2,1)}) %reduce-scatter.34.cloned.1.call-update) | async-done | bytes 1327120 | tf_op jit(solution)/shard_map/reduce_scatter | solution.py:321
  1927.4 3.0 convert_element_type.217
  1930.4 179.5 %reduce-scatter.36.cloned.1.call-done = bf16[288,2304]{1,0:T(8,128)(2,1)} async-done(((bf16[2304,2304]{1,0:T(8,128)(2,1)}), bf16[288,2304]{1,0:T(8,128)(2,1)}) %reduce-scatter.36.cloned.1.call-update) | async-done | bytes 1327120 | tf_op jit(solution)/shard_map/reduce_scatter | solution.py:324
  2109.9 3.0 convert_element_type.219
  (301 shorter events, 121.9 us)
Async XLA Ops:
  7.2 6.8 copy-start.24
  7.2 44.4 %all-gather.17.cloned.1.call-start = ((), (), s32[]{:S(2)}) async-start(), calls=%async_computation.14 | async-start | bytes 1327104 | tf_op jit(solution)/shard_map/all_gather | solution.py:111
  7.9 69.6 %all-gather.15.cloned.1.call-start = ((), (), s32[]{:S(2)}) async-start(), calls=%async_computation.13 | async-start | bytes 2949120 | tf_op jit(solution)/shard_map/all_gather | solution.py:55
  9.8 41.8 %copy-start.34 = (f32[128]{0:T(128)}, f32[128]{0:T(128)S(1)}, u32[]{:S(2)}) copy-start(f32[128]{0:T(128)S(1)} %fusion.130) | copy-start | bytes 1540
  10.5 41.1 %copy-start.22 = (f32[2304]{0:T(1024)}, f32[2304]{0:T(1024)S(1)}, u32[]{:S(2)}) copy-start(f32[2304]{0:T(1024)S(1)} %broadcast_add_fusion.3) | copy-start | bytes 27652
  12.6 107.2 %all-gather.21.cloned.1.call-start = ((), (), s32[]{:S(2)}) async-start(), calls=%async_computation.16 | async-start | bytes 1327104 | tf_op jit(solution)/shard_map/all_gather | solution.py:112
  13.4 159.4 %all-gather.19.cloned.1.call-start = ((), (), s32[]{:S(2)}) async-start(), calls=%async_computation.15 | async-start | bytes 2654208 | tf_op jit(solution)/shard_map/all_gather | solution.py:110
  14.0 211.8 %all-gather.39.cloned.1.call-start = ((), (), s32[]{:S(2)}) async-start(), calls=%async_computation.38 | async-start | bytes 2359296 | tf_op jit(solution)/shard_map/all_gather | solution.py:138
  16.0 108.2 %copy-start.32 = (f32[128]{0:T(128)}, f32[128]{0:T(128)S(1)}, u32[]{:S(2)}) copy-start(f32[128]{0:T(128)S(1)} %multiply_exponential_fusion) | copy-start | bytes 1540
  16.0 108.2 %copy-start.27 = (f32[512]{0:T(512)}, f32[512]{0:T(512)S(1)}, u32[]{:S(2)}) copy-start(f32[512]{0:T(512)S(1)} %add_convert_fusion.2) | copy-start | bytes 6148
  82.3 43.7 %copy-start.25 = (s32[8]{0:T(128)S(1)}, s32[8]{0:T(128)}, u32[]{:S(2)}) copy-start(s32[8]{0:T(128)} %param.36) | copy-start | bytes 100
  82.3 192.7 %all-gather.23.cloned.1.call-start = ((), (), s32[]{:S(2)}) async-start(), calls=%async_computation.17 | async-start | bytes 2359296 | tf_op jit(solution)/shard_map/all_gather | solution.py:139
  123.4 204.2 %all-gather.25.cloned.1.call-start = ((), (), s32[]{:S(2)}) async-start(), calls=%async_computation.18 | async-start | bytes 2654208 | tf_op jit(solution)/shard_map/all_gather | solution.py:113
  124.1 248.8 %reduce-scatter.14.cloned.1.call-start = ((), (), s32[]{:S(2)}) async-start(), calls=%async_computation.19 | async-start | bytes 2949120 | tf_op jit(solution)/shard_map/reduce_scatter | solution.py:59
  126.0 50.6 %copy-start.13 = (f32[512,128]{0,1:T(8,128)}, f32[512,128]{0,1:T(8,128)S(1)}, u32[]{:S(2)}) copy-start(f32[512,128]{0,1:T(8,128)S(1)} %get-tuple-element.824) | copy-start | bytes 786436
  286.3 1.4 copy-start.9
  321.5 10.6 copy-start.1
  326.1 1.5 copy-start.19
  332.1 42.1 %copy-start = (bf16[128,2304]{1,0:T(8,128)(2,1)S(1)}, bf16[128,2304]{1,0:T(8,128)(2,1)}, u32[]{:S(2)}) copy-start(bf16[128,2304]{1,0:T(8,128)(2,1)} %param.23) | copy-start | bytes 1769476
  332.2 70.1 %all-gather.27.cloned.1.call-start = ((), (), s32[]{:S(2)}) async-start(), calls=%async_computation.20 | async-start | bytes 2949120 | tf_op jit(solution)/shard_map/all_gather | solution.py:55
  378.0 178.1 %all-gather.29.cloned.1.call-start = ((), (), s32[]{:S(2)}) async-start(), calls=%async_computation.21 | async-start | bytes 11943936 | tf_op jit(solution)/shard_map/all_gather | solution.py:114
  378.6 330.6 %all-gather.31.cloned.1.call-start = ((), (), s32[]{:S(2)}) async-start(), calls=%async_computation.22 | async-start | bytes 11943936 | tf_op jit(solution)/shard_map/all_gather | solution.py:115
  379.3 482.8 %all-gather.33.cloned.1.call-start = ((), (), s32[]{:S(2)}) async-start(), calls=%async_computation.23 | async-start | bytes 11943936 | tf_op jit(solution)/shard_map/all_gather | solution.py:116
  379.9 525.9 %reduce-scatter.16.cloned.1.call-start = ((), (), s32[]{:S(2)}) async-start(), calls=%async_computation.24 | async-start | bytes 2949120 | tf_op jit(solution)/shard_map/reduce_scatter | solution.py:59
  873.4 33.6 %copy-start.8 = (bf16[128,2304]{1,0:T(8,128)(2,1)S(1)}, bf16[128,2304]{1,0:T(8,128)(2,1)}, u32[]{:S(2)}) copy-start(bf16[128,2304]{1,0:T(8,128)(2,1)} %param.24) | copy-start | bytes 1769476
  873.4 62.4 %all-gather.35.cloned.1.call-start = ((), (), s32[]{:S(2)}) async-start(), calls=%async_computation.25 | async-start | bytes 2949120 | tf_op jit(solution)/shard_map/all_gather | solution.py:55
  911.6 94.4 %reduce-scatter.18.cloned.1.call-start = ((), (), s32[]{:S(2)}) async-start(), calls=%async_computation.26 | async-start | bytes 2949120 | tf_op jit(solution)/shard_map/reduce_scatter | solution.py:59
  935.9 27.7 %slice-start = ((s8[10616832]{0:T(1024)(128)(4,1)}), s8[4194304]{0:T(1024)(128)(4,1)S(1)}, s32[]{:S(2)}) async-start(s8[10616832]{0:T(1024)(128)(4,1)} %bitcast.149), calls=%async_computation.39 | async-start | bytes 8388608
  935.9 27.7 %slice-start.1 = ((s8[10616832]{0:T(1024)(128)(4,1)}), s8[4194304]{0:T(1024)(128)(4,1)S(1)}, s32[]{:S(2)}) async-start(s8[10616832]{0:T(1024)(128)(4,1)} %bitcast.149), calls=%async_computation.40 | async-start | bytes 8388608
  951.2 12.3 copy-start.42
  951.2 12.3 slice-start.2
  972.7 33.3 %copy-start.2 = (bf16[128,2304]{1,0:T(8,128)(2,1)S(1)}, bf16[128,2304]{1,0:T(8,128)(2,1)}, u32[]{:S(2)}) copy-start(bf16[128,2304]{1,0:T(8,128)(2,1)} %reduce-scatter.14.cloned.1.call-done) | copy-start | bytes 1769476
  972.7 35.0 %copy-start.6 = (bf16[128,2304]{1,0:T(8,128)(2,1)S(1)}, bf16[128,2304]{1,0:T(8,128)(2,1)}, u32[]{:S(2)}) copy-start(bf16[128,2304]{1,0:T(8,128)(2,1)} %reduce-scatter.16.cloned.1.call-done) | copy-start | bytes 1769476
  972.7 64.5 %all-gather.37.cloned.1.call-start = ((), (), s32[]{:S(2)}) async-start(), calls=%async_computation.27 | async-start | bytes 2949120 | tf_op jit(solution)/shard_map/all_gather | solution.py:55
  1010.8 1.0 copy-start.4
  1010.8 26.4 %copy-start.7 = (f32[512,2,256]{0,2,1:T(8,128)S(1)}, f32[512,2,256]{0,2,1:T(8,128)}, u32[]{:S(2)}) copy-start(f32[512,2,256]{0,2,1:T(8,128)} %copy.52) | copy-start | bytes 3145732
  1013.0 161.3 %reduce-scatter.20.cloned.1.call-start = ((), (), s32[]{:S(2)}) async-start(), calls=%async_computation.28 | async-start | bytes 2359296 | tf_op jit(solution)/shard_map/reduce_scatter | solution.py:276
  1048.7 1.9 copy-start.3
  1048.8 1.9 copy-start.20
  1089.1 1.0 copy-start.16
  1089.1 155.9 %reduce-scatter.22.cloned.1.call-start = ((), (), s32[]{:S(2)}) async-start(), calls=%async_computation.29 | async-start | bytes 2359296 | tf_op jit(solution)/shard_map/reduce_scatter | solution.py:282
  1089.7 227.2 %reduce-scatter.26.cloned.1.call-start = ((), (), s32[]{:S(2)}) async-start(), calls=%async_computation.31 | async-start | bytes 2654208 | tf_op jit(solution)/shard_map/reduce_scatter | solution.py:312
  1090.1 1.7 copy-start.38
  1094.6 1.7 copy-start.11
  1094.6 294.2 %reduce-scatter.32.cloned.1.call-start = ((), (), s32[]{:S(2)}) async-start(), calls=%async_computation.34 | async-start | bytes 2654208 | tf_op jit(solution)/shard_map/reduce_scatter | solution.py:329
  1100.2 75.2 %copy-start.28 = (f32[512]{0:T(512)S(1)}, f32[512]{0:T(512)}, u32[]{:S(2)}) copy-start(f32[512]{0:T(512)} %copy-done.27) | copy-start | bytes 6148
  1100.2 75.2 %copy-start.33 = (f32[128]{0:T(128)S(1)}, f32[128]{0:T(128)}, u32[]{:S(2)}) copy-start(f32[128]{0:T(128)} %copy-done.32) | copy-start | bytes 1540
  1100.2 356.0 %reduce-scatter.28.cloned.1.call-start = ((), (), s32[]{:S(2)}) async-start(), calls=%async_computation.32 | async-start | bytes 1327104 | tf_op jit(solution)/shard_map/reduce_scatter | solution.py:315
  1177.2 67.8 %copy-start.39 = (bf16[512,2304]{1,0:T(8,128)(2,1)S(1)}, bf16[512,2304]{1,0:T(8,128)(2,1)}, u32[]{:S(2)}) copy-start(bf16[512,2304]{1,0:T(8,128)(2,1)} %all-gather.15.cloned.1.call-done) | copy-start | bytes 7077892
  1180.9 342.1 %reduce-scatter.30.cloned.1.call-start = ((), (), s32[]{:S(2)}) async-start(), calls=%async_computation.33 | async-start | bytes 1327104 | tf_op jit(solution)/shard_map/reduce_scatter | solution.py:318
  1247.8 2.4 copy-start.12
  1247.8 310.9 %reduce-scatter.24.cloned.1.call-start = ((), (), s32[]{:S(2)}) async-start(), calls=%async_computation.30 | async-start | bytes 2949120 | tf_op jit(solution)/shard_map/reduce_scatter | solution.py:59
  1250.3 1.5 copy-start.15
  1250.3 1.5 copy-start.21
  1254.0 1.7 copy-start.41
  1254.0 490.3 %reduce-scatter.38.cloned.1.call-start = ((), (), s32[]{:S(2)}) async-start(), calls=%async_computation.37 | async-start | bytes 11943936 | tf_op jit(solution)/shard_map/reduce_scatter | solution.py:332
  1265.7 1.7 copy-start.40
  1265.7 661.7 %reduce-scatter.34.cloned.1.call-start = ((), (), s32[]{:S(2)}) async-start(), calls=%async_computation.35 | async-start | bytes 11943936 | tf_op jit(solution)/shard_map/reduce_scatter | solution.py:321
  1277.4 832.5 %reduce-scatter.36.cloned.1.call-start = ((), (), s32[]{:S(2)}) async-start(), calls=%async_computation.36 | async-start | bytes 11943936 | tf_op jit(solution)/shard_map/reduce_scatter | solution.py:324
  1287.8 271.0 %copy-start.23 = (f32[2304]{0:T(1024)S(1)}, f32[2304]{0:T(1024)}, u32[]{:S(2)}) copy-start(f32[2304]{0:T(1024)} %copy-done.22) | copy-start | bytes 27652
  1287.8 270.9 %copy-start.35 = (f32[128]{0:T(128)S(1)}, f32[128]{0:T(128)}, u32[]{:S(2)}) copy-start(f32[128]{0:T(128)} %copy-done.34) | copy-start | bytes 1540
  1287.8 272.7 %copy-start.26 = (f32[2304]{0:T(1024)S(1)}, f32[2304]{0:T(1024)}, u32[]{:S(2)}) copy-start(f32[2304]{0:T(1024)} %get-tuple-element.734) | copy-start | bytes 27652
  1287.8 318.7 %copy-start.37 = (f32[128]{0:T(128)S(1)}, f32[128]{0:T(128)}, u32[]{:S(2)}) copy-start(f32[128]{0:T(128)} %copy-done.36) | copy-start | bytes 1540
  1287.8 318.7 %copy-start.5 = (f32[128,2304]{1,0:T(8,128)S(1)}, f32[128,2304]{1,0:T(8,128)}, u32[]{:S(2)}) copy-start(f32[128,2304]{1,0:T(8,128)} %copy-done.4) | copy-start | bytes 3538948
  (8 other events, 6.0 us)
Sparse Core Ops, SparseCore 0:
  10.2 41.3 all-gather.16
  53.7 23.7 all-gather.14
  79.7 40.1 all-gather.20
  121.9 50.8 all-gather.18
  175.3 50.4 all-gather.38
  228.4 46.5 all-gather.22
  277.2 50.4 all-gather.24
  332.3 40.6 reduce-scatter.13
  378.1 24.0 all-gather.26
  404.5 151.5 all-gather.28
  558.5 150.6 all-gather.30
  711.4 150.6 all-gather.32
  873.6 32.1 reduce-scatter.15
  911.7 24.0 all-gather.34
  972.9 33.0 reduce-scatter.17
  1013.1 24.0 all-gather.36
  1089.2 85.0 reduce-scatter.19
  1178.1 66.8 reduce-scatter.21
  1248.9 67.9 reduce-scatter.25
  1320.6 68.1 reduce-scatter.31
  1392.6 63.5 reduce-scatter.27
  1460.0 63.0 reduce-scatter.29
  1526.3 32.3 reduce-scatter.23
  1562.2 182.0 reduce-scatter.37
  1748.3 179.0 reduce-scatter.33
  1930.8 179.0 reduce-scatter.35
where the time goes:
time: 2130 us; the launch traced here: 2120 us
  waiting for transfers between devices  1750 us (82%)
  matrix products  152 us (7%)
  other arithmetic  103 us (5%)
  blocking collectives  46 us (2%)
  local copies, waits for them, and re-layouts  38.1 us (2%)
    reduce_scatter x1, waiting for transfers between devices, on_device(): lax.psum_scatter(grad_gate.astype(jnp.bfloat16), 'blk', scatter_dimension...  180 us
    reduce_scatter x1, waiting for transfers between devices, on_device(): lax.psum_scatter(grad_up.astype(jnp.bfloat16), 'blk', scatter_dimension=0...  180 us
    all_gather x1, waiting for transfers between devices, on_device(): lax.all_gather(shards[4], 'blk', axis=0, tiled=True)  154 us
    all_gather x1, waiting for transfers between devices, on_device(): lax.all_gather(shards[5], 'blk', axis=0, tiled=True)  141 us
    all_gather x1, waiting for transfers between devices, on_device(): lax.all_gather(shards[6], 'blk', axis=1, tiled=True)  140 us
    reduce_scatter x4, waiting for transfers between devices, from_block(): lax.psum_scatter(partial_sum.astype(jnp.bfloat16), 'heads', scatter_dimen...  139 us
    reduce_scatter x1, waiting for transfers between devices, on_device(): lax.psum_scatter(grad_down.astype(jnp.bfloat16), 'blk', scatter_dimension...  135 us
    all_gather x4, waiting for transfers between devices, to_block(): return lax.all_gather(row_part, 'heads', axis=0, tiled=True)  95.7 us
  transfers between devices with their start and end apart: 26, of which 26 were waited for; matrix products, arithmetic and copies ran while one was open for 8% of the time, Pallas kernels for 0%

commit v1 on v0

v1 whole, which is shorter than its diff:
```python
import functools
import math

import jax
import jax.numpy as jnp
from jax import lax
from jax.experimental import pallas as pl
from jax.experimental.pallas import tpu as pltpu
from jax.sharding import PartitionSpec as P

HEAD_DIM = 256


softcap = 50.0
epsilon = 1e-06
score_scale = HEAD_DIM ** (-0.5)
bf16 = jnp.bfloat16
f32 = jnp.float32


def contract(left_side, right_side, left_dim, right_dim):
    return lax.dot_general(
        left_side,
        right_side,
        (((left_dim,), (right_dim,)), ((), ())),
        preferred_element_type=f32,
    )


def factor_of(values):
    return lax.rsqrt(jnp.mean(values * values, axis=-1, keepdims=True) + epsilon)


def normalize(values, weight_gain):
    return values * factor_of(values) * (1.0 + weight_gain)


def normalize_back(values, weight_gain, upstream):
    factor = factor_of(values)
    unit = values * factor
    scaled = upstream * (1.0 + weight_gain)
    inner = jnp.mean(scaled * unit, axis=-1, keepdims=True)
    return (scaled - unit * inner) * factor, jnp.sum(upstream * unit, axis=0)


def rope_tables(positions):
    half_dim = HEAD_DIM // 2
    frequency = jnp.exp(
        jnp.arange(half_dim, dtype=f32) * (-2.0 * math.log(10000.0) / HEAD_DIM)
    )
    angles = positions.astype(f32)[:, None] * frequency[None, :]
    return (jnp.cos(angles), jnp.sin(angles))


def rotate(tensor, cosine, sine_table):
    half_dim = HEAD_DIM // 2
    first_half = tensor[..., :half_dim]
    second_half = tensor[..., half_dim:]
    return jnp.concatenate(
        [
            first_half * cosine - second_half * sine_table,
            second_half * cosine + first_half * sine_table,
        ],
        axis=-1,
    )


def swap_core(v):
    return lax.ppermute(v, "heads", [(i, i ^ 1) for i in range(4)])


def swap_y(v):
    return lax.ppermute(v, "heads", [(i, i ^ 2) for i in range(4)])


def swap_x(v):
    blocks = lax.axis_size("blk")
    return lax.ppermute(v, "blk", [(i, i ^ 1) for i in range(blocks)])


def pair_up(own, other, place, axis):
    first = jnp.where(place == 0, own, other)
    second = jnp.where(place == 0, other, own)
    return jnp.concatenate([first, second], axis=axis)


def shift_z(v, step, senders):
    pairs = []
    for z in senders:
        for x in range(2):
            pairs.append((2 * z + x, 2 * (z + step) + x))
    return lax.ppermute(v, "blk", pairs)


class Place:
    def __init__(self):
        self.blocks = lax.axis_size("blk")
        self.nz = self.blocks // 2
        self.b = lax.axis_index("blk")
        self.h = lax.axis_index("heads")
        self.z, self.x = self.b // 2, self.b % 2
        self.y, self.c = self.h // 2, self.h % 2


def gather_z(at, unit):
    nz = at.nz
    up, down = unit, unit
    ups, downs = [None], [None]
    for s in range(1, nz):
        up = shift_z(up, 1, range(s - 1, nz - 1))
        down = shift_z(down, -1, range(1, nz - s + 1))
        ups.append(up)
        downs.append(down)
    return [unit] + [jnp.where(at.z >= s, ups[s], downs[nz - s]) for s in range(1, nz)]


def scatter_z(at, parts):
    nz = at.nz
    up = down = None
    for t in range(1, nz):
        k = nz - t
        send_up = parts[nz - k].astype(f32)
        send_down = parts[k].astype(f32)
        if up is not None:
            send_up = send_up + up.astype(f32)
            send_down = send_down + down.astype(f32)
        up = shift_z(send_up.astype(bf16), 1, range(0, nz - k))
        down = shift_z(send_down.astype(bf16), -1, range(k, nz))
    return parts[0].astype(f32) + (up.astype(f32) + down.astype(f32))


def deal_z(at, parts):
    nz = at.nz
    got = [parts[0]]
    for s in range(1, nz):
        up = shift_z(parts[nz - s], s, range(0, nz - s))
        down = shift_z(parts[nz - s], s - nz, range(nz - s, nz))
        got.append(jnp.where(at.z >= s, up, down))
    return got


def turn(at, whole):
    return [
        lax.dynamic_index_in_dim(whole, (at.z - s) % at.nz, 0, keepdims=False)
        for s in range(at.nz)
    ]


def unturn(at, parts):
    whole = jnp.zeros((at.nz,) + parts[0].shape, parts[0].dtype)
    for s, part in enumerate(parts):
        whole = lax.dynamic_update_index_in_dim(whole, part, (at.z - s) % at.nz, 0)
    return whole


def gather_zx(at, unit):
    got = []
    for part in gather_z(at, unit):
        got.append(pair_up(part[None], swap_x(part)[None], at.x, 0))
    return unturn(at, got)


def gather_xz(at, unit):
    both = pair_up(unit[None], swap_x(unit)[None], at.x, 0)
    return unturn(at, gather_z(at, both))


def pick(pair, place):
    mine = jnp.where(place == 0, pair[0], pair[1])
    other = jnp.where(place == 0, pair[1], pair[0])
    return mine, other


def scatter_zx(at, parts):
    total = scatter_z(at, parts)
    mine, other = pick(total, at.x)
    return mine + swap_x(other.astype(bf16)).astype(f32)


def scatter_xz(at, parts):
    sums = []
    for part in parts:
        mine, other = pick(part, at.x)
        sums.append(mine.astype(f32) + swap_x(other.astype(bf16)).astype(f32))
    return scatter_z(at, sums)


def rows_to_block(at, own):
    both = pair_up(own, swap_core(own), at.c, 0)
    pair = pair_up(both[None], swap_y(both)[None], at.y, 0)
    return pair.reshape(4 * own.shape[0], own.shape[1])


def rows_from_block(at, partial_sum):
    rows = partial_sum.shape[0] // 4
    parts = partial_sum.reshape(2, 2, rows, partial_sum.shape[1])
    mine, other = pick(parts.swapaxes(0, 1), at.c)
    total = mine + swap_core(other.astype(bf16)).astype(f32)
    mine, other = pick(total, at.y)
    return mine + swap_y(other.astype(bf16)).astype(f32)


def spread_weight(at, shard):
    rows, units = shard.shape
    half = rows // 2
    keep, send = pick(shard.reshape(2, half, units), at.c)
    wide = pair_up(keep[None], swap_core(send)[None], at.c, 0)
    quarter = 2 * units // at.nz
    per_core = units // quarter
    pieces = wide.reshape(2, half, per_core, quarter).transpose(0, 2, 1, 3)
    pieces = pieces.reshape(at.nz, half, quarter)
    got = unturn(at, deal_z(at, turn(at, pieces)))
    got = pair_up(got[:, None], swap_x(got)[:, None], at.x, 1)
    got = pair_up(got, swap_y(got), at.y, 3)
    got = pair_up(got[:, :, None], swap_core(got)[:, :, None], at.c, 2)
    return got.reshape(at.blocks * rows, 2 * quarter)


def collect_weight(at, grad):
    depth, width = grad.shape
    half, quarter = depth // (2 * at.blocks), width // 2
    parts = grad.reshape(at.nz, 2, 2, half, width)
    mine, other = pick(parts.transpose(2, 0, 1, 3, 4), at.c)
    total = mine + swap_core(other.astype(bf16)).astype(f32)
    mine, other = pick((total[..., :quarter], total[..., quarter:]), at.y)
    total = mine + swap_y(other.astype(bf16)).astype(f32)
    mine, other = pick((total[:, 0], total[:, 1]), at.x)
    total = mine + swap_x(other.astype(bf16)).astype(f32)
    got = unturn(at, deal_z(at, turn(at, total.astype(bf16))))
    per_core = at.nz // 2
    wide = got.reshape(2, per_core, half, quarter).transpose(0, 2, 1, 3)
    wide = wide.reshape(2, half, per_core * quarter)
    mine, other = pick(wide, at.c)
    rows = pair_up(mine, swap_core(other), at.c, 0)
    return rows.astype(f32)


def sum_all(at, values):
    total = values
    for bit in (1, 2):
        total = total + lax.ppermute(total, "heads", [(i, i ^ bit) for i in range(4)])
    bit = 1
    while bit < at.blocks:
        total = total + lax.ppermute(total, "blk", [(i, i ^ bit) for i in range(at.blocks)])
        bit *= 2
    return total


class Permutes:
    def __init__(self, at):
        self.at = at
        self.block, self.blocks, self.nz = at.b, at.blocks, at.nz

    def start(self, own, attn_shard, ff_shards):
        at = self.at
        depth = own.shape[1]
        attn_full = gather_zx(at, attn_shard).reshape(depth, -1)
        return self.gather_heads(own), attn_full, [spread_weight(at, w) for w in ff_shards]

    def gather_heads(self, own):
        return rows_to_block(self.at, own)

    def scatter_heads(self, partial):
        return rows_from_block(self.at, partial)

    def gather_kv(self, own):
        whole = gather_zx(self.at, own)
        return whole.reshape((self.blocks,) + own.shape)

    def split(self, whole):
        return turn(self.at, whole.reshape((self.nz, whole.shape[0] // self.nz) + whole.shape[1:]))

    def scatter_kv(self, parts):
        return scatter_xz(self.at, self.split(parts))

    def gather_z(self, own):
        whole = unturn(self.at, gather_z(self.at, own))
        return whole.reshape(-1, own.shape[1])

    def scatter_z(self, partial):
        return scatter_z(self.at, self.split(partial))

    def scatter_attn(self, grad):
        rows = grad.shape[0] // self.blocks
        return scatter_xz(self.at, self.split(grad.reshape(self.blocks, rows, -1)))

    def collect(self, grads):
        return [collect_weight(self.at, g) for g in grads]


MESH = pl.DeviceIdType.MESH
anywhere = pl.BlockSpec(memory_space=pl.ANY)
in_vmem = pl.BlockSpec(memory_space=pltpu.VMEM)


def remote(src, dst, send_sem, recv_sem, target):
    return pltpu.make_async_remote_copy(
        src_ref=src,
        dst_ref=dst,
        send_sem=send_sem,
        recv_sem=recv_sem,
        device_id=target,
        device_id_type=MESH,
    )


class Spot:
    def __init__(self, nz):
        self.nz = nz
        h, b = lax.axis_index("heads"), lax.axis_index("blk")
        self.y, self.c = h // 2, h % 2
        self.z, self.x = b // 2, b % 2

    def device(self, z=None, x=None, y=None, c=None):
        z = self.z if z is None else z
        x = self.x if x is None else x
        y = self.y if y is None else y
        c = self.c if c is None else c
        return (2 * y + c, 2 * z + x)

    def greet(self, devices):
        barrier = pltpu.get_barrier_semaphore()
        for device in devices:
            pl.semaphore_signal(barrier, inc=1, device_id=device, device_id_type=MESH)
        pl.semaphore_wait(barrier, len(devices))

    def plane(self):
        found = []
        for dx, dy, dc in [(0, 0, 1), (1, 0, 0), (1, 0, 1), (0, 1, 0), (0, 1, 1), (1, 1, 0), (1, 1, 1)]:
            found.append(self.device(x=flip(self.x, dx), y=flip(self.y, dy), c=flip(self.c, dc)))
        return found

    def column(self, both_cores):
        found = []
        for s in range(1, self.nz):
            z = (self.z + s) % self.nz
            found.append(self.device(z=z))
            if both_cores:
                found.append(self.device(z=z, c=1 - self.c))
        return found


def flip(bit, by):
    return 1 - bit if by else bit


def add_rows(out, left, right, step=16):
    rows = left.shape[0]

    @pl.loop(0, rows // step)
    def _(i):
        at = pl.ds(pl.multiple_of(i * step, step), step)
        out[at, :] = (left[at, :].astype(f32) + right[at, :].astype(f32)).astype(out.dtype)


class LineGather:
    def __init__(self, spot, entry, sems):
        self.spot, self.entry = spot, entry
        self.send, self.recv = sems

    def copies(self, s):
        p, nz = self.spot, self.spot.nz
        up_at = lax.rem(p.z - s + 1 + nz, nz)
        down_at = lax.rem(p.z + s - 1, nz)
        up_z = lax.rem(p.z + 1, nz)
        down_z = lax.rem(p.z + nz - 1, nz)
        up = remote(
            self.entry(up_at), self.entry(up_at), self.send.at[0, s], self.recv.at[0, s], p.device(z=up_z)
        )
        down = remote(
            self.entry(down_at),
            self.entry(down_at),
            self.send.at[1, s],
            self.recv.at[1, s],
            p.device(z=down_z),
        )
        return (
            ((p.z >= s - 1) & (p.z < nz - 1), p.z >= s, up),
            ((p.z <= nz - s) & (p.z > 0), p.z <= nz - 1 - s, down),
        )

    def start(self, s):
        for sends, _, copy in self.copies(s):
            pl.when(sends)(copy.start)

    def arrive(self, s):
        for _, receives, copy in self.copies(s):
            pl.when(receives)(copy.wait_recv)

    def finish(self):
        for s in range(1, self.spot.nz):
            for sends, _, copy in self.copies(s):
                pl.when(sends)(copy.wait_send)

    def newest(self, s):
        p, nz = self.spot, self.spot.nz
        return (
            (p.z >= s, lax.rem(p.z - s + nz, nz)),
            (p.z <= nz - 1 - s, lax.rem(p.z + s, nz)),
        )


class LineScatter:
    def __init__(self, spot, parts, up, down, sems):
        self.spot, self.parts, self.up, self.down = spot, parts, up, down
        self.send, self.recv = sems

    def copies(self, t):
        p, nz = self.spot, self.spot.nz
        k = nz - t
        up_at, down_at = lax.rem(p.z + k, nz), lax.rem(p.z - k + nz, nz)
        up = remote(
            self.parts.at[up_at],
            self.up.at[t - 1],
            self.send.at[0, t],
            self.recv.at[0, t],
            p.device(z=lax.rem(p.z + 1, nz)),
        )
        down = remote(
            self.parts.at[down_at],
            self.down.at[t - 1],
            self.send.at[1, t],
            self.recv.at[1, t],
            p.device(z=lax.rem(p.z + nz - 1, nz)),
        )
        return (
            (p.z <= nz - 1 - k, (p.z >= 1) & (p.z <= t), up),
            (p.z >= k, (p.z <= nz - 2) & (p.z >= nz - 1 - t), down),
        )

    def start(self, t):
        for sends, _, copy in self.copies(t):
            pl.when(sends)(copy.start)

    def arrive(self, t):
        p, nz = self.spot, self.spot.nz
        k = nz - t
        for way, (_, receives, copy) in enumerate(self.copies(t)):

            @pl.when(receives)
            def _(way=way, copy=copy):
                copy.wait_recv()
                if t < nz - 1:
                    index = lax.rem(p.z + k - 1, nz) if way == 0 else lax.rem(p.z - k + 1 + nz, nz)
                    came = (self.up if way == 0 else self.down).at[t - 1]
                    add_rows(self.parts.at[index], self.parts.at[index], came)

    def finish(self):
        for t in range(1, self.spot.nz):
            for sends, _, copy in self.copies(t):
                pl.when(sends)(copy.wait_send)

    def total(self, out, step=16):
        p, last = self.spot, self.spot.nz - 2
        mine = self.parts.at[p.z]
        inner = (p.z > 0) & (p.z < p.nz - 1)

        @pl.when(p.z == 0)
        def _():
            add_rows(out, mine, self.down.at[last], step)

        @pl.when(p.z == p.nz - 1)
        def _():
            add_rows(out, mine, self.up.at[last], step)

        @pl.when(inner)
        def _():
            @pl.loop(0, out.shape[0] // step)
            def _(i):
                at = pl.ds(pl.multiple_of(i * step, step), step)
                sides = self.up[last, at, :].astype(f32) + self.down[last, at, :].astype(f32)
                out[at, :] = (mine[at, :].astype(f32) + sides).astype(out.dtype)


def core_copies(spot, entries, sems):
    send, recv = sems
    other = spot.device(c=1 - spot.c)
    return [remote(e, e, send.at[i], recv.at[i], other) for i, e in enumerate(entries)]


class PlaneGather:
    def __init__(self, spot, own, whole, sems, local_sem):
        self.spot, self.own, self.whole = spot, own, whole
        self.send, self.recv = sems
        self.local = pltpu.make_async_copy(own, whole.at[2 * spot.y + spot.c], local_sem)

    def copies(self):
        p = self.spot
        part = 2 * p.y + p.c
        found = []
        for i, (dx, dy) in enumerate([(1, 0), (0, 1), (1, 1), (0, 0)]):
            target = p.device(x=flip(p.x, dx), y=flip(p.y, dy), c=p.x)
            found.append(
                remote(self.own, self.whole.at[part], self.send.at[i], self.recv.at[part], target)
            )
        return found

    def start(self):
        p = self.spot
        *away, home = self.copies()
        for copy in away:
            copy.start()
        pl.when(p.c == p.x)(self.local.start)
        pl.when(p.c != p.x)(home.start)

    def finish(self):
        p = self.spot
        *away, home = self.copies()
        for copy in away:
            copy.wait_send()
        pl.when(p.c == p.x)(self.local.wait)
        pl.when(p.c != p.x)(home.wait_send)
        for part in range(4):
            copy = remote(
                self.own, self.whole.at[part], self.send.at[0], self.recv.at[part], p.device(c=1 - p.c)
            )
            mine = (p.c == p.x) & (part == 2 * p.y + p.c)
            pl.when(jnp.logical_not(mine))(copy.wait_recv)


def exclusive_or(z, i):
    low, high = lax.rem(z, 2), lax.rem(z // 2, 2)
    rest = z - 2 * high - low
    return rest + 2 * flip(high, i // 2) + flip(low, i % 2)


class Spread:
    def __init__(self, spot, shard, full, sems):
        self.spot, self.shard, self.full = spot, shard, full
        self.send, self.recv = sems
        self.quarter = full.shape[-1] // 2
        self.nz = spot.nz
        self.per_core = self.nz // 2

    def place(self, z, x, c, y):
        columns = pl.ds(pl.multiple_of(y * self.quarter, 128), self.quarter)
        return self.full.at[z, x, c, :, columns]


    def deal(self, piece, half):
        p = self.spot
        z = p.c * self.per_core + piece
        columns = pl.ds(piece * self.quarter, self.quarter)
        src = self.shard.at[half, :, columns]
        return z, remote(
            src,
            self.place(p.z, p.x, half, p.y),
            self.send.at[6 * self.nz + 2 * piece + half],
            self.recv.at[p.z],
            p.device(z=z, c=half),
        )

    def local(self, piece):
        p = self.spot
        columns = pl.ds(piece * self.quarter, self.quarter)
        return pltpu.make_async_copy(
            self.shard.at[p.c, :, columns],
            self.place(p.z, p.x, p.c, p.y),
            self.recv.at[p.z],
        )

    def start(self):
        p = self.spot
        for piece in range(self.per_core):
            for half in range(2):
                z, copy = self.deal(piece, half)
                here = (z == p.z) & (p.c == half)
                pl.when(jnp.logical_not(here))(copy.start)
                pl.when(here)(self.local(piece).start)

    def dealt(self, source):
        p = self.spot
        here = self.place(source, p.x, p.c, p.y)
        ours = (source == p.z) & (p.c == p.z // self.per_core)
        came = remote(here, here, self.send.at[0], self.recv.at[source], p.device(c=1 - p.c))
        pl.when(jnp.logical_not(ours))(came.wait_recv)
        pl.when(ours)(self.local(0).wait)

    def first(self, z):
        p = self.spot
        here = self.place(z, p.x, p.c, p.y)
        x = p.x + (1 - 2 * p.x) * (1 - p.c)
        y = p.y + (1 - 2 * p.y) * p.c
        return remote(
            here, here, self.send.at[self.nz + z], self.recv.at[self.nz + z], p.device(x=x, y=y)
        )

    def second(self, z, which):
        p = self.spot
        x, y = p.x, p.y
        if which:
            x = p.x + (1 - 2 * p.x) * (1 - p.c)
            y = p.y + (1 - 2 * p.y) * p.c
        here = self.place(z, x, p.c, y)
        tx = p.x + (1 - 2 * p.x) * p.c
        ty = p.y + (1 - 2 * p.y) * (1 - p.c)
        sem = 2 * self.nz + 2 * z + which
        return remote(here, here, self.send.at[sem], self.recv.at[sem], p.device(x=tx, y=ty))

    def across(self, z, x):
        p = self.spot
        here = self.full.at[z, x, p.c]
        sem = 4 * self.nz + 2 * z + x
        return remote(here, here, self.send.at[sem], self.recv.at[sem], p.device(c=1 - p.c))

    def finish(self):
        p = self.spot
        for piece in range(self.per_core):
            for half in range(2):
                z, copy = self.deal(piece, half)
                here = (z == p.z) & (p.c == half)
                pl.when(jnp.logical_not(here))(copy.wait_send)
        for z in range(self.nz):
            self.first(z).wait_send()
            for which in range(2):
                self.second(z, which).wait_send()
            for x in range(2):
                self.across(z, x).wait()


def start_kernel(nz, own, attn, gate, up, down, rows, attn_full, gate_full, up_full, down_full, *sems):
    (t_send, t_recv, a_send, a_recv, l_send, l_recv, x_send, x_recv, f_send, f_recv, local) = sems
    p = Spot(nz)
    p.greet(p.plane() + p.column(True))
    tokens = PlaneGather(p, own, rows, (t_send, t_recv), local.at[0])
    spreads = [
        Spread(p, shard, full, (f_send.at[i], f_recv.at[i]))
        for i, (shard, full) in enumerate(((gate, gate_full), (up, up_full), (down, down_full)))
    ]
    line = LineGather(p, lambda z: attn_full.at[z, p.c], (l_send, l_recv))
    keep = pltpu.make_async_copy(attn, attn_full.at[p.z, p.c], local.at[1])
    trade = remote(
        attn, attn_full.at[p.z, p.x], a_send, a_recv, p.device(x=1 - p.x, c=1 - p.c)
    )
    same = p.c == p.x
    pl.when(same)(keep.start)
    pl.when(jnp.logical_not(same))(trade.start)
    tokens.start()
    spreads[0].start()
    pl.when(same)(keep.wait)
    pl.when(jnp.logical_not(same))(trade.wait_recv)
    line.start(1)
    across = core_copies(p, [attn_full.at[z, p.c] for z in range(nz)], (x_send, x_recv))

    def stage_first(spread, i):
        z = exclusive_or(p.z, i)
        spread.dealt(z)
        spread.first(z).start()
        spread.second(z, 0).start()

    def stage_second(spread, i):
        z = exclusive_or(p.z, i)
        spread.first(z).wait_recv()
        spread.second(z, 1).start()

    def stage_core(spread, i):
        z = exclusive_or(p.z, i)
        for which in range(2):
            spread.second(z, which).wait_recv()
        for x in range(2):
            spread.across(z, x).start()

    spreads[1].start()
    stage_first(spreads[0], 0)
    line.arrive(1)
    line.start(2)
    for i in range(1, nz):
        stage_first(spreads[0], i)
    spreads[2].start()
    line.arrive(2)
    line.start(3)
    for i in range(nz):
        stage_first(spreads[1], i)
        stage_second(spreads[0], i)
    line.arrive(3)
    for copy in across:
        copy.start()
    for i in range(nz):
        stage_first(spreads[2], i)
        stage_core(spreads[0], i)
        stage_second(spreads[1], i)
    for i in range(nz):
        stage_second(spreads[2], i)
        stage_core(spreads[1], i)
    for i in range(nz):
        stage_core(spreads[2], i)
    tokens.finish()
    pl.when(jnp.logical_not(same))(trade.wait_send)
    line.finish()
    for copy in across:
        copy.wait()
    for spread in spreads:
        spread.finish()


def gather_kv_kernel(nz, own, full, send, recv, x_send, x_recv, local):
    p = Spot(nz)
    p.greet([p.device(c=1 - p.c)] + p.column(False))
    line = LineGather(p, lambda z: full.at[z, p.c], (send, recv))
    keep = pltpu.make_async_copy(own, full.at[p.z, p.c], local)
    keep.start()
    keep.wait()
    line.start(1)
    across = core_copies(p, [full.at[z, p.c] for z in range(nz)], (x_send, x_recv))
    for s in range(2, nz):
        line.arrive(s - 1)
        line.start(s)
    line.arrive(nz - 1)
    for copy in across:
        copy.start()
    line.finish()
    for copy in across:
        copy.wait()


def gather_heads_kernel(nz, own, whole, send, recv, local):
    p = Spot(nz)
    p.greet(p.plane())
    tokens = PlaneGather(p, own, whole, (send, recv), local)
    tokens.start()
    tokens.finish()


def scatter_heads_kernel(nz, parts, out, came, send, recv):
    p = Spot(nz)
    p.greet(p.plane())
    head = 2 * p.y + p.x

    def copy_to(part, slot):
        y, c = part // 2, part % 2
        return remote(
            parts.at[part], came.at[head], send.at[part], recv.at[slot], p.device(x=p.c, y=y, c=c)
        )

    ours = 2 * p.y + p.c
    for part in range(4):
        here = (p.x == p.c) & (part == ours)
        pl.when(jnp.logical_not(here))(copy_to(part, head).start)
    for part in range(4):
        here = (p.x == p.c) & (part == ours)
        pl.when(jnp.logical_not(here))(copy_to(part, head).wait_send)
        arrived = remote(
            parts.at[part], came.at[part], send.at[part], recv.at[part], p.device(c=1 - p.c)
        )
        mine = (p.x == p.c) & (part == head)
        pl.when(jnp.logical_not(mine))(arrived.wait_recv)

    @pl.when(p.x == p.c)
    def _():
        came[head] = parts[ours]

    rows = out.shape[0]

    @pl.loop(0, rows // 16)
    def _(i):
        at = pl.ds(pl.multiple_of(i * 16, 16), 16)
        low = came[0, at, :].astype(f32) + came[1, at, :].astype(f32)
        out[at, :] = low + (came[2, at, :].astype(f32) + came[3, at, :].astype(f32))


def gather_z_kernel(nz, own, full, send, recv, local):
    p = Spot(nz)
    p.greet(p.column(False))
    line = LineGather(p, lambda z: full.at[z], (send, recv))
    keep = pltpu.make_async_copy(own, full.at[p.z], local)
    keep.start()
    keep.wait()
    line.start(1)
    for s in range(2, nz):
        line.arrive(s - 1)
        line.start(s)
    line.arrive(nz - 1)
    line.finish()


def scatter_z_kernel(nz, given, out, parts, up, down, send, recv, local):
    p = Spot(nz)
    p.greet(p.column(False))
    bring = pltpu.make_async_copy(given, parts, local)
    bring.start()
    bring.wait()
    line = LineScatter(p, parts, up, down, (send, recv))
    for t in range(1, nz):
        line.start(t)
        line.arrive(t)
    line.total(out)
    line.finish()


def scatter_pair_kernel(nz, trade_back, given, out, parts, came, up, down, *sems):
    (x_send, x_recv, send, recv, local, b_send, b_recv) = sems
    p = Spot(nz)
    found = [p.device(c=1 - p.c)] + p.column(False)
    if trade_back:
        found.append(p.device(x=1 - p.x, c=1 - p.c))
    p.greet(found)
    order = [nz - 1, 0] + list(range(1, nz - 1))
    away = [
        remote(given.at[z, 1 - p.c], came.at[z], x_send.at[z], x_recv.at[z], p.device(c=1 - p.c))
        for z in range(nz)
    ]
    bring = [pltpu.make_async_copy(given.at[z, p.c], parts.at[z], local.at[z]) for z in range(nz)]
    for z in order:
        away[z].start()
        bring[z].start()
    line = LineScatter(p, parts, up, down, (send, recv))
    for z in order:
        away[z].wait_recv()
        bring[z].wait()
        add_rows(parts.at[z], parts.at[z], came.at[z])
    for t in range(1, nz):
        line.start(t)
        line.arrive(t)
    if not trade_back:
        line.total(out)
    else:
        line.total(came.at[0])
        away[0].wait_send()
        same = p.c == p.x
        back = remote(came.at[0], out, b_send, b_recv, p.device(x=1 - p.x, c=1 - p.c))
        keep = pltpu.make_async_copy(came.at[0], out, b_recv)
        pl.when(same)(keep.start)
        pl.when(jnp.logical_not(same))(back.start)
        pl.when(same)(keep.wait)
        pl.when(jnp.logical_not(same))(back.wait)
    for z in range(1 if trade_back else 0, nz):
        away[z].wait_send()
    line.finish()


def collect_kernel(nz, given, out, mine, came, first_in, second_in, *sems):
    (l_send, c_send, c_recv, f_send, f_recv, s_send, s_recv, d_send, d_recv) = sems
    p = Spot(nz)
    p.greet(p.plane() + p.column(True))
    half, quarter = given.shape[3], given.shape[4] // 2
    other_core = p.device(c=1 - p.c)
    order = [exclusive_or(p.z, i) for i in (3, 2, 1, 0)]

    def bring(z, x):
        return pltpu.make_async_copy(given.at[z, x, p.c], mine.at[z, x], l_send.at[2 * z + x])

    def across(z, x):
        sem = 2 * z + x
        return remote(
            given.at[z, x, 1 - p.c], came.at[z, x], c_send.at[sem], c_recv.at[sem], other_core
        )

    def columns(y):
        return pl.ds(pl.multiple_of(y * quarter, 128), quarter)

    fx = p.x + (1 - 2 * p.x) * p.c
    fy = p.y + (1 - 2 * p.y) * (1 - p.c)
    sx = p.x + (1 - 2 * p.x) * (1 - p.c)
    sy = p.y + (1 - 2 * p.y) * p.c

    def first(z, which):
        x, y = fx, fy
        if which:
            x = fx + (1 - 2 * fx) * (1 - p.c)
            y = fy + (1 - 2 * fy) * p.c
        sem = 2 * z + which
        return remote(
            mine.at[z, x, :, columns(y)],
            first_in.at[z, which],
            f_send.at[sem],
            f_recv.at[sem],
            p.device(x=fx, y=fy),
        )

    def second(z):
        return remote(
            mine.at[z, sx, :, columns(sy)],
            second_in.at[z],
            s_send.at[z],
            s_recv.at[z],
            p.device(x=sx, y=sy),
        )

    per_core = nz // 2

    def out_at(z, half_of):
        return out.at[half_of, :, pl.ds(pl.multiple_of(lax.rem(z, per_core) * quarter, 128), quarter)]

    owner = p.z // per_core

    def deal(z):
        return remote(
            mine.at[z, p.x, :, columns(p.y)],
            out_at(p.z, p.c),
            d_send.at[z],
            d_recv.at[2 * lax.rem(p.z, per_core) + p.c],
            p.device(z=z, c=owner),
        )

    def keep(z):
        return pltpu.make_async_copy(
            mine.at[z, p.x, :, columns(p.y)],
            out_at(p.z, p.c),
            d_recv.at[2 * lax.rem(p.z, per_core) + p.c],
        )

    for z in order:
        for x in range(2):
            across(z, x).start()
            bring(z, x).start()

    def summed_over_core(z):
        for x in range(2):
            across(z, x).wait_recv()
            bring(z, x).wait()
            add_rows(mine.at[z, x], mine.at[z, x], came.at[z, x])
        for which in range(2):
            first(z, which).start()

    def summed_over_first(z):
        for which in (1, 0):
            x, y = p.x, p.y
            if which:
                x, y = sx, sy
            first(z, which).wait_recv()
            place = mine.at[z, x, :, columns(y)]
            add_rows(place, place, first_in.at[z, which])
            if which:
                second(z).start()

    def summed_over_second(z):
        second(z).wait_recv()
        place = mine.at[z, p.x, :, columns(p.y)]
        add_rows(place, place, second_in.at[z])
        here = (z == p.z) & (p.c == owner)
        pl.when(jnp.logical_not(here))(deal(z).start)
        pl.when(here)(keep(z).start)

    for i in range(nz + 2):
        if i < nz:
            summed_over_core(order[i])
        if 0 <= i - 1 < nz:
            summed_over_first(order[i - 1])
        if 0 <= i - 2 < nz:
            summed_over_second(order[i - 2])
    for piece in range(per_core):
        for half_of in range(2):
            z = p.c * per_core + piece
            place = out_at(z, half_of)
            arrived = remote(
                place, place, d_send.at[0], d_recv.at[2 * piece + half_of], other_core
            )
            ours = (z == p.z) & (p.c == half_of)
            pl.when(jnp.logical_not(ours))(arrived.wait_recv)
    for z in range(nz):
        here = (z == p.z) & (p.c == owner)
        pl.when(jnp.logical_not(here))(deal(z).wait_send)
        pl.when(here)(keep(z).wait)
        second(z).wait_send()
        for which in range(2):
            first(z, which).wait_send()
        for x in range(2):
            across(z, x).wait_send()


class Kernels:
    def __init__(self, at):
        self.at = at
        self.blocks, self.nz = at.blocks, at.nz
        self.block = 2 * at.z + at.c
        self.number = 0

    def call(self, body, out_shape, scratch, vmem=(), out_vmem=(), sent=0):
        def run(*operands):
            self.number += 1
            many = isinstance(out_shape, list)
            specs = [in_vmem if i in out_vmem else anywhere for i in range(len(out_shape) if many else 1)]
            return pl.pallas_call(
                body,
                out_shape=out_shape,
                in_specs=[in_vmem if i in vmem else anywhere for i in range(len(operands))],
                out_specs=specs if many else specs[0],
                scratch_shapes=scratch,
                compiler_params=pltpu.CompilerParams(
                    collective_id=self.number, has_side_effects=True, vmem_limit_bytes=48 * 2**20
                ),
                cost_estimate=pl.CostEstimate(
                    flops=0, bytes_accessed=sent, transcendentals=0, remote_bytes_transferred=sent
                ),
            )(*operands)

        return run

    def start(self, own, attn_shard, ff_shards):
        nz = self.nz
        rows, depth = own.shape
        shard_rows, attn_columns = attn_shard.shape
        units = ff_shards[0].shape[1]
        half, width = shard_rows // 2, 4 * units // nz
        dma = pltpu.SemaphoreType.DMA
        full = jax.ShapeDtypeStruct((nz, 2, 2, half, width), bf16)
        outs = [
            jax.ShapeDtypeStruct((4, rows, depth), bf16),
            jax.ShapeDtypeStruct((nz, 2, shard_rows, attn_columns), bf16),
            full, full, full,
        ]
        count = 6 * nz + nz
        scratch = [
            dma((4,)), dma((4,)), dma, dma, dma((2, nz)), dma((2, nz)), dma((nz,)), dma((nz,)),
            dma((3, count)), dma((3, count)), dma((2,)),
        ]
        rows_out, attn_full, *ff = self.call(
            functools.partial(start_kernel, nz), outs, scratch, sent=20_000_000
        )(own, attn_shard, *[w.reshape(2, half, units) for w in ff_shards])
        return (
            rows_out.reshape(4 * rows, depth),
            attn_full.reshape(depth, attn_columns),
            [w.reshape(depth, width) for w in ff],
        )

    def gather_heads(self, own):
        dma = pltpu.SemaphoreType.DMA
        out = jax.ShapeDtypeStruct((4,) + own.shape, bf16)
        whole = self.call(
            functools.partial(gather_heads_kernel, self.nz), out, [dma((4,)), dma((4,)), dma]
        )(own)
        return whole.reshape(-1, own.shape[1])

    def scatter_heads(self, partial):
        dma = pltpu.SemaphoreType.DMA
        rows, depth = partial.shape[0] // 4, partial.shape[1]
        out = jax.ShapeDtypeStruct((rows, depth), f32)
        scratch = [pltpu.VMEM((4, rows, depth), bf16), dma((4,)), dma((4,))]
        return self.call(
            functools.partial(scatter_heads_kernel, self.nz), out, scratch, vmem=(0,), out_vmem=(0,)
        )(partial.reshape(4, rows, depth))

    def gather_kv(self, own):
        dma = pltpu.SemaphoreType.DMA
        nz = self.nz
        out = jax.ShapeDtypeStruct((nz, 2) + own.shape, bf16)
        scratch = [dma((2, nz)), dma((2, nz)), dma((nz,)), dma((nz,)), dma]
        whole = self.call(functools.partial(gather_kv_kernel, nz), out, scratch)(own)
        return whole.reshape((self.blocks,) + own.shape)

    def gather_z(self, own):
        dma = pltpu.SemaphoreType.DMA
        nz = self.nz
        out = jax.ShapeDtypeStruct((nz,) + own.shape, bf16)
        scratch = [dma((2, nz)), dma((2, nz)), dma]
        whole = self.call(functools.partial(gather_z_kernel, nz), out, scratch)(own)
        return whole.reshape(-1, own.shape[1])

    def scatter_z(self, partial):
        dma = pltpu.SemaphoreType.DMA
        nz = self.nz
        rows, depth = partial.shape[0] // nz, partial.shape[1]
        out = jax.ShapeDtypeStruct((rows, depth), f32)
        line = pltpu.VMEM((nz - 1, rows, depth), bf16)
        scratch = [pltpu.VMEM((nz, rows, depth), bf16), line, line, dma((2, nz)), dma((2, nz)), dma]
        return self.call(
            functools.partial(scatter_z_kernel, nz), out, scratch, out_vmem=(0,)
        )(partial.reshape(nz, rows, depth))

    def scatter_pair(self, given, trade_back):
        dma = pltpu.SemaphoreType.DMA
        nz = self.nz
        _, _, rows, width = given.shape
        out = jax.ShapeDtypeStruct((rows, width), bf16)
        whole = pltpu.VMEM((nz, rows, width), bf16)
        line = pltpu.VMEM((nz - 1, rows, width), bf16)
        scratch = [
            whole, whole, line, line,
            dma((nz,)), dma((nz,)), dma((2, nz)), dma((2, nz)), dma((nz,)), dma, dma,
        ]
        return self.call(
            functools.partial(scatter_pair_kernel, nz, trade_back), out, scratch, out_vmem=(0,)
        )(given)

    def scatter_kv(self, parts):
        return self.scatter_pair(parts.reshape((self.nz, 2) + parts.shape[1:]), False).astype(f32)

    def scatter_attn(self, grad):
        given = grad.reshape(self.nz, 2, grad.shape[0] // self.blocks, grad.shape[1])
        return self.scatter_pair(given, True).astype(f32)

    def collect(self, grads):
        dma = pltpu.SemaphoreType.DMA
        nz = self.nz
        depth, width = grads[0].shape
        half, quarter = depth // (4 * nz), width // 2
        out = jax.ShapeDtypeStruct((2, half, nz // 2 * quarter), bf16)
        whole = pltpu.VMEM((nz, 2, half, width), bf16)
        scratch = [
            whole,
            whole,
            pltpu.VMEM((nz, 2, half, quarter), bf16),
            pltpu.VMEM((nz, half, quarter), bf16),
            dma((2 * nz,)), dma((2 * nz,)), dma((2 * nz,)), dma((2 * nz,)), dma((2 * nz,)),
            dma((nz,)), dma((nz,)), dma((nz,)), dma((nz,)),
        ]
        run = self.call(functools.partial(collect_kernel, nz), out, scratch)
        found = []
        for grad in grads:
            shard = run(grad.reshape(nz, 2, 2, half, width))
            found.append(shard.reshape(2 * half, -1).astype(f32))
        return found


def causal_mask(rows):
    shape = (rows, rows)
    return lax.broadcasted_iota(jnp.int32, shape, 1) <= lax.broadcasted_iota(jnp.int32, shape, 0)


def forward_kernel(kinds, q_ref, kv_ref, out_ref, exact_ref, inv_ref, acc, total):
    step, last = pl.program_id(0), pl.num_programs(0) - 1
    heads, rows, dim = q_ref.shape
    kind = kinds[step]

    @pl.when(step == 0)
    def _():
        acc[...] = jnp.zeros_like(acc)
        total[...] = jnp.zeros_like(total)

    def work(own):
        for head in range(heads):
            raw = contract(q_ref[head], kv_ref[0, :, :dim], 1, 1)
            weights = jnp.exp(softcap * jnp.tanh(raw * (score_scale / softcap)))
            if own:
                weights = jnp.where(causal_mask(rows), weights, 0.0)
            total[head] += jnp.sum(weights, axis=-1, keepdims=True)
            acc[head] += contract(weights.astype(bf16), kv_ref[0, :, dim:], 1, 0)

    @pl.when(kind == 1)
    def _():
        work(False)

    @pl.when(kind == 2)
    def _():
        work(True)

    @pl.when(step == last)
    def _():
        for head in range(heads):
            inverse = 1.0 / total[head]
            value = acc[head] * inverse
            inv_ref[head] = inverse
            exact_ref[:, head * dim : (head + 1) * dim] = value
            out_ref[:, head * dim : (head + 1) * dim] = value.astype(bf16)


def whole2(step, kinds):
    return (0, 0)


def whole3(step, kinds):
    return (0, 0, 0)


def by_step(step, kinds):
    return (step, 0, 0)


def attend(kinds, queries, all_kv):
    heads, rows, dim = queries.shape
    return pl.pallas_call(
        forward_kernel,
        grid_spec=pltpu.PrefetchScalarGridSpec(
            num_scalar_prefetch=1,
            grid=(all_kv.shape[0],),
            in_specs=[
                pl.BlockSpec((heads, rows, dim), whole3),
                pl.BlockSpec((1, rows, 2 * dim), by_step),
            ],
            out_specs=[
                pl.BlockSpec((rows, heads * dim), whole2),
                pl.BlockSpec((rows, heads * dim), whole2),
                pl.BlockSpec((heads, rows, 1), whole3),
            ],
            scratch_shapes=[
                pltpu.VMEM((heads, rows, dim), f32),
                pltpu.VMEM((heads, rows, 1), f32),
            ],
        ),
        out_shape=[
            jax.ShapeDtypeStruct((rows, heads * dim), bf16),
            jax.ShapeDtypeStruct((rows, heads * dim), f32),
            jax.ShapeDtypeStruct((heads, rows, 1), f32),
        ],
        compiler_params=pltpu.CompilerParams(vmem_limit_bytes=40 * 2**20),
        cost_estimate=pl.CostEstimate(
            flops=3 * 4 * heads * rows * rows * dim,
            bytes_accessed=8 * rows * dim * heads,
            transcendentals=6 * heads * rows * rows,
        ),
    )(kinds, queries, all_kv)


def backward_kernel(kinds, q_ref, kv_ref, up_ref, exact_ref, inv_ref, dq_ref, dkv_ref):
    step = pl.program_id(0)
    heads, rows, dim = q_ref.shape
    kind = kinds[step]

    @pl.when(step == 0)
    def _():
        dq_ref[...] = jnp.zeros_like(dq_ref)

    def work(own):
        dk = jnp.zeros((rows, dim), f32)
        dv = jnp.zeros((rows, dim), f32)
        for head in range(heads):
            columns = slice(head * dim, (head + 1) * dim)
            up = up_ref[:, columns]
            delta = jnp.sum(up.astype(f32) * exact_ref[:, columns], axis=-1, keepdims=True)
            raw = contract(q_ref[head], kv_ref[0, :, :dim], 1, 1)
            bounded = jnp.tanh(raw * (score_scale / softcap))
            probs = jnp.exp(softcap * bounded) * inv_ref[head]
            if own:
                probs = jnp.where(causal_mask(rows), probs, 0.0)
            d_probs = contract(up, kv_ref[0, :, dim:], 1, 1)
            d_raw = probs * (d_probs - delta) * ((1.0 - bounded * bounded) * score_scale)
            d_raw = d_raw.astype(bf16)
            dq_ref[head] += contract(d_raw, kv_ref[0, :, :dim], 1, 0)
            dk += contract(d_raw, q_ref[head], 0, 0)
            dv += contract(probs.astype(bf16), up, 0, 0)
        dkv_ref[0, :, :dim] = dk.astype(bf16)
        dkv_ref[0, :, dim:] = dv.astype(bf16)

    @pl.when(kind == 1)
    def _():
        work(False)

    @pl.when(kind == 0)
    def _():
        dkv_ref[...] = jnp.zeros_like(dkv_ref)

    @pl.when(kind == 2)
    def _():
        work(True)


def attend_back(kinds, queries, all_kv, upstream, exact, inverse):
    heads, rows, dim = queries.shape
    blocks = all_kv.shape[0]
    return pl.pallas_call(
        backward_kernel,
        grid_spec=pltpu.PrefetchScalarGridSpec(
            num_scalar_prefetch=1,
            grid=(blocks,),
            in_specs=[
                pl.BlockSpec((heads, rows, dim), whole3),
                pl.BlockSpec((1, rows, 2 * dim), by_step),
                pl.BlockSpec((rows, heads * dim), whole2),
                pl.BlockSpec((rows, heads * dim), whole2),
                pl.BlockSpec((heads, rows, 1), whole3),
            ],
            out_specs=[
                pl.BlockSpec((heads, rows, dim), whole3),
                pl.BlockSpec((1, rows, 2 * dim), by_step),
            ],
        ),
        out_shape=[
            jax.ShapeDtypeStruct((heads, rows, dim), f32),
            jax.ShapeDtypeStruct((blocks, rows, 2 * dim), bf16),
        ],
        compiler_params=pltpu.CompilerParams(vmem_limit_bytes=40 * 2**20),
        cost_estimate=pl.CostEstimate(
            flops=3 * 10 * heads * rows * rows * dim,
            bytes_accessed=16 * rows * dim * heads,
            transcendentals=6 * heads * rows * rows,
        ),
    )(kinds, queries, all_kv, upstream, exact, inverse)


def on_device(
    tokens,
    cotangent,
    norm_attn_in,
    w_query,
    w_key,
    w_value,
    w_out,
    norm_attn_out,
    norm_ff_in,
    w_gate,
    w_up,
    w_down,
    norm_ff_out,
    block_group,
    block_role,
):
    at = Place()
    own_rows, depth = tokens.shape
    shard_rows, units = w_gate.shape
    regular = at.nz == 4 and shard_rows % 32 == 0 and (2 * units // at.nz) % 128 == 0
    comm = Kernels(at) if regular else Permutes(at)
    blocks = at.blocks
    block_len = own_rows * lax.axis_size("heads")
    prompt_len = blocks // 4
    block_ids = jnp.arange(blocks, dtype=jnp.int32)
    my_group = jnp.sum(jnp.where(block_ids == comm.block, block_group, 0))
    my_role = jnp.sum(jnp.where(block_ids == comm.block, block_role, 0))
    positions = jnp.where(
        my_role < prompt_len, my_role * block_len, prompt_len * block_len
    ) + jnp.arange(block_len, dtype=jnp.int32)
    cosine, sine_table = rope_tables(positions)
    prompt = (block_group == my_group) & (block_role < prompt_len) & (block_role < my_role)
    kinds = jnp.where(block_ids == comm.block, 2, prompt.astype(jnp.int32)).astype(jnp.int32)

    token_f32 = tokens.astype(f32)
    heads_width = w_query.shape[1]
    qkv_width = heads_width + 2 * HEAD_DIM
    attn_shard = jnp.concatenate([w_query, w_key, w_value, w_out.T], axis=1)
    normed_one, attn_full, (gate_full, up_full, down_full) = comm.start(
        normalize(token_f32, norm_attn_in).astype(bf16), attn_shard, (w_gate, w_up, w_down.T)
    )
    qkv_full, out_full = attn_full[:, :qkv_width], attn_full[:, qkv_width:]
    qkv_lin = jnp.dot(normed_one, qkv_full, preferred_element_type=f32)
    queries = jnp.stack(
        [
            rotate(qkv_lin[:, :HEAD_DIM], cosine, sine_table),
            rotate(qkv_lin[:, HEAD_DIM:heads_width], cosine, sine_table),
        ]
    ).astype(bf16)
    own_kv = jnp.concatenate(
        [
            rotate(qkv_lin[:, heads_width : heads_width + HEAD_DIM], cosine, sine_table),
            qkv_lin[:, heads_width + HEAD_DIM :],
        ],
        axis=1,
    ).astype(bf16)
    all_kv = comm.gather_kv(own_kv)
    attn_rows, attended, inverse = attend(kinds, queries, all_kv)
    attn_proj = comm.scatter_heads(contract(attn_rows, out_full, 1, 1).astype(bf16))
    middle = token_f32 + normalize(attn_proj, norm_attn_out)

    normed_two = comm.gather_z(normalize(middle, norm_ff_in).astype(bf16))
    gate_lin = jnp.dot(normed_two, gate_full, preferred_element_type=f32)
    up_lin = jnp.dot(normed_two, up_full, preferred_element_type=f32)
    hidden = (jax.nn.gelu(gate_lin, approximate=True) * up_lin).astype(bf16)
    ff_proj = comm.scatter_z(contract(hidden, down_full, 1, 1).astype(bf16))
    layer_out = middle + normalize(ff_proj, norm_ff_out)

    upstream = cotangent.astype(f32)
    d_ff, grad_ff_out = normalize_back(ff_proj, norm_ff_out, upstream)
    d_ff_rows = comm.gather_z(d_ff.astype(bf16))
    d_hidden = contract(d_ff_rows, down_full, 1, 0)
    _, glu_back = jax.vjp(
        lambda gate_in, up_in: jax.nn.gelu(gate_in, approximate=True) * up_in, gate_lin, up_lin
    )
    d_gate, d_up = glu_back(d_hidden)
    d_gate = d_gate.astype(bf16)
    d_up = d_up.astype(bf16)
    d_partial = contract(d_gate, gate_full, 1, 1) + contract(d_up, up_full, 1, 1)
    d_normed_two = comm.scatter_z(d_partial.astype(bf16))

    d_middle_part, grad_ff_in = normalize_back(middle, norm_ff_in, d_normed_two)
    d_middle = upstream + d_middle_part
    d_proj, grad_attn_out = normalize_back(attn_proj, norm_attn_out, d_middle)
    d_proj_rows = comm.gather_heads(d_proj.astype(bf16))
    d_attended = contract(d_proj_rows, out_full, 1, 0).astype(bf16)
    d_query, d_kv_parts = attend_back(kinds, queries, all_kv, d_attended, attended, inverse)
    d_kv = comm.scatter_kv(d_kv_parts)
    d_qkv_lin = jnp.concatenate(
        [
            rotate(d_query[0], cosine, -sine_table),
            rotate(d_query[1], cosine, -sine_table),
            rotate(d_kv[:, :HEAD_DIM], cosine, -sine_table),
            d_kv[:, HEAD_DIM:],
        ],
        axis=1,
    ).astype(bf16)
    d_normed_one = comm.scatter_heads(contract(d_qkv_lin, qkv_full, 1, 1).astype(bf16))
    grad_attn = comm.scatter_attn(
        jnp.concatenate(
            [contract(normed_one, d_qkv_lin, 0, 0), contract(d_proj_rows, attn_rows, 0, 0)], axis=1
        ).astype(bf16)
    )
    grad_gate, grad_up, grad_down = comm.collect(
        [
            contract(normed_two, d_gate, 0, 0).astype(bf16),
            contract(normed_two, d_up, 0, 0).astype(bf16),
            contract(d_ff_rows, hidden, 0, 0).astype(bf16),
        ]
    )
    d_token_part, grad_attn_in = normalize_back(token_f32, norm_attn_in, d_normed_one)
    input_grad = (d_middle + d_token_part).astype(bf16)
    gains = sum_all(at, jnp.stack([grad_attn_in, grad_attn_out, grad_ff_in, grad_ff_out]))
    return (
        layer_out.astype(bf16),
        input_grad,
        gains[0],
        grad_attn[:, :heads_width],
        grad_attn[:, heads_width : heads_width + HEAD_DIM],
        grad_attn[:, heads_width + HEAD_DIM : qkv_width],
        grad_attn[:, qkv_width:].T,
        gains[1],
        gains[2],
        grad_gate,
        grad_up,
        grad_down.T,
        gains[3],
    )


def solution(mesh):
    rows, weight, turned = P(("blk", "heads"), None), P("blk", "heads"), P("heads", "blk")
    return jax.shard_map(
        on_device,
        mesh=mesh,
        in_specs=(
            rows, rows, P(), weight, weight, weight, turned, P(), P(), weight, weight, turned,
            P(), P(), P(),
        ),
        out_specs=(
            rows, rows, P(), weight, weight, weight, turned, P(), P(), weight, weight, turned, P(),
        ),
        check_vma=False,
    )
```

time: 2130 us -> 1030 us (0.48)
  waiting for transfers between devices: 1750 us -> 2.95 us
  Pallas kernels: 0 us -> 830 us
  other arithmetic: 103 us -> 41.4 us
  blocking collectives: 46 us -> 0 us
  matrix products: 152 us -> 120 us
  local copies, waits for them, and re-layouts: 38.1 us -> 15.1 us
    reduce_scatter x13 -> x0, waiting for transfers between devices: 1000 us -> none  [the longest x1 180 us: on_device(): lax.psum_scatter(grad_gate.astype(jnp.bfloat16), 'blk', scatter_dimension...]
    pallas_call x0 -> x16, Pallas kernels: none -> 830 us  [the longest x14 823 us: run(): pl.pallas_call(body, out_shape=out_shape, in_specs=[in_vmem if i in vmem...]
    all_gather x13 -> x0, waiting for transfers between devices: 747 us -> none  [the longest x1 154 us: on_device(): lax.all_gather(shards[4], 'blk', axis=0, tiled=True)]
    psum x1 -> x0, blocking collectives: 46 us -> none  [on_device(): lax.psum((grad_attn_in, grad_attn_out, grad_ff_in, grad_ff_out), ('heads'...]
    dot_general x14 -> x3, matrix products: 62.4 us -> 25.6 us  [the longest x1 11.4 us: on_device(): gate_lin = jnp.dot(normed_two, gate_full, preferred_element_type=f32)]
    dot_general x14 -> x12, matrix products: 90 us -> 94.5 us  [contract(): lax.dot_general(left_side, right_side, (((left_dim,), (right_dim,)), ((),...]
  transfers between devices with their start and end apart: 26 -> 5, of which waited for: 26 -> 3; matrix products, arithmetic and copies ran while one was open for 8% -> 6% of each run, Pallas kernels for 0% -> 26%
where the time goes in v1:
time: 1030 us; the launch traced here: 1020 us
  Pallas kernels  830 us (81%)
  matrix products  120 us (12%)
  other arithmetic  41.4 us (4%)
  local copies, waits for them, and re-layouts  15.1 us (1%)
    pallas_call x14, Pallas kernels, run(): pl.pallas_call(body, out_shape=out_shape, in_specs=[in_vmem if i in vmem...  823 us
    dot_general x12, matrix products, contract(): lax.dot_general(left_side, right_side, (((left_dim,), (right_dim,)), ((),...  94.5 us
  transfers between devices with their start and end apart: 5, of which 3 were waited for; matrix products, arithmetic and copies ran while one was open for 6% of the time, Pallas kernels for 26%

profile of v1, /device:TPU:2, one launch (start us, length us, event | category | flops | bytes accessed | tf_op | source)
XLA Modules:
  0.0 1021.0 jit_solution(2674712424281948029)
XLA Ops:
  0.7 1.4 fusion.33
  2.2 1.3 select_reduce_fusion
  4.8 2.0 fusion.92.kinds
  8.2 1.3 fusion.26.own
  9.4 1.3 pad_maximum_fusion.1.attn
  10.7 1.3 copy-done.4
  12.1 195.1 %shard_map.246 = (bf16[4,128,2304]{2,1,0:T(8,128)(2,1)}, bf16[4,2,288,1536]{3,2,1,0:T(8,128)(2,1)}, bf16[4,2,2,144,2304]{4,3,2,1,0:T(8,128)(2,1)}, bf16[4,2,2,14...) custom-call(bf16[128,2304]{1,0:T(8,128)(2,1)S(1)} %fusion.26.own, bf16[288,1536]{1,0:T(8,128)(2,1)S(1)} %pad_maximum_fusion.1.attn, ...), custom_call_target="tpu_custom_call" | custom-call | bytes 20000000 | tf_op jit(solution)/shard_map/pallas_call | solution.py:973
  207.2 5.2 fusion.9
  212.5 1.3 fusion.83
  213.9 62.0 %shard_map.247 = bf16[4,2,512,512]{3,2,1,0:T(8,128)(2,1)S(1)} custom-call(bf16[512,512]{1,0:T(8,128)(2,1)S(1)} %pad_maximum_fusion.3.own), custom_call_target="tpu_custom_call" | custom-call | tf_op jit(solution)/shard_map/pallas_call | solution.py:973
  276.0 2.8 shard_map.248
  278.8 3.9 convolution_convert_fusion.5
  282.8 29.9 %shard_map.249 = f32[128,2304]{1,0:T(8,128)S(1)} custom-call(bf16[4,128,2304]{2,1,0:T(8,128)(2,1)S(1)} %bitcast.97), custom_call_target="tpu_custom_call" | custom-call | tf_op jit(solution)/shard_map/pallas_call | solution.py:973
  313.5 45.5 %shard_map.250 = bf16[4,128,2304]{2,1,0:T(8,128)(2,1)S(1)} custom-call(bf16[128,2304]{1,0:T(8,128)(2,1)S(1)} %multiply_convert_fusion.3.own), custom_call_target="tpu_custom_call" | custom-call | tf_op jit(solution)/shard_map/pallas_call | solution.py:973
  359.0 11.4 %fusion.95 = f32[512,2304]{1,0:T(8,128)} fusion(bf16[512,2304]{1,0:T(8,128)(2,1)S(1)} %bitcast.89, bf16[2304,2304]{1,0:T(8,128)(2,1)} %bitcast.114), kind=kOutput, calls=%fused_computation.162 | convolution fusion | flops 5435817984 | bytes 17694720 | tf_op jit(solution)/shard_map/dot_general | solution.py:1333
  370.5 9.0 multiply_convert_fusion.1
  379.5 10.8 %convolution_convert_fusion.4 = bf16[512,2304]{1,0:T(8,128)(2,1)S(1)} fusion(bf16[512,2304]{1,0:T(8,128)(2,1)S(1)} %get-tuple-element.62, bf16[2304,2304]{1,0:T(8,128)(2,1)} %bitcast.116), kind=kOutput, calls=%fused_computation.17 | convolution fusion | flops 5436997632 | bytes 15335424 | tf_op jit(solution)/shard_map/dot_general | solution.py:22
  390.3 40.7 %shard_map.251 = f32[128,2304]{1,0:T(8,128)S(1)} custom-call(bf16[4,128,2304]{2,1,0:T(8,128)(2,1)S(1)} %bitcast.98), custom_call_target="tpu_custom_call" | custom-call | tf_op jit(solution)/shard_map/pallas_call | solution.py:973
  432.2 1.2 fusion.25
  433.4 38.3 %shard_map.252 = bf16[4,128,2304]{2,1,0:T(8,128)(2,1)S(1)} custom-call(bf16[128,2304]{1,0:T(8,128)(2,1)S(1)} %get-tuple-element.56.own), custom_call_target="tpu_custom_call" | custom-call | tf_op jit(solution)/shard_map/pallas_call | solution.py:973
  471.7 15.4 %multiply_convert_fusion = (bf16[512,2304]{1,0:T(8,128)(2,1)}, bf16[512,2304]{1,0:T(8,128)(2,1)S(1)}) fusion(f32[512,2304]{1,0:T(8,128)} %fusion.95, f32[512,2304]{1,0:T(8,128)} %get-tuple-element.63, bf16[512,2304]{1,0:T(8,128)(2,1)S(1)} %bitcast.93, bf16[2304,2304]{1,0:T(8,128)(2,1)} %bitcast.117), kind=kOutput, calls=%fused_computation.14 | convolution fusion | flops 5464129536 | bytes 27131904 | tf_op jit(solution)/shard_map/dot_general | solution.py:22
  487.2 12.2 %fusion.96 = f32[512,2304]{1,0:T(8,128)} fusion(bf16[512,2304]{1,0:T(8,128)(2,1)S(1)} %get-tuple-element.49, bf16[2304,2304]{1,0:T(8,128)(2,1)} %bitcast.115), kind=kOutput, calls=%fused_computation.163 | convolution fusion | flops 5435817984 | bytes 17694720 | tf_op jit(solution)/shard_map/dot_general | solution.py:22
  499.4 11.0 %fusion.7 = bf16[512,2304]{1,0:T(8,128)(2,1)S(1)} fusion(f32[512,2304]{1,0:T(8,128)} %fusion.96, bf16[512,2304]{1,0:T(8,128)(2,1)} %get-tuple-element.48, bf16[2304,2304]{1,0:T(8,128)(2,1)} %bitcast.110), kind=kOutput, calls=%fused_computation.19 | convolution fusion | flops 5438177280 | bytes 20054016 | tf_op jit(solution)/shard_map/dot_general | solution.py:22
  510.5 39.9 %shard_map.253 = f32[128,2304]{1,0:T(8,128)S(1)} custom-call(bf16[4,128,2304]{2,1,0:T(8,128)(2,1)S(1)} %bitcast.95), custom_call_target="tpu_custom_call" | custom-call | tf_op jit(solution)/shard_map/pallas_call | solution.py:973
  551.4 1.6 multiply_reduce_fusion.1
  553.6 1.5 multiply_convert_fusion.2.own
  555.1 31.7 %shard_map.254 = bf16[4,128,2304]{2,1,0:T(8,128)(2,1)S(1)} custom-call(bf16[128,2304]{1,0:T(8,128)(2,1)S(1)} %multiply_convert_fusion.2.own), custom_call_target="tpu_custom_call" | custom-call | tf_op jit(solution)/shard_map/pallas_call | solution.py:973
  586.8 3.2 fusion.20.up_ref
  590.0 4.8 shard_map.255
  594.9 43.8 %shard_map.256 = bf16[512,512]{1,0:T(8,128)(2,1)S(1)} custom-call(bf16[4,2,512,512]{3,2,1,0:T(8,128)(2,1)S(1)} %bitcast.88), custom_call_target="tpu_custom_call" | custom-call | tf_op jit(solution)/shard_map/pallas_call | solution.py:973
  639.3 1.1 fusion.91
  640.5 1.2 fusion.90
  641.7 1.2 fusion.89
  642.9 1.2 fusion.88
  644.0 1.2 fusion.87
  645.2 1.2 fusion.86
  646.5 5.6 convolution_convert_fusion.3
  652.2 28.8 %shard_map.257 = f32[128,2304]{1,0:T(8,128)S(1)} custom-call(bf16[4,128,2304]{2,1,0:T(8,128)(2,1)S(1)} %bitcast.96), custom_call_target="tpu_custom_call" | custom-call | tf_op jit(solution)/shard_map/pallas_call | solution.py:973
  681.0 0.9 fusion.32
  682.7 1.0 collective-permute-start
  683.7 8.4 convolution_convert_fusion
  692.0 8.3 convolution_convert_fusion.1
  700.4 8.4 convolution_convert_fusion.2
  708.7 4.3 copy.28
  713.7 2.6 fusion.31
  716.3 63.6 %shard_map.261 = bf16[2,144,2304]{2,1,0:T(8,128)(2,1)S(1)} custom-call(bf16[4,2,2,144,2304]{4,3,2,1,0:T(8,128)(2,1)} %bitcast.104), custom_call_target="tpu_custom_call" | custom-call | tf_op jit(solution)/shard_map/pallas_call | solution.py:973
  779.9 1.8 convert_bitcast_fusion
  781.7 62.3 %shard_map.260 = bf16[2,144,2304]{2,1,0:T(8,128)(2,1)S(1)} custom-call(bf16[4,2,2,144,2304]{4,3,2,1,0:T(8,128)(2,1)} %bitcast.103), custom_call_target="tpu_custom_call" | custom-call | tf_op jit(solution)/shard_map/pallas_call | solution.py:973
  844.0 1.8 bitcast_convert_fusion
  845.8 62.8 %shard_map.259 = bf16[2,144,2304]{2,1,0:T(8,128)(2,1)S(1)} custom-call(bf16[4,2,2,144,2304]{4,3,2,1,0:T(8,128)(2,1)} %bitcast.102), custom_call_target="tpu_custom_call" | custom-call | tf_op jit(solution)/shard_map/pallas_call | solution.py:973
  908.6 1.8 bitcast_convert_fusion.1
  911.5 4.3 convolution_convert_fusion.6
  915.8 2.5 copy.29
  920.0 3.1 convolution_convert_fusion.7
  923.9 0.9 collective-permute-start.2
  924.8 6.0 pad_maximum_fusion.given
  930.8 78.4 %shard_map.258 = bf16[288,1536]{1,0:T(8,128)(2,1)S(1)} custom-call(bf16[4,2,288,1536]{3,2,1,0:T(8,128)(2,1)} %pad_maximum_fusion.given), custom_call_target="tpu_custom_call" | custom-call | tf_op jit(solution)/shard_map/pallas_call | solution.py:973
  1009.4 3.8 collective-permute-start.3
  1013.2 0.9 slice_bitcast_fusion
  1014.1 1.1 collective-permute-done.3
  1015.2 1.4 collective-permute-start.4
  1016.6 0.8 fusion.94
  1017.4 0.9 slice.134
  1018.3 1.8 collective-permute-done.4
  (131 shorter events, 12.0 us)
Async XLA Ops:
  0.6 10.1 copy-start.3
  0.7 10.1 copy-start.2
  0.7 211.8 %copy-start.28 = (f32[128]{0:T(128)}, f32[128]{0:T(128)S(1)}, u32[]{:S(2)}) copy-start(f32[128]{0:T(128)S(1)} %multiply_exponential_fusion) | copy-start | bytes 1540
  2.1 205.0 %copy-start.34 = (f32[128]{0:T(128)}, f32[128]{0:T(128)S(1)}, u32[]{:S(2)}) copy-start(f32[128]{0:T(128)S(1)} %add_rsqrt_fusion.3) | copy-start | bytes 1540
  6.7 205.7 %copy-start.26 = (f32[512]{0:T(512)}, f32[512]{0:T(512)S(1)}, u32[]{:S(2)}) copy-start(f32[512]{0:T(512)S(1)} %add_convert_fusion.1) | copy-start | bytes 6148
  10.7 1.3 copy-start.4
  278.8 3.9 copy-start.5
  278.8 3.9 copy-start.7
  278.8 3.9 copy-start.9
  282.7 30.1 %copy-start.32 = (f32[2304]{0:T(1024)S(1)}, f32[2304]{0:T(1024)}, u32[]{:S(2)}) copy-start(f32[2304]{0:T(1024)} %param.23) | copy-start | bytes 27652
  282.7 30.1 %copy-start.33 = (f32[2304]{0:T(1024)S(1)}, f32[2304]{0:T(1024)}, u32[]{:S(2)}) copy-start(f32[2304]{0:T(1024)} %param.22) | copy-start | bytes 27652
  282.8 30.1 %copy-start.11 = (bf16[128,2304]{1,0:T(8,128)(2,1)S(1)}, bf16[128,2304]{1,0:T(8,128)(2,1)}, u32[]{:S(2)}) copy-start(bf16[128,2304]{1,0:T(8,128)(2,1)} %param.15) | copy-start | bytes 1769476
  313.5 57.0 %slice-start = ((s8[10616832]{0:T(1024)(128)(4,1)}), s8[2228224]{0:T(1024)(128)(4,1)S(1)}, s32[]{:S(2)}) async-start(s8[10616832]{0:T(1024)(128)(4,1)} %bitcast.111), calls=%async_computation | async-start | bytes 4456448
  359.0 11.5 %slice-start.1 = ((s8[10616832]{0:T(1024)(128)(4,1)}), s8[4194304]{0:T(1024)(128)(4,1)S(1)}, s32[]{:S(2)}) async-start(s8[10616832]{0:T(1024)(128)(4,1)} %bitcast.111), calls=%async_computation.1 | async-start | bytes 8388608
  359.0 11.5 %slice-start.2 = ((s8[10616832]{0:T(1024)(128)(4,1)}), s8[4194304]{0:T(1024)(128)(4,1)S(1)}, s32[]{:S(2)}) async-start(s8[10616832]{0:T(1024)(128)(4,1)} %bitcast.111), calls=%async_computation.2 | async-start | bytes 8388608
  379.5 10.8 %copy-start.36 = (bf16[512,2304]{1,0:T(8,128)(2,1)}, bf16[512,2304]{1,0:T(8,128)(2,1)S(1)}, u32[]{:S(2)}) copy-start(bf16[512,2304]{1,0:T(8,128)(2,1)S(1)} %get-tuple-element.62) | copy-start | bytes 7077892
  390.3 40.9 %copy-start.13 = (bf16[128,2304]{1,0:T(8,128)(2,1)S(1)}, bf16[128,2304]{1,0:T(8,128)(2,1)}, u32[]{:S(2)}) copy-start(bf16[128,2304]{1,0:T(8,128)(2,1)} %param.16) | copy-start | bytes 1769476
  471.7 15.4 %copy-start = (bf16[4,128,2304]{2,1,0:T(8,128)(2,1)}, bf16[4,128,2304]{2,1,0:T(8,128)(2,1)S(1)}, u32[]{:S(2)}) copy-start(bf16[4,128,2304]{2,1,0:T(8,128)(2,1)S(1)} %shard_map.252) | copy-start | bytes 7077892
  487.2 12.2 %copy-start.38 = (bf16[512,2304]{1,0:T(8,128)(2,1)}, bf16[512,2304]{1,0:T(8,128)(2,1)S(1)}, u32[]{:S(2)}) copy-start(bf16[512,2304]{1,0:T(8,128)(2,1)S(1)} %get-tuple-element.49) | copy-start | bytes 7077892
  586.8 3.2 copy-start.6
  586.8 3.2 copy-start.10
  638.7 0.7 copy-start.27
  638.7 0.7 copy-start.29
  646.5 5.6 copy-start.30
  652.1 28.9 %copy-start.12 = (bf16[128,2304]{1,0:T(8,128)(2,1)S(1)}, bf16[128,2304]{1,0:T(8,128)(2,1)}, u32[]{:S(2)}) copy-start(bf16[128,2304]{1,0:T(8,128)(2,1)} %param.15) | copy-start | bytes 1769476
  652.1 28.9 %copy-start.35 = (f32[128]{0:T(128)S(1)}, f32[128]{0:T(128)}, u32[]{:S(2)}) copy-start(f32[128]{0:T(128)} %copy-done.34) | copy-start | bytes 1540
  652.1 29.8 %copy-start.15 = (f32[1,2304]{1,0:T(1,128)S(1)}, f32[1,2304]{1,0:T(1,128)}, u32[]{:S(2)}) copy-start(f32[1,2304]{1,0:T(1,128)} %stack.33) | copy-start | bytes 27652
  652.1 29.8 %copy-start.17 = (f32[1,2304]{1,0:T(1,128)S(1)}, f32[1,2304]{1,0:T(1,128)}, u32[]{:S(2)}) copy-start(f32[1,2304]{1,0:T(1,128)} %stack.32) | copy-start | bytes 27652
  652.1 29.8 %copy-start.20 = (f32[1,2304]{1,0:T(1,128)S(1)}, f32[1,2304]{1,0:T(1,128)}, u32[]{:S(2)}) copy-start(f32[1,2304]{1,0:T(1,128)} %stack.31) | copy-start | bytes 27652
  652.2 31.5 %copy-start.1 = (bf16[4,128,2304]{2,1,0:T(8,128)(2,1)S(1)}, bf16[4,128,2304]{2,1,0:T(8,128)(2,1)}, u32[]{:S(2)}) copy-start(bf16[4,128,2304]{2,1,0:T(8,128)(2,1)} %copy-done) | copy-start | bytes 7077892
  652.2 31.5 %copy-start.37 = (bf16[512,2304]{1,0:T(8,128)(2,1)S(1)}, bf16[512,2304]{1,0:T(8,128)(2,1)}, u32[]{:S(2)}) copy-start(bf16[512,2304]{1,0:T(8,128)(2,1)} %copy-done.36) | copy-start | bytes 7077892
  682.0 10.1 copy-start.23
  682.7 9.4 copy-start.40
  682.7 235.6 %collective-permute-start = (f32[4,2304]{1,0:T(4,128)}, f32[4,2304]{1,0:T(4,128)}, u32[]{:S(2)}, u32[]{:S(2)}) collective-permute-start(f32[4,2304]{1,0:T(4,128)} %pad_maximum_fusion.4), channel_id=1, source_target_pairs={{0,8},{8,0},{16,24},{24,16},{1,9},{9,1},{17,25},{25,17},{2,10},{10... | collective-permute-start | bytes 110600 | tf_op jit(solution)/shard_map/ppermute | solution.py:241
  692.0 8.3 copy-start.39
  908.6 2.6 copy-start.14
  908.6 2.9 copy-start.31
  915.7 2.5 copy-start.16
  915.7 2.5 copy-start.18
  915.8 2.5 copy-start.21
  915.8 2.5 copy-start.24
  915.8 4.2 copy-start.8
  919.1 4.0 collective-permute-start.1
  919.9 3.2 copy-start.19
  919.9 3.2 copy-start.22
  919.9 3.2 copy-start.25
  923.9 85.5 %collective-permute-start.2 = (f32[4,2304]{1,0:T(4,128)S(1)}, f32[4,2304]{1,0:T(4,128)S(1)}, u32[]{:S(2)}, u32[]{:S(2)}) collective-permute-start(f32[4,2304]{1,0:T(4,128)S(1)} %fusion.121), channel_id=1, source_target_pairs={{0,1},{1,0},{2,3},{3,2},{4,5},{5,4},{6,7},{7,6},{8,9},{9,8},{10,11... | collective-permute-start | bytes 110600 | tf_op jit(solution)/shard_map/ppermute | solution.py:244
  1009.4 5.7 collective-permute-start.3
  1015.2 4.9 collective-permute-start.4

commit v2 on v1

v2 whole, which is shorter than its diff:
```python
import math

import jax
import jax.numpy as jnp
from jax import lax
from jax.experimental import pallas as pl
from jax.experimental.pallas import tpu as pltpu
from jax.sharding import PartitionSpec as P

HEAD_DIM = 256


softcap = 50.0
epsilon = 1e-06
score_scale = HEAD_DIM ** (-0.5)
bf16 = jnp.bfloat16
f32 = jnp.float32


def contract(left_side, right_side, left_dim, right_dim):
    return lax.dot_general(
        left_side,
        right_side,
        (((left_dim,), (right_dim,)), ((), ())),
        preferred_element_type=f32,
    )


def factor_of(values):
    return lax.rsqrt(jnp.mean(values * values, axis=-1, keepdims=True) + epsilon)


def normalize(values, weight_gain):
    return values * factor_of(values) * (1.0 + weight_gain)


def normalize_back(values, weight_gain, upstream):
    factor = factor_of(values)
    unit = values * factor
    scaled = upstream * (1.0 + weight_gain)
    inner = jnp.mean(scaled * unit, axis=-1, keepdims=True)
    return (scaled - unit * inner) * factor, jnp.sum(upstream * unit, axis=0)


def rope_tables(positions):
    half_dim = HEAD_DIM // 2
    frequency = jnp.exp(
        jnp.arange(half_dim, dtype=f32) * (-2.0 * math.log(10000.0) / HEAD_DIM)
    )
    angles = positions.astype(f32)[:, None] * frequency[None, :]
    return (jnp.cos(angles), jnp.sin(angles))


def rotate(tensor, cosine, sine_table):
    half_dim = HEAD_DIM // 2
    first_half = tensor[..., :half_dim]
    second_half = tensor[..., half_dim:]
    return jnp.concatenate(
        [
            first_half * cosine - second_half * sine_table,
            second_half * cosine + first_half * sine_table,
        ],
        axis=-1,
    )


def swap_core(v):
    return lax.ppermute(v, "heads", [(i, i ^ 1) for i in range(4)])


def swap_y(v):
    return lax.ppermute(v, "heads", [(i, i ^ 2) for i in range(4)])


def swap_x(v):
    blocks = lax.axis_size("blk")
    return lax.ppermute(v, "blk", [(i, i ^ 1) for i in range(blocks)])


def pair_up(own, other, place, axis):
    first = jnp.where(place == 0, own, other)
    second = jnp.where(place == 0, other, own)
    return jnp.concatenate([first, second], axis=axis)


def shift_z(v, step, senders):
    pairs = []
    for z in senders:
        for x in range(2):
            pairs.append((2 * z + x, 2 * (z + step) + x))
    return lax.ppermute(v, "blk", pairs)


class Place:
    def __init__(self):
        self.blocks = lax.axis_size("blk")
        self.nz = self.blocks // 2
        self.b = lax.axis_index("blk")
        self.h = lax.axis_index("heads")
        self.z, self.x = self.b // 2, self.b % 2
        self.y, self.c = self.h // 2, self.h % 2


def gather_z(at, unit):
    nz = at.nz
    up, down = unit, unit
    ups, downs = [None], [None]
    for s in range(1, nz):
        up = shift_z(up, 1, range(s - 1, nz - 1))
        down = shift_z(down, -1, range(1, nz - s + 1))
        ups.append(up)
        downs.append(down)
    return [unit] + [jnp.where(at.z >= s, ups[s], downs[nz - s]) for s in range(1, nz)]


def scatter_z(at, parts):
    nz = at.nz
    up = down = None
    for t in range(1, nz):
        k = nz - t
        send_up = parts[nz - k].astype(f32)
        send_down = parts[k].astype(f32)
        if up is not None:
            send_up = send_up + up.astype(f32)
            send_down = send_down + down.astype(f32)
        up = shift_z(send_up.astype(bf16), 1, range(0, nz - k))
        down = shift_z(send_down.astype(bf16), -1, range(k, nz))
    return parts[0].astype(f32) + (up.astype(f32) + down.astype(f32))


def deal_z(at, parts):
    nz = at.nz
    got = [parts[0]]
    for s in range(1, nz):
        up = shift_z(parts[nz - s], s, range(0, nz - s))
        down = shift_z(parts[nz - s], s - nz, range(nz - s, nz))
        got.append(jnp.where(at.z >= s, up, down))
    return got


def turn(at, whole):
    return [
        lax.dynamic_index_in_dim(whole, (at.z - s) % at.nz, 0, keepdims=False)
        for s in range(at.nz)
    ]


def unturn(at, parts):
    whole = jnp.zeros((at.nz,) + parts[0].shape, parts[0].dtype)
    for s, part in enumerate(parts):
        whole = lax.dynamic_update_index_in_dim(whole, part, (at.z - s) % at.nz, 0)
    return whole


def gather_zx(at, unit):
    got = []
    for part in gather_z(at, unit):
        got.append(pair_up(part[None], swap_x(part)[None], at.x, 0))
    return unturn(at, got)


def gather_xz(at, unit):
    both = pair_up(unit[None], swap_x(unit)[None], at.x, 0)
    return unturn(at, gather_z(at, both))


def pick(pair, place):
    mine = jnp.where(place == 0, pair[0], pair[1])
    other = jnp.where(place == 0, pair[1], pair[0])
    return mine, other


def scatter_zx(at, parts):
    total = scatter_z(at, parts)
    mine, other = pick(total, at.x)
    return mine + swap_x(other.astype(bf16)).astype(f32)


def scatter_xz(at, parts):
    sums = []
    for part in parts:
        mine, other = pick(part, at.x)
        sums.append(mine.astype(f32) + swap_x(other.astype(bf16)).astype(f32))
    return scatter_z(at, sums)


def rows_to_block(at, own):
    both = pair_up(own, swap_core(own), at.c, 0)
    pair = pair_up(both[None], swap_y(both)[None], at.y, 0)
    return pair.reshape(4 * own.shape[0], own.shape[1])


def rows_from_block(at, partial_sum):
    rows = partial_sum.shape[0] // 4
    parts = partial_sum.reshape(2, 2, rows, partial_sum.shape[1])
    mine, other = pick(parts.swapaxes(0, 1), at.c)
    total = mine + swap_core(other.astype(bf16)).astype(f32)
    mine, other = pick(total, at.y)
    return mine + swap_y(other.astype(bf16)).astype(f32)


def spread_weight(at, shard):
    rows, units = shard.shape
    half = rows // 2
    keep, send = pick(shard.reshape(2, half, units), at.c)
    wide = pair_up(keep[None], swap_core(send)[None], at.c, 0)
    quarter = 2 * units // at.nz
    per_core = units // quarter
    pieces = wide.reshape(2, half, per_core, quarter).transpose(0, 2, 1, 3)
    pieces = pieces.reshape(at.nz, half, quarter)
    got = unturn(at, deal_z(at, turn(at, pieces)))
    got = pair_up(got[:, None], swap_x(got)[:, None], at.x, 1)
    got = pair_up(got, swap_y(got), at.y, 3)
    got = pair_up(got[:, :, None], swap_core(got)[:, :, None], at.c, 2)
    return got.reshape(at.blocks * rows, 2 * quarter)


def collect_weight(at, grad):
    depth, width = grad.shape
    half, quarter = depth // (2 * at.blocks), width // 2
    parts = grad.reshape(at.nz, 2, 2, half, width)
    mine, other = pick(parts.transpose(2, 0, 1, 3, 4), at.c)
    total = mine + swap_core(other.astype(bf16)).astype(f32)
    mine, other = pick((total[..., :quarter], total[..., quarter:]), at.y)
    total = mine + swap_y(other.astype(bf16)).astype(f32)
    mine, other = pick((total[:, 0], total[:, 1]), at.x)
    total = mine + swap_x(other.astype(bf16)).astype(f32)
    got = unturn(at, deal_z(at, turn(at, total.astype(bf16))))
    per_core = at.nz // 2
    wide = got.reshape(2, per_core, half, quarter).transpose(0, 2, 1, 3)
    wide = wide.reshape(2, half, per_core * quarter)
    mine, other = pick(wide, at.c)
    rows = pair_up(mine, swap_core(other), at.c, 0)
    return rows.astype(f32)


def sum_all(at, values):
    total = values
    for bit in (1, 2):
        total = total + lax.ppermute(total, "heads", [(i, i ^ bit) for i in range(4)])
    bit = 1
    while bit < at.blocks:
        total = total + lax.ppermute(total, "blk", [(i, i ^ bit) for i in range(at.blocks)])
        bit *= 2
    return total


class Permutes:
    def __init__(self, at):
        self.at = at
        self.block, self.blocks, self.nz = at.b, at.blocks, at.nz

    def split(self, whole):
        return turn(self.at, whole.reshape((self.nz, whole.shape[0] // self.nz) + whole.shape[1:]))

    def start(self, own, attn_shard, gate, up):
        at = self.at
        attn_full = gather_zx(at, attn_shard).reshape(own.shape[1], -1)
        return rows_to_block(at, own), attn_full, spread_weight(at, gate), spread_weight(at, up)

    def scatter_heads_deal(self, partial, down):
        return rows_from_block(self.at, partial), spread_weight(self.at, down)

    def gather_kv(self, own):
        return gather_zx(self.at, own).reshape((self.blocks,) + own.shape)

    def gather_z_copy(self, own, pieces):
        return self.gather_z(own), pieces

    def gather_z(self, own):
        whole = unturn(self.at, gather_z(self.at, own))
        return whole.reshape(-1, own.shape[1])

    def scatter_z(self, partial):
        return scatter_z(self.at, self.split(partial))

    def scatter_z_sums(self, partial, grad):
        return self.scatter_z(partial), collect_weight(self.at, grad)

    def gather_heads_back(self, own, sums):
        return rows_to_block(self.at, own), sums

    def scatter_kv_sums(self, parts, grad):
        return scatter_xz(self.at, self.split(parts)), collect_weight(self.at, grad)

    def scatter_heads_back(self, partial, sums):
        return rows_from_block(self.at, partial), sums

    def finish(self, attn_grad, grad, gains):
        rows = attn_grad.shape[0] // self.blocks
        attn = scatter_xz(self.at, self.split(attn_grad.reshape(self.blocks, rows, -1)))
        return attn, collect_weight(self.at, grad), sum_all(self.at, gains)


MESH = pl.DeviceIdType.MESH
DMA = pltpu.SemaphoreType.DMA
anywhere = pl.BlockSpec(memory_space=pl.ANY)
in_vmem = pl.BlockSpec(memory_space=pltpu.VMEM)


def remote(src, dst, send_sem, recv_sem, target):
    return pltpu.make_async_remote_copy(
        src_ref=src,
        dst_ref=dst,
        send_sem=send_sem,
        recv_sem=recv_sem,
        device_id=target,
        device_id_type=MESH,
    )


def flip(bit, by):
    return 1 - bit if by else bit


def exclusive_or(z, i):
    low, high = lax.rem(z, 2), lax.rem(z // 2, 2)
    rest = z - 2 * high - low
    return rest + 2 * flip(high, i // 2) + flip(low, i % 2)


class Spot:
    def __init__(self, nz):
        self.nz = nz
        h, b = lax.axis_index("heads"), lax.axis_index("blk")
        self.y, self.c = h // 2, h % 2
        self.z, self.x = b // 2, b % 2

    def device(self, z=None, x=None, y=None, c=None):
        z = self.z if z is None else z
        x = self.x if x is None else x
        y = self.y if y is None else y
        c = self.c if c is None else c
        return (2 * y + c, 2 * z + x)

    def partner(self):
        return self.device(c=1 - self.c)

    def greet(self):
        found = []
        for dx, dy, dc in [(0, 0, 1), (1, 0, 0), (1, 0, 1), (0, 1, 0), (0, 1, 1), (1, 1, 0), (1, 1, 1)]:
            found.append(self.device(x=flip(self.x, dx), y=flip(self.y, dy), c=flip(self.c, dc)))
        for s in range(1, self.nz):
            z = lax.rem(self.z + s, self.nz)
            found += [self.device(z=z), self.device(z=z, c=1 - self.c)]
        barrier = pltpu.get_barrier_semaphore()
        for device in found:
            pl.semaphore_signal(barrier, inc=1, device_id=device, device_id_type=MESH)
        pl.semaphore_wait(barrier, len(found))


def add_rows(out, left, right, step=16):
    rows = left.shape[0]

    @pl.loop(0, rows // step)
    def _(i):
        at = pl.ds(pl.multiple_of(i * step, step), step)
        out[at, :] = (left[at, :].astype(f32) + right[at, :].astype(f32)).astype(out.dtype)


class LineGather:
    def __init__(self, spot, entry, send, recv):
        self.spot, self.entry = spot, entry
        self.send, self.recv = send, recv

    def copies(self, s):
        p, nz = self.spot, self.spot.nz
        up_at = lax.rem(p.z - s + 1 + nz, nz)
        down_at = lax.rem(p.z + s - 1, nz)
        up = remote(
            self.entry(up_at),
            self.entry(up_at),
            self.send.at[0, s],
            self.recv.at[0, s],
            p.device(z=lax.rem(p.z + 1, nz)),
        )
        down = remote(
            self.entry(down_at),
            self.entry(down_at),
            self.send.at[1, s],
            self.recv.at[1, s],
            p.device(z=lax.rem(p.z + nz - 1, nz)),
        )
        return (
            ((p.z >= s - 1) & (p.z < nz - 1), p.z >= s, up),
            ((p.z <= nz - s) & (p.z > 0), p.z <= nz - 1 - s, down),
        )

    def start(self, s):
        for sends, _, copy in self.copies(s):
            pl.when(sends)(copy.start)

    def arrive(self, s):
        for _, receives, copy in self.copies(s):
            pl.when(receives)(copy.wait_recv)

    def finish(self):
        for s in range(1, self.spot.nz):
            for sends, _, copy in self.copies(s):
                pl.when(sends)(copy.wait_send)

    def newest(self, s):
        p, nz = self.spot, self.spot.nz
        return (
            (p.z >= s, lax.rem(p.z - s + nz, nz)),
            (p.z <= nz - 1 - s, lax.rem(p.z + s, nz)),
        )


class LineScatter:
    def __init__(self, spot, parts, up, down, send, recv):
        self.spot, self.parts, self.up, self.down = spot, parts, up, down
        self.send, self.recv = send, recv

    def copies(self, t):
        p, nz = self.spot, self.spot.nz
        k = nz - t
        up = remote(
            self.parts.at[lax.rem(p.z + k, nz)],
            self.up.at[t - 1],
            self.send.at[0, t],
            self.recv.at[0, t],
            p.device(z=lax.rem(p.z + 1, nz)),
        )
        down = remote(
            self.parts.at[lax.rem(p.z - k + nz, nz)],
            self.down.at[t - 1],
            self.send.at[1, t],
            self.recv.at[1, t],
            p.device(z=lax.rem(p.z + nz - 1, nz)),
        )
        return (
            (p.z <= nz - 1 - k, (p.z >= 1) & (p.z <= t), up),
            (p.z >= k, (p.z <= nz - 2) & (p.z >= nz - 1 - t), down),
        )

    def start(self, t):
        for sends, _, copy in self.copies(t):
            pl.when(sends)(copy.start)

    def arrive(self, t):
        p, nz = self.spot, self.spot.nz
        k = nz - t
        for way, (_, receives, copy) in enumerate(self.copies(t)):

            @pl.when(receives)
            def _(way=way, copy=copy):
                copy.wait_recv()
                if t < nz - 1:
                    index = lax.rem(p.z + k - 1, nz) if way == 0 else lax.rem(p.z - k + 1 + nz, nz)
                    came = (self.up if way == 0 else self.down).at[t - 1]
                    add_rows(self.parts.at[index], self.parts.at[index], came)

    def finish(self):
        for t in range(1, self.spot.nz):
            for sends, _, copy in self.copies(t):
                pl.when(sends)(copy.wait_send)

    def total(self, out, step=16):
        p, last = self.spot, self.spot.nz - 2
        mine = self.parts.at[p.z]
        inner = (p.z > 0) & (p.z < p.nz - 1)

        @pl.when(p.z == 0)
        def _():
            add_rows(out, mine, self.down.at[last], step)

        @pl.when(p.z == p.nz - 1)
        def _():
            add_rows(out, mine, self.up.at[last], step)

        @pl.when(inner)
        def _():
            @pl.loop(0, out.shape[0] // step)
            def _(i):
                at = pl.ds(pl.multiple_of(i * step, step), step)
                sides = self.up[last, at, :].astype(f32) + self.down[last, at, :].astype(f32)
                out[at, :] = (mine[at, :].astype(f32) + sides).astype(out.dtype)


class Task:
    ins = ()
    outs = ()
    scratch = ()
    vmem_ins = ()
    vmem_outs = ()

    def steps(self, p, ins, outs, scratch):
        raise NotImplementedError


class PlaneGather(Task):
    vmem_ins = (0,)
    vmem_outs = (0,)

    def __init__(self, own):
        self.ins = (own,)
        self.outs = (jax.ShapeDtypeStruct((4,) + own.shape, bf16),)
        self.scratch = (DMA((4,)), DMA((4,)), DMA)

    def steps(self, p, ins, outs, scratch):
        (own,), (whole,), (send, recv, local) = ins, outs, scratch
        part = 2 * p.y + p.c
        keep = pltpu.make_async_copy(own, whole.at[part], local)
        copies = []
        for i, (dx, dy) in enumerate([(1, 0), (0, 1), (1, 1), (0, 0)]):
            target = p.device(x=flip(p.x, dx), y=flip(p.y, dy), c=p.x)
            copies.append(remote(own, whole.at[part], send.at[i], recv.at[part], target))
        *away, home = copies
        for copy in away:
            copy.start()
        pl.when(p.c == p.x)(keep.start)
        pl.when(p.c != p.x)(home.start)
        yield
        for copy in away:
            copy.wait_send()
        pl.when(p.c == p.x)(keep.wait)
        pl.when(p.c != p.x)(home.wait_send)
        for slot in range(4):
            came = remote(own, whole.at[slot], send.at[0], recv.at[slot], p.partner())
            mine = (p.c == p.x) & (part == slot)
            pl.when(jnp.logical_not(mine))(came.wait_recv)


class PlaneScatter(Task):
    vmem_ins = (0,)
    vmem_outs = (0,)

    def __init__(self, partial):
        rows, depth = partial.shape[0] // 4, partial.shape[1]
        self.ins = (partial.reshape(4, rows, depth),)
        self.outs = (jax.ShapeDtypeStruct((rows, depth), f32),)
        self.scratch = (pltpu.VMEM((4, rows, depth), bf16), DMA((4,)), DMA((4,)))

    def steps(self, p, ins, outs, scratch):
        (parts,), (out,), (came, send, recv) = ins, outs, scratch
        head, ours = 2 * p.y + p.x, 2 * p.y + p.c

        def copy_to(part):
            target = p.device(x=p.c, y=part // 2, c=part % 2)
            return remote(parts.at[part], came.at[head], send.at[part], recv.at[head], target)

        for part in range(4):
            here = (p.x == p.c) & (part == ours)
            pl.when(jnp.logical_not(here))(copy_to(part).start)
        yield
        for part in range(4):
            here = (p.x == p.c) & (part == ours)
            pl.when(jnp.logical_not(here))(copy_to(part).wait_send)
            arrived = remote(parts.at[part], came.at[part], send.at[part], recv.at[part], p.partner())
            mine = (p.x == p.c) & (part == head)
            pl.when(jnp.logical_not(mine))(arrived.wait_recv)

        @pl.when(p.x == p.c)
        def _():
            came[head] = parts[ours]

        @pl.loop(0, out.shape[0] // 16)
        def _(i):
            at = pl.ds(pl.multiple_of(i * 16, 16), 16)
            low = came[0, at, :].astype(f32) + came[1, at, :].astype(f32)
            out[at, :] = low + (came[2, at, :].astype(f32) + came[3, at, :].astype(f32))


class PairGather(Task):
    vmem_ins = (0,)
    vmem_outs = (0,)

    def __init__(self, nz, own, trade):
        self.trade = trade
        self.ins = (own,)
        self.outs = (jax.ShapeDtypeStruct((nz, 2) + own.shape, bf16),)
        self.scratch = (DMA((2, nz)), DMA((2, nz)), DMA((nz,)), DMA((nz,)), DMA, DMA, DMA)

    def steps(self, p, ins, outs, scratch):
        (own,), (full,), (send, recv, x_send, x_recv, t_send, t_recv, local) = ins, outs, scratch
        nz = p.nz
        keep = pltpu.make_async_copy(own, full.at[p.z, p.c], local)
        line = LineGather(p, lambda z: full.at[z, p.c], send, recv)

        def across(z):
            here = full.at[z, p.c]
            return remote(here, here, x_send.at[z], x_recv.at[z], p.partner())

        if self.trade:
            same = p.c == p.x
            move = remote(own, full.at[p.z, p.x], t_send, t_recv, p.device(x=1 - p.x, c=1 - p.c))
            pl.when(same)(keep.start)
            pl.when(jnp.logical_not(same))(move.start)
            yield
            pl.when(same)(keep.wait)
            pl.when(jnp.logical_not(same))(move.wait_recv)
        else:
            keep.start()
            keep.wait()
        line.start(1)
        across(p.z).start()
        yield
        for s in range(1, nz):
            line.arrive(s)
            if s < nz - 1:
                line.start(s + 1)
            for came, z in line.newest(s):
                pl.when(came)(across(z).start)
            yield
        line.finish()
        if self.trade:
            pl.when(jnp.logical_not(same))(move.wait_send)
        for z in range(nz):
            across(z).wait()


class ZGather(Task):
    vmem_ins = (0,)
    vmem_outs = (0,)

    def __init__(self, nz, own):
        self.ins = (own,)
        self.outs = (jax.ShapeDtypeStruct((nz,) + own.shape, bf16),)
        self.scratch = (DMA((2, nz)), DMA((2, nz)), DMA)

    def steps(self, p, ins, outs, scratch):
        (own,), (full,), (send, recv, local) = ins, outs, scratch
        line = LineGather(p, lambda z: full.at[z], send, recv)
        keep = pltpu.make_async_copy(own, full.at[p.z], local)
        keep.start()
        keep.wait()
        line.start(1)
        yield
        for s in range(1, p.nz):
            line.arrive(s)
            if s < p.nz - 1:
                line.start(s + 1)
            yield
        line.finish()


class ZScatter(Task):
    vmem_outs = (0,)

    def __init__(self, nz, partial):
        rows, depth = partial.shape[0] // nz, partial.shape[1]
        self.ins = (partial.reshape(nz, rows, depth),)
        self.outs = (jax.ShapeDtypeStruct((rows, depth), f32),)
        line = pltpu.VMEM((nz - 1, rows, depth), bf16)
        self.scratch = (
            pltpu.VMEM((nz, rows, depth), bf16), line, line, DMA((2, nz)), DMA((2, nz)), DMA
        )

    def steps(self, p, ins, outs, scratch):
        (given,), (out,), (parts, up, down, send, recv, local) = ins, outs, scratch
        bring = pltpu.make_async_copy(given, parts, local)
        bring.start()
        bring.wait()
        line = LineScatter(p, parts, up, down, send, recv)
        line.start(1)
        yield
        for t in range(1, p.nz):
            line.arrive(t)
            if t < p.nz - 1:
                line.start(t + 1)
            yield
        line.total(out)
        line.finish()


class PairScatter(Task):
    vmem_outs = (0,)

    def __init__(self, nz, given, trade):
        _, _, rows, width = given.shape
        self.trade = trade
        self.ins = (given,)
        self.outs = (jax.ShapeDtypeStruct((rows, width), bf16),)
        whole = pltpu.VMEM((nz, rows, width), bf16)
        line = pltpu.VMEM((nz - 1, rows, width), bf16)
        self.scratch = (
            whole, whole, line, line,
            DMA((nz,)), DMA((nz,)), DMA((2, nz)), DMA((2, nz)), DMA((nz,)), DMA, DMA, DMA,
        )

    def steps(self, p, ins, outs, scratch):
        (given,), (out,) = ins, outs
        parts, came, up, down, x_send, x_recv, send, recv, local, b_send, b_recv, b_local = scratch
        nz = p.nz
        order = [exclusive_or(p.z, i) for i in (3, 2, 1, 0)]

        def away(z):
            return remote(given.at[z, 1 - p.c], came.at[z], x_send.at[z], x_recv.at[z], p.partner())

        def bring(z):
            return pltpu.make_async_copy(given.at[z, p.c], parts.at[z], local.at[z])

        for z in order:
            away(z).start()
            bring(z).start()
        yield
        for z in order:
            away(z).wait_recv()
            bring(z).wait()
            add_rows(parts.at[z], parts.at[z], came.at[z])
        line = LineScatter(p, parts, up, down, send, recv)
        line.start(1)
        yield
        for t in range(1, nz):
            line.arrive(t)
            if t < nz - 1:
                line.start(t + 1)
            yield
        if not self.trade:
            line.total(out)
        else:
            line.total(came.at[0])
            same = p.c == p.x
            back = remote(came.at[0], out, b_send, b_recv, p.device(x=1 - p.x, c=1 - p.c))
            keep = pltpu.make_async_copy(came.at[0], out, b_local)
            pl.when(same)(keep.start)
            pl.when(jnp.logical_not(same))(back.start)
            yield
            pl.when(same)(keep.wait)
            pl.when(jnp.logical_not(same))(back.wait)
        for z in order:
            away(z).wait_send()
        line.finish()


class Deal:
    def __init__(self, p, shard, place, quarter, send, recv):
        self.p, self.shard, self.place, self.quarter = p, shard, place, quarter
        self.send, self.recv = send, recv
        self.per_core = p.nz // 2

    def piece(self, piece, half):
        columns = pl.ds(piece * self.quarter, self.quarter)
        return self.shard.at[half, :, columns]

    def away(self, piece, half):
        p = self.p
        z = p.c * self.per_core + piece
        return z, remote(
            self.piece(piece, half),
            self.place(p.z, half),
            self.send.at[2 * piece + half],
            self.recv.at[p.z],
            p.device(z=z, c=half),
        )

    def local(self, piece):
        p = self.p
        columns = pl.ds(piece * self.quarter, self.quarter)
        return pltpu.make_async_copy(
            self.shard.at[p.c, :, columns], self.place(p.z, p.c), self.recv.at[p.z]
        )

    def start(self, in_plane):
        p = self.p
        for piece in range(self.per_core):
            for half in range(2):
                z, copy = self.away(piece, half)
                if in_plane:
                    pl.when((z == p.z) & (p.c != half))(copy.start)
                    pl.when((z == p.z) & (p.c == half))(self.local(piece).start)
                else:
                    pl.when(z != p.z)(copy.start)

    def arrive(self, source):
        p = self.p
        here = self.place(source, p.c)
        ours = (source == p.z) & (p.c == p.z // self.per_core)
        came = remote(here, here, self.send.at[0], self.recv.at[source], p.partner())
        pl.when(jnp.logical_not(ours))(came.wait_recv)
        pl.when(ours)(self.local(0).wait)

    def finish(self):
        p = self.p
        for piece in range(self.per_core):
            for half in range(2):
                z, copy = self.away(piece, half)
                here = (z == p.z) & (p.c == half)
                pl.when(jnp.logical_not(here))(copy.wait_send)


class DealTask(Task):
    vmem_outs = (0,)

    def __init__(self, nz, shard):
        rows, units = shard.shape
        self.ins = (shard.reshape(2, rows // 2, units),)
        self.outs = (jax.ShapeDtypeStruct((nz, rows // 2, 2 * units // nz), bf16),)
        self.scratch = (DMA((nz,)), DMA((nz,)))

    def steps(self, p, ins, outs, scratch):
        (shard,), (pieces,), (send, recv) = ins, outs, scratch
        deal = Deal(p, shard, lambda z, half: pieces.at[z], pieces.shape[-1], send, recv)
        deal.start(False)
        deal.start(True)
        yield
        for i in range(p.nz):
            deal.arrive(exclusive_or(p.z, i))
        deal.finish()


class Copies(Task):
    vmem_outs = (0,)

    def __init__(self, nz, given, dealt):
        self.dealt = dealt
        if dealt:
            _, half, quarter = given.shape
            self.ins = (given,)
        else:
            rows, units = given.shape
            half, quarter = rows // 2, 2 * units // nz
            self.ins = (given.reshape(2, half, units),)
        self.quarter = quarter
        self.outs = (jax.ShapeDtypeStruct((nz, 2, 2, half, 2 * quarter), bf16),)
        self.scratch = (
            DMA((nz,)), DMA((nz,)), DMA((nz,)), DMA((nz,)), DMA((nz, 2)), DMA((nz, 2)),
            DMA((nz, 2)), DMA((nz, 2)),
        )

    def steps(self, p, ins, outs, scratch):
        (given,), (full,) = ins, outs
        d_send, d_recv, f_send, f_recv, s_send, s_recv, x_send, x_recv = scratch
        nz, quarter = p.nz, self.quarter

        def place(z, x, c, y):
            columns = pl.ds(pl.multiple_of(y * quarter, 128), quarter)
            return full.at[z, x, c, :, columns]

        fx, fy = p.x + (1 - 2 * p.x) * (1 - p.c), p.y + (1 - 2 * p.y) * p.c
        sx, sy = p.x + (1 - 2 * p.x) * p.c, p.y + (1 - 2 * p.y) * (1 - p.c)

        def own(z):
            return given.at[z] if self.dealt else place(z, p.x, p.c, p.y)

        def first(z):
            target = p.device(x=fx, y=fy)
            return remote(own(z), place(z, p.x, p.c, p.y), f_send.at[z], f_recv.at[z], target)

        def second(z, which):
            x, y = (fx, fy) if which else (p.x, p.y)
            here = place(z, x, p.c, y)
            src = here if which else own(z)
            target = p.device(x=sx, y=sy)
            return remote(src, here, s_send.at[z, which], s_recv.at[z, which], target)

        def across(z, x):
            here = full.at[z, x, p.c]
            return remote(here, here, x_send.at[z, x], x_recv.at[z, x], p.partner())

        def keep(z):
            return pltpu.make_async_copy(given.at[z], place(z, p.x, p.c, p.y), d_send.at[z])

        order = [exclusive_or(p.z, i) for i in range(nz)]
        if self.dealt:
            for z in order:
                first(z).start()
                second(z, 0).start()
                keep(z).start()
            for z in order:
                keep(z).wait()
            yield
        else:
            deal = Deal(
                p, given, lambda z, half: place(z, p.x, half, p.y), quarter, d_send, d_recv
            )
            deal.start(True)
            yield
            deal.arrive(order[0])
            first(order[0]).start()
            second(order[0], 0).start()
            yield
            deal.start(False)
            yield
            for z in order[1:]:
                deal.arrive(z)
                first(z).start()
                second(z, 0).start()
                yield
        for z in order:
            first(z).wait_recv()
            second(z, 1).start()
            yield
        for z in order:
            second(z, 0).wait_recv()
            second(z, 1).wait_recv()
            across(z, 0).start()
            across(z, 1).start()
            yield
        for z in range(nz):
            first(z).wait_send()
            for i in range(2):
                second(z, i).wait_send()
                across(z, i).wait()
        if not self.dealt:
            deal.finish()


class DealBack:
    def __init__(self, p, source, out, quarter, send, recv):
        self.p, self.source, self.out, self.quarter = p, source, out, quarter
        self.send, self.recv = send, recv
        self.per_core = p.nz // 2
        self.owner = p.z // self.per_core

    def out_at(self, z, half):
        start = pl.multiple_of(lax.rem(z, self.per_core) * self.quarter, 128)
        return self.out.at[half, :, pl.ds(start, self.quarter)]

    def away(self, z):
        p = self.p
        return remote(
            self.source(z),
            self.out_at(p.z, p.c),
            self.send.at[z],
            self.recv.at[2 * lax.rem(p.z, self.per_core) + p.c],
            p.device(z=z, c=self.owner),
        )

    def keep(self, z):
        p = self.p
        return pltpu.make_async_copy(
            self.source(z),
            self.out_at(p.z, p.c),
            self.recv.at[2 * lax.rem(p.z, self.per_core) + p.c],
        )

    def start(self, z):
        p = self.p
        here = (z == p.z) & (p.c == self.owner)
        pl.when(jnp.logical_not(here))(self.away(z).start)
        pl.when(here)(self.keep(z).start)

    def finish(self):
        p = self.p
        for piece in range(self.per_core):
            for half in range(2):
                z = p.c * self.per_core + piece
                place = self.out_at(z, half)
                came = remote(
                    place, place, self.send.at[0], self.recv.at[2 * piece + half], p.partner()
                )
                ours = (z == p.z) & (p.c == half)
                pl.when(jnp.logical_not(ours))(came.wait_recv)
        for z in range(p.nz):
            here = (z == p.z) & (p.c == self.owner)
            pl.when(jnp.logical_not(here))(self.away(z).wait_send)
            pl.when(here)(self.keep(z).wait)


class DealBackTask(Task):
    vmem_outs = (0,)

    def __init__(self, nz, sums):
        _, half, quarter = sums.shape
        self.ins = (sums,)
        self.outs = (jax.ShapeDtypeStruct((2, half, nz // 2 * quarter), bf16),)
        self.scratch = (DMA((nz,)), DMA((nz,)))

    def steps(self, p, ins, outs, scratch):
        (sums,), (out,), (send, recv) = ins, outs, scratch
        deal = DealBack(p, lambda z: sums.at[z], out, sums.shape[-1], send, recv)
        for i in (3, 2, 1, 0):
            deal.start(exclusive_or(p.z, i))
        yield
        deal.finish()


class Sums(Task):
    def __init__(self, nz, grad, deal):
        depth, width = grad.shape
        half, quarter = depth // (4 * nz), width // 2
        self.deal = deal
        self.ins = (grad.reshape(nz, 2, 2, half, width),)
        if deal:
            self.outs = (jax.ShapeDtypeStruct((2, half, nz // 2 * quarter), bf16),)
        else:
            self.outs = (jax.ShapeDtypeStruct((nz, half, quarter), bf16),)
            self.vmem_outs = (0,)
        whole = pltpu.VMEM((nz, 2, half, width), bf16)
        self.scratch = (
            whole,
            whole,
            pltpu.VMEM((nz, 2, half, quarter), bf16),
            pltpu.VMEM((nz, half, quarter), bf16),
            DMA((nz, 2)), DMA((nz, 2)), DMA((nz, 2)), DMA((nz, 2)), DMA((nz, 2)),
            DMA((nz,)), DMA((nz,)), DMA((nz,)), DMA((nz,)),
        )

    def steps(self, p, ins, outs, scratch):
        (given,), (out,) = ins, outs
        mine, came, first_in, second_in, *sems = scratch
        local, c_send, c_recv, f_send, f_recv, s_send, s_recv, d_send, d_recv = sems
        nz, quarter = p.nz, given.shape[4] // 2
        order = [exclusive_or(p.z, i) for i in (3, 2, 1, 0)]

        def bring(z, x):
            return pltpu.make_async_copy(given.at[z, x, p.c], mine.at[z, x], local.at[z, x])

        def across(z, x):
            src = given.at[z, x, 1 - p.c]
            return remote(src, came.at[z, x], c_send.at[z, x], c_recv.at[z, x], p.partner())

        def place(z, x, y):
            return mine.at[z, x, :, pl.ds(pl.multiple_of(y * quarter, 128), quarter)]

        fx, fy = p.x + (1 - 2 * p.x) * p.c, p.y + (1 - 2 * p.y) * (1 - p.c)
        sx, sy = p.x + (1 - 2 * p.x) * (1 - p.c), p.y + (1 - 2 * p.y) * p.c

        def first(z, which):
            x, y = (1 - p.x, 1 - p.y) if which else (fx, fy)
            target = p.device(x=fx, y=fy)
            return remote(
                place(z, x, y), first_in.at[z, which], f_send.at[z, which], f_recv.at[z, which], target
            )

        def second(z):
            target = p.device(x=sx, y=sy)
            return remote(place(z, sx, sy), second_in.at[z], s_send.at[z], s_recv.at[z], target)

        back = DealBack(p, lambda z: place(z, p.x, p.y), out, quarter, d_send, d_recv)
        for z in order:
            for x in range(2):
                across(z, x).start()
                bring(z, x).start()
        yield
        for z in order:
            for x in range(2):
                across(z, x).wait_recv()
                bring(z, x).wait()
                add_rows(mine.at[z, x], mine.at[z, x], came.at[z, x])
            for which in (1, 0):
                first(z, which).start()
            yield
        for i in range(nz + 1):
            if i < nz:
                z = order[i]
                for which in (1, 0):
                    at = place(z, sx, sy) if which else place(z, p.x, p.y)
                    first(z, which).wait_recv()
                    add_rows(at, at, first_in.at[z, which])
                    if which:
                        second(z).start()
                yield
            if i >= 1:
                z = order[i - 1]
                second(z).wait_recv()
                at = place(z, p.x, p.y)
                if self.deal:
                    add_rows(at, at, second_in.at[z])
                    back.start(z)
                else:
                    add_rows(out.at[z], at, second_in.at[z])
                yield
        if self.deal:
            back.finish()
        for z in range(nz):
            second(z).wait_send()
            for i in range(2):
                first(z, i).wait_send()
                across(z, i).wait_send()


class SumAll(Task):
    vmem_ins = (0,)
    vmem_outs = (0,)

    def __init__(self, values):
        self.ins = (values,)
        self.outs = (jax.ShapeDtypeStruct(values.shape, f32),)
        stage = pltpu.VMEM((5,) + values.shape, f32)
        self.scratch = (stage, stage, DMA((5,)), DMA((5,)))

    def steps(self, p, ins, outs, scratch):
        (given,), (out,), (stage, came, send, recv) = ins, outs, scratch
        targets = [
            p.partner(),
            p.device(y=1 - p.y),
            p.device(x=1 - p.x),
            p.device(z=exclusive_or(p.z, 1)),
            p.device(z=exclusive_or(p.z, 2)),
        ]
        stage[0] = given[...]
        for i, target in enumerate(targets):
            copy = remote(stage.at[i], came.at[i], send.at[i], recv.at[i], target)
            copy.start()
            yield
            copy.wait()
            total = stage[i] + came[i]
            if i < 4:
                stage[i + 1] = total
            else:
                out[...] = total


def run_tasks(nz, number, tasks, order=""):
    counts = [(len(t.ins), len(t.outs), len(t.scratch)) for t in tasks]

    def split(refs, which):
        found = []
        for count in counts:
            found.append(refs[: count[which]])
            refs = refs[count[which] :]
        return found, refs

    def body(*refs):
        ins, refs = split(refs, 0)
        outs, refs = split(refs, 1)
        scratch, refs = split(refs, 2)
        p = Spot(nz)
        p.greet()
        running = [t.steps(p, *given) for t, *given in zip(tasks, ins, outs, scratch)]
        done = [False] * len(tasks)
        for digit in order:
            i = int(digit)
            if not done[i]:
                done[i] = next(running[i], "end") == "end"
        while not all(done):
            for i, steps in enumerate(running):
                if not done[i]:
                    done[i] = next(steps, "end") == "end"

    sent = sum(x.size * 2 for t in tasks for x in t.ins)
    held = [s for t in tasks for s in t.scratch if getattr(s, "memory_space", None) == pltpu.VMEM]
    held += [t.ins[i] for t in tasks for i in t.vmem_ins] + [t.outs[i] for t in tasks for i in t.vmem_outs]
    vmem = sum(math.prod(s.shape) * jnp.dtype(s.dtype).itemsize for s in held)
    results = pl.pallas_call(
        body,
        out_shape=[o for t in tasks for o in t.outs],
        in_specs=[in_vmem if i in t.vmem_ins else anywhere for t in tasks for i in range(len(t.ins))],
        out_specs=[
            in_vmem if i in t.vmem_outs else anywhere for t in tasks for i in range(len(t.outs))
        ],
        scratch_shapes=[s for t in tasks for s in t.scratch],
        compiler_params=pltpu.CompilerParams(
            collective_id=number, has_side_effects=True, vmem_limit_bytes=vmem + 4 * 2**20
        ),
        cost_estimate=pl.CostEstimate(
            flops=0, bytes_accessed=sent, transcendentals=0, remote_bytes_transferred=sent
        ),
    )(*[x for t in tasks for x in t.ins])
    found, _ = split(list(results), 1)
    return [f[0] for f in found]


START_ORDER = "10231223" + "13222" + "12222" + "3331" + "2222" + "33333333"


class Kernels:
    def __init__(self, at):
        self.at = at
        self.blocks, self.nz = at.blocks, at.nz
        self.block = 2 * at.z + at.c
        self.number = 0

    def run(self, tasks, order=""):
        self.number += 1
        return run_tasks(self.nz, self.number, tasks, order)

    def flat(self, whole):
        return whole.reshape(-1, whole.shape[-1])

    def start(self, own, attn_shard, gate, up):
        nz = self.nz
        tasks = [
            PlaneGather(own),
            PairGather(nz, attn_shard, True),
            Copies(nz, gate, False),
            Copies(nz, up, False),
        ]
        found = self.run(tasks, START_ORDER)
        return [self.flat(w) for w in found]

    def scatter_heads_deal(self, partial, down):
        return self.run([PlaneScatter(partial), DealTask(self.nz, down)], "10")

    def gather_kv(self, own):
        (whole,) = self.run([PairGather(self.nz, own, False)])
        return whole.reshape((self.blocks,) + own.shape)

    def gather_z_copy(self, own, pieces):
        return [
            self.flat(w) for w in self.run([ZGather(self.nz, own), Copies(self.nz, pieces, True)], "01001111011110")
        ]

    def gather_z(self, own):
        return self.flat(self.run([ZGather(self.nz, own)])[0])

    def scatter_z(self, partial):
        return self.run([ZScatter(self.nz, partial)])[0]

    def scatter_z_sums(self, partial, grad):
        return self.run([ZScatter(self.nz, partial), Sums(self.nz, grad, False)], "1011110" + "11110" + "11110")

    def gather_heads_back(self, own, sums):
        rows, shard = self.run([PlaneGather(own), DealBackTask(self.nz, sums)], "01")
        return self.flat(rows), self.flat(shard)

    def scatter_kv_sums(self, parts, grad):
        given = parts.reshape((self.nz, 2) + parts.shape[1:])
        kv, sums = self.run([PairScatter(self.nz, given, False), Sums(self.nz, grad, False)], "10" + "11" + "0" + "110" + "11110" + "11110")
        return kv.astype(f32), sums

    def scatter_heads_back(self, partial, sums):
        rows, shard = self.run([PlaneScatter(partial), DealBackTask(self.nz, sums)], "01")
        return rows, self.flat(shard)

    def finish(self, attn_grad, grad, gains):
        rows = attn_grad.shape[0] // self.blocks
        given = attn_grad.reshape(self.nz, 2, rows, attn_grad.shape[1])
        attn, shard, total = self.run(
            [
                PairScatter(self.nz, given, True),
                Sums(self.nz, grad, True),
                SumAll(gains.reshape(8, -1)),
            ],
            "01012" + "1121" + "0" + "1121" + "0" + "1121" + "0" + "1121",
        )
        return attn, self.flat(shard), total.reshape(gains.shape)


def causal_mask(rows):
    shape = (rows, rows)
    return lax.broadcasted_iota(jnp.int32, shape, 1) <= lax.broadcasted_iota(jnp.int32, shape, 0)


def forward_kernel(kinds, q_ref, kv_ref, out_ref, exact_ref, inv_ref, acc, total):
    step, last = pl.program_id(0), pl.num_programs(0) - 1
    heads, rows, dim = q_ref.shape
    kind = kinds[step]

    @pl.when(step == 0)
    def _():
        acc[...] = jnp.zeros_like(acc)
        total[...] = jnp.zeros_like(total)

    def work(own):
        for head in range(heads):
            raw = contract(q_ref[head], kv_ref[0, :, :dim], 1, 1)
            weights = jnp.exp(softcap * jnp.tanh(raw * (score_scale / softcap)))
            if own:
                weights = jnp.where(causal_mask(rows), weights, 0.0)
            total[head] += jnp.sum(weights, axis=-1, keepdims=True)
            acc[head] += contract(weights.astype(bf16), kv_ref[0, :, dim:], 1, 0)

    @pl.when(kind == 1)
    def _():
        work(False)

    @pl.when(kind == 2)
    def _():
        work(True)

    @pl.when(step == last)
    def _():
        for head in range(heads):
            inverse = 1.0 / total[head]
            value = acc[head] * inverse
            inv_ref[head] = inverse
            exact_ref[:, head * dim : (head + 1) * dim] = value
            out_ref[:, head * dim : (head + 1) * dim] = value.astype(bf16)


def whole2(step, kinds):
    return (0, 0)


def whole3(step, kinds):
    return (0, 0, 0)


def by_step(step, kinds):
    return (step, 0, 0)


def attend(kinds, queries, all_kv):
    heads, rows, dim = queries.shape
    return pl.pallas_call(
        forward_kernel,
        grid_spec=pltpu.PrefetchScalarGridSpec(
            num_scalar_prefetch=1,
            grid=(all_kv.shape[0],),
            in_specs=[
                pl.BlockSpec((heads, rows, dim), whole3),
                pl.BlockSpec((1, rows, 2 * dim), by_step),
            ],
            out_specs=[
                pl.BlockSpec((rows, heads * dim), whole2),
                pl.BlockSpec((rows, heads * dim), whole2),
                pl.BlockSpec((heads, rows, 1), whole3),
            ],
            scratch_shapes=[
                pltpu.VMEM((heads, rows, dim), f32),
                pltpu.VMEM((heads, rows, 1), f32),
            ],
        ),
        out_shape=[
            jax.ShapeDtypeStruct((rows, heads * dim), bf16),
            jax.ShapeDtypeStruct((rows, heads * dim), f32),
            jax.ShapeDtypeStruct((heads, rows, 1), f32),
        ],
        compiler_params=pltpu.CompilerParams(vmem_limit_bytes=40 * 2**20),
        cost_estimate=pl.CostEstimate(
            flops=3 * 4 * heads * rows * rows * dim,
            bytes_accessed=8 * rows * dim * heads,
            transcendentals=6 * heads * rows * rows,
        ),
    )(kinds, queries, all_kv)


def backward_kernel(kinds, q_ref, kv_ref, up_ref, exact_ref, inv_ref, dq_ref, dkv_ref):
    step = pl.program_id(0)
    heads, rows, dim = q_ref.shape
    kind = kinds[step]

    @pl.when(step == 0)
    def _():
        dq_ref[...] = jnp.zeros_like(dq_ref)

    def work(own):
        dk = jnp.zeros((rows, dim), f32)
        dv = jnp.zeros((rows, dim), f32)
        for head in range(heads):
            columns = slice(head * dim, (head + 1) * dim)
            up = up_ref[:, columns]
            delta = jnp.sum(up.astype(f32) * exact_ref[:, columns], axis=-1, keepdims=True)
            raw = contract(q_ref[head], kv_ref[0, :, :dim], 1, 1)
            bounded = jnp.tanh(raw * (score_scale / softcap))
            probs = jnp.exp(softcap * bounded) * inv_ref[head]
            if own:
                probs = jnp.where(causal_mask(rows), probs, 0.0)
            d_probs = contract(up, kv_ref[0, :, dim:], 1, 1)
            d_raw = probs * (d_probs - delta) * ((1.0 - bounded * bounded) * score_scale)
            d_raw = d_raw.astype(bf16)
            dq_ref[head] += contract(d_raw, kv_ref[0, :, :dim], 1, 0)
            dk += contract(d_raw, q_ref[head], 0, 0)
            dv += contract(probs.astype(bf16), up, 0, 0)
        dkv_ref[0, :, :dim] = dk.astype(bf16)
        dkv_ref[0, :, dim:] = dv.astype(bf16)

    @pl.when(kind == 1)
    def _():
        work(False)

    @pl.when(kind == 0)
    def _():
        dkv_ref[...] = jnp.zeros_like(dkv_ref)

    @pl.when(kind == 2)
    def _():
        work(True)


def attend_back(kinds, queries, all_kv, upstream, exact, inverse):
    heads, rows, dim = queries.shape
    blocks = all_kv.shape[0]
    return pl.pallas_call(
        backward_kernel,
        grid_spec=pltpu.PrefetchScalarGridSpec(
            num_scalar_prefetch=1,
            grid=(blocks,),
            in_specs=[
                pl.BlockSpec((heads, rows, dim), whole3),
                pl.BlockSpec((1, rows, 2 * dim), by_step),
                pl.BlockSpec((rows, heads * dim), whole2),
                pl.BlockSpec((rows, heads * dim), whole2),
                pl.BlockSpec((heads, rows, 1), whole3),
            ],
            out_specs=[
                pl.BlockSpec((heads, rows, dim), whole3),
                pl.BlockSpec((1, rows, 2 * dim), by_step),
            ],
        ),
        out_shape=[
            jax.ShapeDtypeStruct((heads, rows, dim), f32),
            jax.ShapeDtypeStruct((blocks, rows, 2 * dim), bf16),
        ],
        compiler_params=pltpu.CompilerParams(vmem_limit_bytes=40 * 2**20),
        cost_estimate=pl.CostEstimate(
            flops=3 * 10 * heads * rows * rows * dim,
            bytes_accessed=16 * rows * dim * heads,
            transcendentals=6 * heads * rows * rows,
        ),
    )(kinds, queries, all_kv, upstream, exact, inverse)


def on_device(
    tokens,
    cotangent,
    norm_attn_in,
    w_query,
    w_key,
    w_value,
    w_out,
    norm_attn_out,
    norm_ff_in,
    w_gate,
    w_up,
    w_down,
    norm_ff_out,
    block_group,
    block_role,
):
    at = Place()
    own_rows, depth = tokens.shape
    shard_rows, units = w_gate.shape
    regular = at.nz == 4 and shard_rows % 32 == 0 and (2 * units // at.nz) % 128 == 0
    comm = Kernels(at) if regular else Permutes(at)
    blocks = at.blocks
    block_len = own_rows * lax.axis_size("heads")
    prompt_len = blocks // 4
    block_ids = jnp.arange(blocks, dtype=jnp.int32)
    my_group = jnp.sum(jnp.where(block_ids == comm.block, block_group, 0))
    my_role = jnp.sum(jnp.where(block_ids == comm.block, block_role, 0))
    positions = jnp.where(
        my_role < prompt_len, my_role * block_len, prompt_len * block_len
    ) + jnp.arange(block_len, dtype=jnp.int32)
    cosine, sine_table = rope_tables(positions)
    prompt = (block_group == my_group) & (block_role < prompt_len) & (block_role < my_role)
    kinds = jnp.where(block_ids == comm.block, 2, prompt.astype(jnp.int32)).astype(jnp.int32)

    token_f32 = tokens.astype(f32)
    heads_width = w_query.shape[1]
    qkv_width = heads_width + 2 * HEAD_DIM
    attn_shard = jnp.concatenate([w_query, w_key, w_value, w_out.T], axis=1)
    normed_one, attn_full, gate_full, up_full = comm.start(
        normalize(token_f32, norm_attn_in).astype(bf16), attn_shard, w_gate, w_up
    )
    qkv_full, out_full = attn_full[:, :qkv_width], attn_full[:, qkv_width:]
    qkv_lin = jnp.dot(normed_one, qkv_full, preferred_element_type=f32)
    queries = jnp.stack(
        [
            rotate(qkv_lin[:, :HEAD_DIM], cosine, sine_table),
            rotate(qkv_lin[:, HEAD_DIM:heads_width], cosine, sine_table),
        ]
    ).astype(bf16)
    own_kv = jnp.concatenate(
        [
            rotate(qkv_lin[:, heads_width : heads_width + HEAD_DIM], cosine, sine_table),
            qkv_lin[:, heads_width + HEAD_DIM :],
        ],
        axis=1,
    ).astype(bf16)
    all_kv = comm.gather_kv(own_kv)
    attn_rows, attended, inverse = attend(kinds, queries, all_kv)
    attn_proj, down_pieces = comm.scatter_heads_deal(
        contract(attn_rows, out_full, 1, 1).astype(bf16), w_down.T
    )
    middle = token_f32 + normalize(attn_proj, norm_attn_out)

    normed_two, down_full = comm.gather_z_copy(
        normalize(middle, norm_ff_in).astype(bf16), down_pieces
    )
    gate_lin = jnp.dot(normed_two, gate_full, preferred_element_type=f32)
    up_lin = jnp.dot(normed_two, up_full, preferred_element_type=f32)
    hidden = (jax.nn.gelu(gate_lin, approximate=True) * up_lin).astype(bf16)
    ff_proj = comm.scatter_z(contract(hidden, down_full, 1, 1).astype(bf16))
    layer_out = middle + normalize(ff_proj, norm_ff_out)

    upstream = cotangent.astype(f32)
    d_ff, grad_ff_out = normalize_back(ff_proj, norm_ff_out, upstream)
    d_ff_rows = comm.gather_z(d_ff.astype(bf16))
    d_hidden = contract(d_ff_rows, down_full, 1, 0)
    _, glu_back = jax.vjp(
        lambda gate_in, up_in: jax.nn.gelu(gate_in, approximate=True) * up_in, gate_lin, up_lin
    )
    d_gate, d_up = glu_back(d_hidden)
    d_gate = d_gate.astype(bf16)
    d_up = d_up.astype(bf16)
    d_partial = contract(d_gate, gate_full, 1, 1) + contract(d_up, up_full, 1, 1)
    d_normed_two, down_sums = comm.scatter_z_sums(
        d_partial.astype(bf16), contract(d_ff_rows, hidden, 0, 0).astype(bf16)
    )

    d_middle_part, grad_ff_in = normalize_back(middle, norm_ff_in, d_normed_two)
    d_middle = upstream + d_middle_part
    d_proj, grad_attn_out = normalize_back(attn_proj, norm_attn_out, d_middle)
    d_proj_rows, grad_down = comm.gather_heads_back(d_proj.astype(bf16), down_sums)
    d_attended = contract(d_proj_rows, out_full, 1, 0).astype(bf16)
    d_query, d_kv_parts = attend_back(kinds, queries, all_kv, d_attended, attended, inverse)
    d_kv, gate_sums = comm.scatter_kv_sums(
        d_kv_parts, contract(normed_two, d_gate, 0, 0).astype(bf16)
    )
    d_qkv_lin = jnp.concatenate(
        [
            rotate(d_query[0], cosine, -sine_table),
            rotate(d_query[1], cosine, -sine_table),
            rotate(d_kv[:, :HEAD_DIM], cosine, -sine_table),
            d_kv[:, HEAD_DIM:],
        ],
        axis=1,
    ).astype(bf16)
    d_normed_one, grad_gate = comm.scatter_heads_back(
        contract(d_qkv_lin, qkv_full, 1, 1).astype(bf16), gate_sums
    )
    d_token_part, grad_attn_in = normalize_back(token_f32, norm_attn_in, d_normed_one)
    input_grad = (d_middle + d_token_part).astype(bf16)
    grad_attn, grad_up, gains = comm.finish(
        jnp.concatenate(
            [contract(normed_one, d_qkv_lin, 0, 0), contract(d_proj_rows, attn_rows, 0, 0)], axis=1
        ).astype(bf16),
        contract(normed_two, d_up, 0, 0).astype(bf16),
        jnp.stack([grad_attn_in, grad_attn_out, grad_ff_in, grad_ff_out]),
    )
    grad_attn, grad_gate, grad_up = [g.astype(f32) for g in (grad_attn, grad_gate, grad_up)]
    return (
        layer_out.astype(bf16),
        input_grad,
        gains[0],
        grad_attn[:, :heads_width],
        grad_attn[:, heads_width : heads_width + HEAD_DIM],
        grad_attn[:, heads_width + HEAD_DIM : qkv_width],
        grad_attn[:, qkv_width:].T,
        gains[1],
        gains[2],
        grad_gate,
        grad_up,
        grad_down.astype(f32).T,
        gains[3],
    )


def solution(mesh):
    rows, weight, turned = P(("blk", "heads"), None), P("blk", "heads"), P("heads", "blk")
    return jax.shard_map(
        on_device,
        mesh=mesh,
        in_specs=(
            rows, rows, P(), weight, weight, weight, turned, P(), P(), weight, weight, turned,
            P(), P(), P(),
        ),
        out_specs=(
            rows, rows, P(), weight, weight, weight, turned, P(), P(), weight, weight, turned, P(),
        ),
        check_vma=False,
    )
```

time: 1030 us -> 853 us (0.83)
  Pallas kernels: 830 us -> 672 us
  matrix products: 120 us -> 106 us
    pallas_call x14 -> x11, Pallas kernels: 823 us -> 661 us  [run_tasks(): pl.pallas_call(body, out_shape=[o for t in tasks for o in t.outs], in_spe...]
    unnamed x88 -> x84, local copies, waits for them, and re-layouts: 3.09 us -> 13.5 us
  transfers between devices with their start and end apart: 5 -> 0, of which waited for: 3 -> 0; matrix products, arithmetic and copies ran while one was open for 6% -> 0% of each run, Pallas kernels for 26% -> 0%
where the time goes in v2:
time: 853 us; the launch traced here: 843 us
  Pallas kernels  672 us (79%)
  matrix products  106 us (12%)
  other arithmetic  38.8 us (5%)
  local copies, waits for them, and re-layouts  23.7 us (3%)
    pallas_call x11, Pallas kernels, run_tasks(): pl.pallas_call(body, out_shape=[o for t in tasks for o in t.outs], in_spe...  661 us
    dot_general x12, matrix products, contract(): lax.dot_general(left_side, right_side, (((left_dim,), (right_dim,)), ((),...  87.3 us

profile of v2, /device:TPU:2, one launch (start us, length us, event | category | flops | bytes accessed | tf_op | source)
XLA Modules:
  0.0 843.3 jit_solution(7479209616444455944)
XLA Ops:
  0.7 1.3 fusion.33
  2.0 1.3 select_reduce_fusion
  4.6 2.1 fusion.92.kinds
  6.7 0.7 broadcast_add_fusion.3
  7.4 0.7 broadcast_add_fusion
  8.2 0.7 broadcast_add_fusion.1
  8.9 1.3 fusion.26.refs_0_
  10.2 1.3 pad_maximum_fusion.1.refs_1_
  11.4 142.4 %shard_map.246 = (bf16[4,128,2304]{2,1,0:T(8,128)(2,1)S(1)}, bf16[4,2,288,1536]{3,2,1,0:T(8,128)(2,1)S(1)}, bf16[4,2,2,144,2304]{4,3,2,1,0:T(8,128)(2,1)}, bf16[4,2,2,144,2304]{4,3,2,1,0:T(8,128)(2,1)}) custom-call(bf16[128,2304]{1,0:T(8,128)(2,1)S(1)} %fusion.26.refs_0_, bf16[288,1536]{1,0:T(8,128)(2,1)S(1)} %pad_maximum_fusion.1.refs_1_, ...), custom_call_target="tpu_custom_call" | custom-call | bytes 4128768 | tf_op jit(solution)/shard_map/pallas_call | solution.py:1128
  153.9 2.6 fusion.9
  156.8 1.3 fusion.83
  158.3 2.4 copy.28
  160.8 53.6 %shard_map.247 = bf16[4,2,512,512]{3,2,1,0:T(8,128)(2,1)S(1)} custom-call(bf16[512,512]{1,0:T(8,128)(2,1)S(1)} %pad_maximum_fusion.3.refs_0_), custom_call_target="tpu_custom_call" | custom-call | bytes 524288 | tf_op jit(solution)/shard_map/pallas_call | solution.py:1128
  214.4 3.7 shard_map.248
  218.1 3.7 convolution_convert_fusion.5
  221.9 29.5 %shard_map.249 = (f32[128,2304]{1,0:T(8,128)S(1)}, bf16[4,144,1152]{2,1,0:T(8,128)(2,1)S(1)}) custom-call(bf16[4,128,2304]{2,1,0:T(8,128)(2,1)S(1)} %bitcast.92, bf16[2,144,2304]{2,1,0:T(8,128)(2,1)S(1)} %bitcast.100), custom_call_target="tpu_custom_call" | custom-call | bytes 3686400 | tf_op jit(solution)/shard_map/pallas_call | solution.py:1128
  252.2 55.8 %shard_map.250 = (bf16[4,128,2304]{2,1,0:T(8,128)(2,1)S(1)}, bf16[4,2,2,144,2304]{4,3,2,1,0:T(8,128)(2,1)S(1)}) custom-call(bf16[128,2304]{1,0:T(8,128)(2,1)S(1)} %multiply_convert_fusion.3.refs_0_, bf16[4,144,1152]{2,1,0:T(8,128)(2,1)S(1)} %get-tuple-element.41.refs_1_), custom_call_target="tpu_custom_call" | custom-call | bytes 1916928 | tf_op jit(solution)/shard_map/pallas_call | solution.py:1128
  307.9 4.0 copy-done.9
  311.9 8.9 %fusion.95 = f32[512,2304]{1,0:T(8,128)S(1)} fusion(bf16[512,2304]{1,0:T(8,128)(2,1)S(1)} %bitcast.111, bf16[2304,2304]{1,0:T(8,128)(2,1)} %bitcast.122), kind=kOutput, calls=%fused_computation.158 | convolution fusion | flops 5435817984 | bytes 17694720 | tf_op jit(solution)/shard_map/dot_general | solution.py:1455
  321.0 7.5 multiply_convert_fusion.1
  328.4 10.8 %convolution_convert_fusion.4 = bf16[512,2304]{1,0:T(8,128)(2,1)S(1)} fusion(bf16[512,2304]{1,0:T(8,128)(2,1)S(1)} %get-tuple-element.90, bf16[2304,2304]{1,0:T(8,128)(2,1)} %bitcast.103), kind=kOutput, calls=%fused_computation.17 | convolution fusion | flops 5436997632 | bytes 15335424 | tf_op jit(solution)/shard_map/dot_general | solution.py:21
  339.2 44.7 %shard_map.251 = f32[128,2304]{1,0:T(8,128)S(1)} custom-call(bf16[4,128,2304]{2,1,0:T(8,128)(2,1)S(1)} %bitcast.99), custom_call_target="tpu_custom_call" | custom-call | bytes 2359296 | tf_op jit(solution)/shard_map/pallas_call | solution.py:1128
  384.6 1.2 fusion.25
  385.8 45.0 %shard_map.252 = bf16[4,128,2304]{2,1,0:T(8,128)(2,1)S(1)} custom-call(bf16[128,2304]{1,0:T(8,128)(2,1)S(1)} %get-tuple-element.80.refs_0_), custom_call_target="tpu_custom_call" | custom-call | bytes 589824 | tf_op jit(solution)/shard_map/pallas_call | solution.py:1128
  430.8 12.5 %multiply_convert_fusion = (bf16[512,2304]{1,0:T(8,128)(2,1)}, bf16[512,2304]{1,0:T(8,128)(2,1)S(1)}) fusion(f32[512,2304]{1,0:T(8,128)S(1)} %copy-done.31, f32[512,2304]{1,0:T(8,128)S(1)} %copy-done.32, bf16[512,2304]{1,0:T(8,128)(2,1)S(1)} %bitcast.97, bf16[2304,2304]{1,0:T(8,128)(2,1)} %bitcast.104), kind=kOutput, calls=%fused_computation.14 | convolution fusion | flops 5464129536 | bytes 27131904 | tf_op jit(solution)/shard_map/dot_general | solution.py:21
  443.4 12.3 %fusion.96 = f32[512,2304]{1,0:T(8,128)} fusion(bf16[512,2304]{1,0:T(8,128)(2,1)S(1)} %get-tuple-element.73, bf16[2304,2304]{1,0:T(8,128)(2,1)} %bitcast.123), kind=kOutput, calls=%fused_computation.159 | convolution fusion | flops 5435817984 | bytes 17694720 | tf_op jit(solution)/shard_map/dot_general | solution.py:21
  455.6 11.0 %fusion.7 = bf16[512,2304]{1,0:T(8,128)(2,1)S(1)} fusion(f32[512,2304]{1,0:T(8,128)} %fusion.96, bf16[512,2304]{1,0:T(8,128)(2,1)} %get-tuple-element.72, bf16[2304,2304]{1,0:T(8,128)(2,1)} %bitcast.118), kind=kOutput, calls=%fused_computation.19 | convolution fusion | flops 5438177280 | bytes 20054016 | tf_op jit(solution)/shard_map/dot_general | solution.py:21
  466.7 7.6 convolution_convert_fusion.2
  474.3 52.0 %shard_map.253 = (f32[128,2304]{1,0:T(8,128)S(1)}, bf16[4,144,1152]{2,1,0:T(8,128)(2,1)S(1)}) custom-call(bf16[4,128,2304]{2,1,0:T(8,128)(2,1)S(1)} %bitcast.90, bf16[4,2,2,144,2304]{4,3,2,1,0:T(8,128)(2,1)S(1)} %bitcast.85), custom_call_target="tpu_custom_call" | custom-call | bytes 12976128 | tf_op jit(solution)/shard_map/pallas_call | solution.py:1128
  526.7 1.6 multiply_reduce_fusion.1
  528.4 1.6 multiply_convert_fusion.2.refs_0_
  529.9 30.5 %shard_map.254 = (bf16[4,128,2304]{2,1,0:T(8,128)(2,1)S(1)}, bf16[2,144,2304]{2,1,0:T(8,128)(2,1)S(1)}) custom-call(bf16[128,2304]{1,0:T(8,128)(2,1)S(1)} %multiply_convert_fusion.2.refs_0_, bf16[4,144,1152]{2,1,0:T(8,128)(2,1)S(1)} %get-tuple-element.47.refs_1_), custom_call_target="tpu_custom_call" | custom-call | bytes 1916928 | tf_op jit(solution)/shard_map/pallas_call | solution.py:1128
  560.5 3.2 fusion.20.up_ref
  563.7 6.9 shard_map.255
  570.7 1.2 fusion.91
  571.9 1.2 fusion.90
  573.1 1.2 fusion.89
  574.2 1.2 fusion.88
  575.5 1.0 copy-done.24
  576.4 1.8 convert_bitcast_fusion
  578.2 2.5 copy.29
  580.7 4.6 convolution_convert_fusion.7
  585.3 8.4 convolution_convert_fusion
  593.7 6.1 convolution_convert_fusion.1
  599.9 56.8 %shard_map.256 = (bf16[512,512]{1,0:T(8,128)(2,1)S(1)}, bf16[4,144,1152]{2,1,0:T(8,128)(2,1)S(1)}) custom-call(bf16[4,2,512,512]{3,2,1,0:T(8,128)(2,1)S(1)} %bitcast.87, bf16[4,2,2,144,2304]{4,3,2,1,0:T(8,128)(2,1)S(1)} %bitcast.86), custom_call_target="tpu_custom_call" | custom-call | bytes 14811136 | tf_op jit(solution)/shard_map/pallas_call | solution.py:1128
  656.8 1.2 fusion.87
  658.0 1.2 fusion.86
  659.3 2.9 convolution_convert_fusion.3
  662.2 29.4 %shard_map.257 = (f32[128,2304]{1,0:T(8,128)S(1)}, bf16[2,144,2304]{2,1,0:T(8,128)(2,1)S(1)}) custom-call(bf16[4,128,2304]{2,1,0:T(8,128)(2,1)S(1)} %bitcast.91, bf16[4,144,1152]{2,1,0:T(8,128)(2,1)S(1)} %get-tuple-element.54.refs_1_), custom_call_target="tpu_custom_call" | custom-call | bytes 3686400 | tf_op jit(solution)/shard_map/pallas_call | solution.py:1128
  692.2 2.6 fusion.31
  694.9 4.2 convolution_convert_fusion.6
  699.1 5.9 pad_maximum_fusion.refs_0_
  705.0 3.0 copy-done
  708.0 4.0 copy-done.1
  712.0 121.2 %shard_map.258 = (bf16[288,1536]{1,0:T(8,128)(2,1)S(1)}, bf16[2,144,2304]{2,1,0:T(8,128)(2,1)S(1)}, f32[8,1152]{1,0:T(8,128)S(1)}) custom-call(bf16[4,2,288,1536]{3,2,1,0:T(8,128)(2,1)S(1)} %copy-done, bf16[4,2,2,144,2304]{4,3,2,1,0:T(8,128)(2,1)S(1)} %bitcast.84, f32[8,1152]{1,0:T(8,128)S(1)} %reshape.194.refs_2_), custom_call_target="tpu_custom_call" | custom-call | bytes 17713152 | tf_op jit(solution)/shard_map/pallas_call | solution.py:1128
  833.3 1.1 copy-done.7
  834.4 0.6 squeeze.23
  835.0 0.6 squeeze.22
  835.6 0.6 squeeze.21
  836.8 0.9 slice.137
  837.7 0.8 fusion.93
  838.7 0.9 slice_bitcast_fusion
  839.6 1.8 bitcast_convert_fusion.1
  841.4 1.8 bitcast_convert_fusion
  (115 shorter events, 4.0 us)
Async XLA Ops:
  2.0 151.9 %copy-start.28 = (f32[128]{0:T(128)}, f32[128]{0:T(128)S(1)}, u32[]{:S(2)}) copy-start(f32[128]{0:T(128)S(1)} %add_rsqrt_fusion.3) | copy-start | bytes 1540
  4.6 6.8 copy-start.5
  4.6 6.8 copy-start.6
  7.4 1.4 copy-start.22
  153.9 2.9 copy-start.10
  218.1 3.7 copy-start.13
  218.1 3.7 copy-start.15
  218.1 3.7 copy-start.4
  221.8 29.7 %copy-start.17 = (bf16[128,2304]{1,0:T(8,128)(2,1)S(1)}, bf16[128,2304]{1,0:T(8,128)(2,1)}, u32[]{:S(2)}) copy-start(bf16[128,2304]{1,0:T(8,128)(2,1)} %param.15) | copy-start | bytes 1769476
  252.1 68.8 %slice-start.2 = ((s8[10616832]{0:T(1024)(128)(4,1)}), s8[4194304]{0:T(1024)(128)(4,1)S(1)}, s32[]{:S(2)}) async-start(s8[10616832]{0:T(1024)(128)(4,1)} %bitcast.119), calls=%async_computation.2 | async-start | bytes 8388608
  307.9 4.0 copy-start.9
  311.9 9.0 %copy-start.11 = (bf16[4,128,2304]{2,1,0:T(8,128)(2,1)}, bf16[4,128,2304]{2,1,0:T(8,128)(2,1)S(1)}, u32[]{:S(2)}) copy-start(bf16[4,128,2304]{2,1,0:T(8,128)(2,1)S(1)} %get-tuple-element.42) | copy-start | bytes 7077892
  311.9 9.0 %slice-start.3 = ((s8[10616832]{0:T(1024)(128)(4,1)}), s8[4194304]{0:T(1024)(128)(4,1)S(1)}, s32[]{:S(2)}) async-start(s8[10616832]{0:T(1024)(128)(4,1)} %bitcast.119), calls=%async_computation.3 | async-start | bytes 8388608
  311.9 9.0 %slice-start.4 = ((s8[10616832]{0:T(1024)(128)(4,1)}), s8[2228224]{0:T(1024)(128)(4,1)S(1)}, s32[]{:S(2)}) async-start(s8[10616832]{0:T(1024)(128)(4,1)} %bitcast.119), calls=%async_computation.4 | async-start | bytes 4456448
  320.9 7.5 copy-start.30
  328.4 10.8 %copy-start.36 = (bf16[512,2304]{1,0:T(8,128)(2,1)}, bf16[512,2304]{1,0:T(8,128)(2,1)S(1)}, u32[]{:S(2)}) copy-start(bf16[512,2304]{1,0:T(8,128)(2,1)S(1)} %get-tuple-element.90) | copy-start | bytes 7077892
  339.2 44.9 %copy-start.19 = (bf16[128,2304]{1,0:T(8,128)(2,1)S(1)}, bf16[128,2304]{1,0:T(8,128)(2,1)}, u32[]{:S(2)}) copy-start(bf16[128,2304]{1,0:T(8,128)(2,1)} %param.16) | copy-start | bytes 1769476
  383.9 46.9 %copy-start.32 = (f32[512,2304]{1,0:T(8,128)S(1)}, f32[512,2304]{1,0:T(8,128)}, u32[]{:S(2)}) copy-start(f32[512,2304]{1,0:T(8,128)} %get-tuple-element.91) | copy-start | bytes 14155780
  384.6 46.3 %copy-start.31 = (f32[512,2304]{1,0:T(8,128)S(1)}, f32[512,2304]{1,0:T(8,128)}, u32[]{:S(2)}) copy-start(f32[512,2304]{1,0:T(8,128)} %copy-done.30) | copy-start | bytes 14155780
  443.4 12.3 %copy-start.33 = (bf16[512,2304]{1,0:T(8,128)(2,1)}, bf16[512,2304]{1,0:T(8,128)(2,1)S(1)}, u32[]{:S(2)}) copy-start(bf16[512,2304]{1,0:T(8,128)(2,1)S(1)} %get-tuple-element.73) | copy-start | bytes 7077892
  560.5 3.2 copy-start.14
  560.5 3.2 copy-start.16
  570.6 4.8 copy-start.2
  575.4 1.0 copy-start.24
  580.7 4.6 copy-start.12
  580.7 4.6 copy-start.35
  585.3 8.4 copy-start.34
  593.7 6.2 copy-start.3
  599.8 59.4 %slice-start = ((s8[7077888]{0:T(1024)(128)(4,1)}), s8[4194304]{0:T(1024)(128)(4,1)S(1)}, s32[]{:S(2)}) async-start(s8[7077888]{0:T(1024)(128)(4,1)} %bitcast.108), calls=%async_computation | async-start | bytes 8388608
  599.8 57.0 %copy-start.25 = (bf16[512,1024]{1,0:T(8,128)(2,1)S(1)}, bf16[512,1024]{1,0:T(8,128)(2,1)}, u32[]{:S(2)}) copy-start(bf16[512,1024]{1,0:T(8,128)(2,1)} %copy-done.24) | copy-start | bytes 3145732
  599.9 59.4 %slice-start.1 = ((s8[7077888]{0:T(1024)(128)(4,1)}), s8[2883584]{0:T(1024)(128)(4,1)S(1)}, s32[]{:S(2)}) async-start(s8[7077888]{0:T(1024)(128)(4,1)} %bitcast.108), calls=%async_computation.1 | async-start | bytes 5767168
  659.3 2.9 copy-start.26
  662.2 29.5 %copy-start.18 = (bf16[128,2304]{1,0:T(8,128)(2,1)S(1)}, bf16[128,2304]{1,0:T(8,128)(2,1)}, u32[]{:S(2)}) copy-start(bf16[128,2304]{1,0:T(8,128)(2,1)} %param.15) | copy-start | bytes 1769476
  662.2 29.5 %copy-start.23 = (f32[2304]{0:T(1024)S(1)}, f32[2304]{0:T(1024)}, u32[]{:S(2)}) copy-start(f32[2304]{0:T(1024)} %copy-done.22) | copy-start | bytes 27652
  662.2 29.5 %copy-start.29 = (f32[128]{0:T(128)S(1)}, f32[128]{0:T(128)}, u32[]{:S(2)}) copy-start(f32[128]{0:T(128)} %copy-done.28) | copy-start | bytes 1540
  692.2 2.7 copy-start.21
  692.2 2.7 copy-start.27
  694.9 4.2 copy-start.20
  705.0 3.0 copy-start
  708.0 4.0 copy-start.1
  833.3 1.1 copy-start.7
  838.7 2.6 copy-start.8

commit v3 on v2

--- a/solution.py
+++ b/solution.py
@@ -253,19 +253,17 @@
     def split(self, whole):
         return turn(self.at, whole.reshape((self.nz, whole.shape[0] // self.nz) + whole.shape[1:]))
 
-    def start(self, own, attn_shard, gate, up):
+    def start(self, own, attn_shard, gate, up, down):
         at = self.at
         attn_full = gather_zx(at, attn_shard).reshape(own.shape[1], -1)
-        return rows_to_block(at, own), attn_full, spread_weight(at, gate), spread_weight(at, up)
-
-    def scatter_heads_deal(self, partial, down):
-        return rows_from_block(self.at, partial), spread_weight(self.at, down)
-
-    def gather_kv(self, own):
-        return gather_zx(self.at, own).reshape((self.blocks,) + own.shape)
-
-    def gather_z_copy(self, own, pieces):
-        return self.gather_z(own), pieces
+        weights = [spread_weight(at, w) for w in (gate, up, down)]
+        return [rows_to_block(at, own), attn_full] + weights
+
+    def gather_kv(self, own, down):
+        return gather_zx(self.at, own).reshape((self.blocks,) + own.shape), down
+
+    def scatter_heads(self, partial):
+        return rows_from_block(self.at, partial)
 
     def gather_z(self, own):
         whole = unturn(self.at, gather_z(self.at, own))
@@ -274,22 +272,44 @@
     def scatter_z(self, partial):
         return scatter_z(self.at, self.split(partial))
 
-    def scatter_z_sums(self, partial, grad):
-        return self.scatter_z(partial), collect_weight(self.at, grad)
-
-    def gather_heads_back(self, own, sums):
-        return rows_to_block(self.at, own), sums
-
-    def scatter_kv_sums(self, parts, grad):
-        return scatter_xz(self.at, self.split(parts)), collect_weight(self.at, grad)
+    def feed_forward(self, own, cotangent, gain, gate, up, down):
+        normed = self.gather_z(own)
+        gate_lin = jnp.dot(normed, gate, preferred_element_type=f32)
+        up_lin = jnp.dot(normed, up, preferred_element_type=f32)
+        hidden = (jax.nn.gelu(gate_lin, approximate=True) * up_lin).astype(bf16)
+        ff_proj = self.scatter_z(contract(hidden, down, 1, 1).astype(bf16))
+        d_ff, _ = normalize_back(ff_proj, gain, cotangent.astype(f32))
+        d_ff_rows = self.gather_z(d_ff.astype(bf16))
+        d_hidden = contract(d_ff_rows, down, 1, 0)
+        _, glu_back = jax.vjp(
+            lambda gate_in, up_in: jax.nn.gelu(gate_in, approximate=True) * up_in, gate_lin, up_lin
+        )
+        d_gate, d_up = [d.astype(bf16) for d in glu_back(d_hidden)]
+        d_partial = contract(d_gate, gate, 1, 1) + contract(d_up, up, 1, 1)
+        d_normed = self.scatter_z(d_partial.astype(bf16))
+        grads = [
+            contract(left, right, 0, 0).astype(bf16)
+            for left, right in ((normed, d_gate), (normed, d_up), (d_ff_rows, hidden))
+        ]
+        return [ff_proj, d_normed] + grads
+
+    def gather_heads(self, own):
+        return rows_to_block(self.at, own)
+
+    def scatter_pairs(self, grad):
+        rows = grad.shape[0] // self.blocks
+        return scatter_xz(self.at, self.split(grad.reshape(self.blocks, rows, -1)))
+
+    def scatter_kv_sums(self, parts, out_grad, grad):
+        kv = scatter_xz(self.at, self.split(parts))
+        return kv, self.scatter_pairs(out_grad), collect_weight(self.at, grad)
 
     def scatter_heads_back(self, partial, sums):
         return rows_from_block(self.at, partial), sums
 
-    def finish(self, attn_grad, grad, gains):
-        rows = attn_grad.shape[0] // self.blocks
-        attn = scatter_xz(self.at, self.split(attn_grad.reshape(self.blocks, rows, -1)))
-        return attn, collect_weight(self.at, grad), sum_all(self.at, gains)
+    def finish(self, qkv_grad, gate_grad, up_grad, gains):
+        gate, up = collect_weight(self.at, gate_grad), collect_weight(self.at, up_grad)
+        return self.scatter_pairs(qkv_grad), gate, up, sum_all(self.at, gains)
 
 
 MESH = pl.DeviceIdType.MESH
@@ -416,14 +436,14 @@
         p, nz = self.spot, self.spot.nz
         k = nz - t
         up = remote(
-            self.parts.at[lax.rem(p.z + k, nz)],
+            self.parts(lax.rem(p.z + k, nz)),
             self.up.at[t - 1],
             self.send.at[0, t],
             self.recv.at[0, t],
             p.device(z=lax.rem(p.z + 1, nz)),
         )
         down = remote(
-            self.parts.at[lax.rem(p.z - k + nz, nz)],
+            self.parts(lax.rem(p.z - k + nz, nz)),
             self.down.at[t - 1],
             self.send.at[1, t],
             self.recv.at[1, t],
@@ -449,7 +469,7 @@
                 if t < nz - 1:
                     index = lax.rem(p.z + k - 1, nz) if way == 0 else lax.rem(p.z - k + 1 + nz, nz)
                     came = (self.up if way == 0 else self.down).at[t - 1]
-                    add_rows(self.parts.at[index], self.parts.at[index], came)
+                    add_rows(self.parts(index), self.parts(index), came)
 
     def finish(self):
         for t in range(1, self.spot.nz):
@@ -458,7 +478,7 @@
 
     def total(self, out, step=16):
         p, last = self.spot, self.spot.nz - 2
-        mine = self.parts.at[p.z]
+        mine = self.parts(p.z)
         inner = (p.z > 0) & (p.z < p.nz - 1)
 
         @pl.when(p.z == 0)
@@ -484,6 +504,7 @@
     scratch = ()
     vmem_ins = ()
     vmem_outs = ()
+    spare = 5
 
     def steps(self, p, ins, outs, scratch):
         raise NotImplementedError
@@ -652,7 +673,7 @@
         bring = pltpu.make_async_copy(given, parts, local)
         bring.start()
         bring.wait()
-        line = LineScatter(p, parts, up, down, send, recv)
+        line = LineScatter(p, lambda z: parts.at[z], up, down, send, recv)
         line.start(1)
         yield
         for t in range(1, p.nz):
@@ -699,7 +720,7 @@
             away(z).wait_recv()
             bring(z).wait()
             add_rows(parts.at[z], parts.at[z], came.at[z])
-        line = LineScatter(p, parts, up, down, send, recv)
+        line = LineScatter(p, lambda z: parts.at[z], up, down, send, recv)
         line.start(1)
         yield
         for t in range(1, nz):
@@ -1062,6 +1083,230 @@
                 across(z, i).wait_send()
 
 
+class FeedForward(Task):
+    vmem_ins = (0, 1, 2)
+    vmem_outs = (0, 1)
+    spare = 10
+
+    def __init__(self, nz, own, cotangent, gain, gate, up, down):
+        rows, depth = own.shape
+        units = gate.shape[1]
+        self.rows, self.depth, self.units = rows, depth, units
+        self.ins = (own, cotangent, gain.reshape(1, depth), gate, up, down)
+        wide = jax.ShapeDtypeStruct((depth, units), bf16)
+        exact = jax.ShapeDtypeStruct((rows, depth), f32)
+        self.outs = (exact, exact, wide, wide, wide)
+        weight = pltpu.VMEM((depth, units), bf16)
+        tokens = pltpu.VMEM((nz * rows, depth), bf16)
+        inner = pltpu.VMEM((nz * rows, units), bf16)
+        line = pltpu.VMEM((2, nz - 1, rows // 2, depth), bf16)
+        self.scratch = (
+            weight, weight, weight, tokens, tokens, inner, inner, inner, tokens, line, line,
+            DMA((8, 2, nz)), DMA((8, 2, nz)), DMA((8,)),
+        )
+
+    def steps(self, p, ins, outs, scratch):
+        own, cotangent, gain, gate_in, up_in, down_in = ins
+        ff_out, dn_out, grad_gate, grad_up, grad_down = outs
+        gate, up, down, normed, d_ff, hidden, gated, upped, parts, above, below, send, recv, local = scratch
+        nz, depth, units = p.nz, self.depth, self.units
+        part = self.rows // 2
+        half_rows = nz * part
+        tile = 768 if units % 768 == 0 and depth % 768 == 0 else 128
+
+        def entry(buffer, half):
+            return lambda z: buffer.at[pl.ds(pl.multiple_of(half * half_rows + z * part, part), part)]
+
+        gathers, scatters = [], []
+        for i, buffer in enumerate((normed, d_ff)):
+            for half in range(2):
+                k = 4 * i + half
+                gathers.append(LineGather(p, entry(buffer, half), send.at[k], recv.at[k]))
+                scatters.append(
+                    LineScatter(
+                        p, entry(parts, half), above.at[half], below.at[half], send.at[k + 2], recv.at[k + 2]
+                    )
+                )
+
+        loads = [
+            pltpu.make_async_copy(src, dst, local.at[i])
+            for i, (src, dst) in enumerate(((gate_in, gate), (up_in, up), (down_in, down)))
+        ]
+
+        def gelu(v):
+            bent = jnp.tanh(math.sqrt(2.0 / math.pi) * (v + 0.044715 * (v * v * v)))
+            return 0.5 * v * (1.0 + bent), bent
+
+        def columns(i):
+            return pl.ds(pl.multiple_of(i * tile, 128), tile)
+
+        def hide(half, low, high):
+            rows = slice(half * half_rows, (half + 1) * half_rows)
+
+            @pl.loop(low, high)
+            def _(i):
+                at = columns(i)
+                gate_lin = jnp.dot(normed[rows, :], gate[:, at], preferred_element_type=f32)
+                up_lin = jnp.dot(normed[rows, :], up[:, at], preferred_element_type=f32)
+                hidden[rows, at] = (gelu(gate_lin)[0] * up_lin).astype(bf16)
+                gated[rows, at] = gate_lin.astype(bf16)
+                upped[rows, at] = up_lin.astype(bf16)
+
+        def project(half):
+            rows = slice(half * half_rows, (half + 1) * half_rows)
+
+            @pl.loop(0, depth // tile)
+            def _(i):
+                at = columns(i)
+                parts[rows, at] = contract(hidden[rows, :], down[at, :], 1, 1).astype(bf16)
+
+        def hide_back(half, low, high):
+            rows = slice(half * half_rows, (half + 1) * half_rows)
+
+            @pl.loop(low, high)
+            def _(i):
+                at = columns(i)
+                d_hidden = jnp.dot(d_ff[rows, :], down[:, at], preferred_element_type=f32)
+                v, u = gated[rows, at].astype(f32), upped[rows, at].astype(f32)
+                value, bent = gelu(v)
+                slope = 0.5 * (1.0 + bent) + (0.5 * math.sqrt(2.0 / math.pi)) * v * (
+                    1.0 - bent * bent
+                ) * (1.0 + (3.0 * 0.044715) * (v * v))
+                gated[rows, at] = (d_hidden * u * slope).astype(bf16)
+                upped[rows, at] = (d_hidden * value).astype(bf16)
+
+        def project_back(half):
+            rows = slice(half * half_rows, (half + 1) * half_rows)
+
+            @pl.loop(0, depth // tile)
+            def _(i):
+                at = columns(i)
+                total = contract(gated[rows, :], gate[at, :], 1, 1)
+                parts[rows, at] = (total + contract(upped[rows, :], up[at, :], 1, 1)).astype(bf16)
+
+        def turn_back(half):
+            start = half * half_rows + p.z * part
+
+            @pl.loop(0, part // 16)
+            def _(i):
+                at = pl.ds(pl.multiple_of(half * part + i * 16, 16), 16)
+                values = ff_out[at, :]
+                scaled = cotangent[at, :].astype(f32) * (1.0 + gain[...])
+                factor = factor_of(values)
+                unit = values * factor
+                mean = jnp.mean(scaled * unit, axis=-1, keepdims=True)
+                here = pl.ds(pl.multiple_of(start + i * 16, 16), 16)
+                d_ff[here, :] = ((scaled - unit * mean) * factor).astype(bf16)
+
+        def weigh(left, right, out, low, high):
+            @pl.loop(low, high)
+            def _(i):
+                at = pl.ds(pl.multiple_of(i * 256, 128), 256)
+                out[at, :] = contract(left[:, at], right[...], 0, 0).astype(bf16)
+
+        def store(i, src, dst):
+            return pltpu.make_async_copy(src, dst, local.at[3 + i])
+
+        blocks = depth // 256
+        tiles = units // tile
+        one, two, one_back, two_back = gathers
+        sum_one, sum_two, sum_one_back, sum_two_back = scatters
+        keep = [
+            pltpu.make_async_copy(own.at[pl.ds(half * part, part)], entry(normed, half)(p.z), local.at[6 + half])
+            for half in range(2)
+        ]
+        keep[0].start()
+        keep[1].start()
+        for load in loads:
+            load.start()
+        keep[0].wait()
+        one.start(1)
+        keep[1].wait()
+        for s in range(1, nz):
+            one.arrive(s)
+            if s < nz - 1:
+                one.start(s + 1)
+            if s == nz - 2:
+                two.start(1)
+        for load in loads:
+            load.wait()
+        hide(0, 0, 1)
+        two.arrive(1)
+        two.start(2)
+        hide(0, 1, tiles)
+        two.arrive(2)
+        two.start(3)
+        project(0)
+        sum_one.start(1)
+        two.arrive(3)
+        hide(1, 0, 1)
+        sum_one.arrive(1)
+        sum_one.start(2)
+        hide(1, 1, tiles)
+        sum_one.arrive(2)
+        sum_one.start(3)
+        project(1)
+        sum_two.start(1)
+        sum_one.arrive(3)
+        sum_one.total(ff_out.at[pl.ds(0, part)])
+        turn_back(0)
+        one_back.start(1)
+        sum_two.arrive(1)
+        sum_two.start(2)
+        one_back.arrive(1)
+        one_back.start(2)
+        sum_two.arrive(2)
+        sum_two.start(3)
+        one_back.arrive(2)
+        one_back.start(3)
+        sum_two.arrive(3)
+        sum_two.total(ff_out.at[pl.ds(part, part)])
+        turn_back(1)
+        two_back.start(1)
+        one_back.arrive(3)
+        sum_one.finish()
+        hide_back(0, 0, 1)
+        two_back.arrive(1)
+        two_back.start(2)
+        hide_back(0, 1, tiles)
+        two_back.arrive(2)
+        two_back.start(3)
+        project_back(0)
+        sum_one_back.start(1)
+        two_back.arrive(3)
+        hide_back(1, 0, 1)
+        sum_one_back.arrive(1)
+        sum_one_back.start(2)
+        hide_back(1, 1, tiles)
+        sum_one_back.arrive(2)
+        sum_one_back.start(3)
+        sum_two.finish()
+        project_back(1)
+        sum_two_back.start(1)
+        weigh(d_ff, hidden, down, 0, blocks)
+        store(0, down, grad_down).start()
+        sum_one_back.arrive(3)
+        sum_two_back.arrive(1)
+        sum_two_back.start(2)
+        sum_one_back.total(dn_out.at[pl.ds(0, part)])
+        weigh(normed, gated, gate, 0, blocks)
+        store(1, gate, grad_gate).start()
+        sum_two_back.arrive(2)
+        sum_two_back.start(3)
+        weigh(normed, upped, up, 0, blocks)
+        store(2, up, grad_up).start()
+        sum_two_back.arrive(3)
+        sum_two_back.total(dn_out.at[pl.ds(part, part)])
+        for gather in gathers:
+            gather.finish()
+        sum_one_back.finish()
+        sum_two_back.finish()
+        store(0, down, grad_down).wait()
+        store(1, gate, grad_gate).wait()
+        store(2, up, grad_up).wait()
+        yield
+
+
 class SumAll(Task):
     vmem_ins = (0,)
     vmem_outs = (0,)
@@ -1122,6 +1367,7 @@
                     done[i] = next(steps, "end") == "end"
 
     sent = sum(x.size * 2 for t in tasks for x in t.ins)
+    spare = max(t.spare for t in tasks) * 2**20
     held = [s for t in tasks for s in t.scratch if getattr(s, "memory_space", None) == pltpu.VMEM]
     held += [t.ins[i] for t in tasks for i in t.vmem_ins] + [t.outs[i] for t in tasks for i in t.vmem_outs]
     vmem = sum(math.prod(s.shape) * jnp.dtype(s.dtype).itemsize for s in held)
@@ -1134,17 +1380,19 @@
         ],
         scratch_shapes=[s for t in tasks for s in t.scratch],
         compiler_params=pltpu.CompilerParams(
-            collective_id=number, has_side_effects=True, vmem_limit_bytes=vmem + 4 * 2**20
+            collective_id=number, has_side_effects=True, vmem_limit_bytes=vmem + spare
         ),
         cost_estimate=pl.CostEstimate(
             flops=0, bytes_accessed=sent, transcendentals=0, remote_bytes_transferred=sent
         ),
     )(*[x for t in tasks for x in t.ins])
     found, _ = split(list(results), 1)
-    return [f[0] for f in found]
-
-
-START_ORDER = "10231223" + "13222" + "12222" + "3331" + "2222" + "33333333"
+    return found[0] if len(tasks) == 1 else [f[0] for f in found]
+
+
+START_ORDER = "10231223" + "132224" + "12222" + "3331" + "2222" + "33333333"
+FINISH_ORDER = "01203111" + "1112" + "03112" + "11220" + "3112" + "2220" + "32222"
+KV_ORDER = "0120" + "12" + "2" + "20" + "12222" + "01" + "222201" + "2222"
 
 
 class Kernels:
@@ -1161,63 +1409,63 @@
     def flat(self, whole):
         return whole.reshape(-1, whole.shape[-1])
 
-    def start(self, own, attn_shard, gate, up):
+    def start(self, own, attn_shard, gate, up, down):
         nz = self.nz
         tasks = [
             PlaneGather(own),
             PairGather(nz, attn_shard, True),
             Copies(nz, gate, False),
             Copies(nz, up, False),
+            DealTask(nz, down),
         ]
-        found = self.run(tasks, START_ORDER)
-        return [self.flat(w) for w in found]
-
-    def scatter_heads_deal(self, partial, down):
-        return self.run([PlaneScatter(partial), DealTask(self.nz, down)], "10")
-
-    def gather_kv(self, own):
-        (whole,) = self.run([PairGather(self.nz, own, False)])
-        return whole.reshape((self.blocks,) + own.shape)
-
-    def gather_z_copy(self, own, pieces):
-        return [
-            self.flat(w) for w in self.run([ZGather(self.nz, own), Copies(self.nz, pieces, True)], "01001111011110")
-        ]
-
-    def gather_z(self, own):
-        return self.flat(self.run([ZGather(self.nz, own)])[0])
-
-    def scatter_z(self, partial):
-        return self.run([ZScatter(self.nz, partial)])[0]
-
-    def scatter_z_sums(self, partial, grad):
-        return self.run([ZScatter(self.nz, partial), Sums(self.nz, grad, False)], "1011110" + "11110" + "11110")
-
-    def gather_heads_back(self, own, sums):
-        rows, shard = self.run([PlaneGather(own), DealBackTask(self.nz, sums)], "01")
-        return self.flat(rows), self.flat(shard)
-
-    def scatter_kv_sums(self, parts, grad):
-        given = parts.reshape((self.nz, 2) + parts.shape[1:])
-        kv, sums = self.run([PairScatter(self.nz, given, False), Sums(self.nz, grad, False)], "10" + "11" + "0" + "110" + "11110" + "11110")
-        return kv.astype(f32), sums
+        *found, pieces = self.run(tasks, START_ORDER)
+        return [self.flat(w) for w in found] + [pieces]
+
+    def gather_kv(self, own, pieces):
+        whole, down = self.run(
+            [PairGather(self.nz, own, False), Copies(self.nz, pieces, True)], "010011110111"
+        )
+        return whole.reshape((self.blocks,) + own.shape), self.flat(down)
+
+    def scatter_heads(self, partial):
+        return self.run([PlaneScatter(partial)])[0]
+
+    def feed_forward(self, own, cotangent, gain, gate, up, down):
+        task = FeedForward(self.nz, own, cotangent, gain, gate, up, down)
+        self.number += 1
+        return run_tasks(self.nz, self.number, [task])
+
+    def gather_heads(self, own):
+        return self.flat(self.run([PlaneGather(own)])[0])
+
+    def scatter_kv_sums(self, parts, out_grad, grad):
+        nz = self.nz
+        given = parts.reshape((nz, 2) + parts.shape[1:])
+        rows = out_grad.shape[0] // self.blocks
+        out_given = out_grad.reshape(nz, 2, rows, out_grad.shape[1])
+        kv, out, sums = self.run(
+            [PairScatter(nz, given, False), PairScatter(nz, out_given, True), Sums(nz, grad, False)],
+            KV_ORDER,
+        )
+        return kv.astype(f32), out, sums
 
     def scatter_heads_back(self, partial, sums):
         rows, shard = self.run([PlaneScatter(partial), DealBackTask(self.nz, sums)], "01")
         return rows, self.flat(shard)
 
-    def finish(self, attn_grad, grad, gains):
-        rows = attn_grad.shape[0] // self.blocks
-        given = attn_grad.reshape(self.nz, 2, rows, attn_grad.shape[1])
-        attn, shard, total = self.run(
+    def finish(self, qkv_grad, gate_grad, up_grad, gains):
+        rows = qkv_grad.shape[0] // self.blocks
+        given = qkv_grad.reshape(self.nz, 2, rows, qkv_grad.shape[1])
+        qkv, gate, up, total = self.run(
             [
                 PairScatter(self.nz, given, True),
-                Sums(self.nz, grad, True),
+                Sums(self.nz, gate_grad, True),
+                Sums(self.nz, up_grad, True),
                 SumAll(gains.reshape(8, -1)),
             ],
-            "01012" + "1121" + "0" + "1121" + "0" + "1121" + "0" + "1121",
-        )
-        return attn, self.flat(shard), total.reshape(gains.shape)
+            FINISH_ORDER,
+        )
+        return qkv, self.flat(gate), self.flat(up), total.reshape(gains.shape)
 
 
 def causal_mask(rows):
@@ -1424,8 +1672,8 @@
     heads_width = w_query.shape[1]
     qkv_width = heads_width + 2 * HEAD_DIM
     attn_shard = jnp.concatenate([w_query, w_key, w_value, w_out.T], axis=1)
-    normed_one, attn_full, gate_full, up_full = comm.start(
-        normalize(token_f32, norm_attn_in).astype(bf16), attn_shard, w_gate, w_up
+    normed_one, attn_full, gate_full, up_full, down_pieces = comm.start(
+        normalize(token_f32, norm_attn_in).astype(bf16), attn_shard, w_gate, w_up, w_down.T
     )
     qkv_full, out_full = attn_full[:, :qkv_width], attn_full[:, qkv_width:]
     qkv_lin = jnp.dot(normed_one, qkv_full, preferred_element_type=f32)
@@ -1442,45 +1690,26 @@
         ],
         axis=1,
     ).astype(bf16)
-    all_kv = comm.gather_kv(own_kv)
+    all_kv, down_full = comm.gather_kv(own_kv, down_pieces)
     attn_rows, attended, inverse = attend(kinds, queries, all_kv)
-    attn_proj, down_pieces = comm.scatter_heads_deal(
-        contract(attn_rows, out_full, 1, 1).astype(bf16), w_down.T
+    attn_proj = comm.scatter_heads(contract(attn_rows, out_full, 1, 1).astype(bf16))
+    middle = token_f32 + normalize(attn_proj, norm_attn_out)
+
+    ff_proj, d_normed_two, gate_sum, up_sum, down_sum = comm.feed_forward(
+        normalize(middle, norm_ff_in).astype(bf16), cotangent, norm_ff_out, gate_full, up_full, down_full
     )
-    middle = token_f32 + normalize(attn_proj, norm_attn_out)
-
-    normed_two, down_full = comm.gather_z_copy(
-        normalize(middle, norm_ff_in).astype(bf16), down_pieces
-    )
-    gate_lin = jnp.dot(normed_two, gate_full, preferred_element_type=f32)
-    up_lin = jnp.dot(normed_two, up_full, preferred_element_type=f32)
-    hidden = (jax.nn.gelu(gate_lin, approximate=True) * up_lin).astype(bf16)
-    ff_proj = comm.scatter_z(contract(hidden, down_full, 1, 1).astype(bf16))
     layer_out = middle + normalize(ff_proj, norm_ff_out)
-
     upstream = cotangent.astype(f32)
-    d_ff, grad_ff_out = normalize_back(ff_proj, norm_ff_out, upstream)
-    d_ff_rows = comm.gather_z(d_ff.astype(bf16))
-    d_hidden = contract(d_ff_rows, down_full, 1, 0)
-    _, glu_back = jax.vjp(
-        lambda gate_in, up_in: jax.nn.gelu(gate_in, approximate=True) * up_in, gate_lin, up_lin
-    )
-    d_gate, d_up = glu_back(d_hidden)
-    d_gate = d_gate.astype(bf16)
-    d_up = d_up.astype(bf16)
-    d_partial = contract(d_gate, gate_full, 1, 1) + contract(d_up, up_full, 1, 1)
-    d_normed_two, down_sums = comm.scatter_z_sums(
-        d_partial.astype(bf16), contract(d_ff_rows, hidden, 0, 0).astype(bf16)
-    )
+    _, grad_ff_out = normalize_back(ff_proj, norm_ff_out, upstream)
 
     d_middle_part, grad_ff_in = normalize_back(middle, norm_ff_in, d_normed_two)
     d_middle = upstream + d_middle_part
     d_proj, grad_attn_out = normalize_back(attn_proj, norm_attn_out, d_middle)
-    d_proj_rows, grad_down = comm.gather_heads_back(d_proj.astype(bf16), down_sums)
+    d_proj_rows = comm.gather_heads(d_proj.astype(bf16))
     d_attended = contract(d_proj_rows, out_full, 1, 0).astype(bf16)
     d_query, d_kv_parts = attend_back(kinds, queries, all_kv, d_attended, attended, inverse)
-    d_kv, gate_sums = comm.scatter_kv_sums(
-        d_kv_parts, contract(normed_two, d_gate, 0, 0).astype(bf16)
+    d_kv, grad_out, down_sums = comm.scatter_kv_sums(
+        d_kv_parts, contract(d_proj_rows, attn_rows, 0, 0).astype(bf16), down_sum
     )
     d_qkv_lin = jnp.concatenate(
         [
@@ -1491,27 +1720,26 @@
         ],
         axis=1,
     ).astype(bf16)
-    d_normed_one, grad_gate = comm.scatter_heads_back(
-        contract(d_qkv_lin, qkv_full, 1, 1).astype(bf16), gate_sums
+    d_normed_one, grad_down = comm.scatter_heads_back(
+        contract(d_qkv_lin, qkv_full, 1, 1).astype(bf16), down_sums
     )
     d_token_part, grad_attn_in = normalize_back(token_f32, norm_attn_in, d_normed_one)
     input_grad = (d_middle + d_token_part).astype(bf16)
-    grad_attn, grad_up, gains = comm.finish(
-        jnp.concatenate(
-            [contract(normed_one, d_qkv_lin, 0, 0), contract(d_proj_rows, attn_rows, 0, 0)], axis=1
-        ).astype(bf16),
-        contract(normed_two, d_up, 0, 0).astype(bf16),
+    grad_qkv, grad_gate, grad_up, gains = comm.finish(
+        contract(normed_one, d_qkv_lin, 0, 0).astype(bf16),
+        gate_sum,
+        up_sum,
         jnp.stack([grad_attn_in, grad_attn_out, grad_ff_in, grad_ff_out]),
     )
-    grad_attn, grad_gate, grad_up = [g.astype(f32) for g in (grad_attn, grad_gate, grad_up)]
+    grad_qkv, grad_gate, grad_up = [g.astype(f32) for g in (grad_qkv, grad_gate, grad_up)]
     return (
         layer_out.astype(bf16),
         input_grad,
         gains[0],
-        grad_attn[:, :heads_width],
-        grad_attn[:, heads_width : heads_width + HEAD_DIM],
-        grad_attn[:, heads_width + HEAD_DIM : qkv_width],
-        grad_attn[:, qkv_width:].T,
+        grad_qkv[:, :heads_width],
+        grad_qkv[:, heads_width : heads_width + HEAD_DIM],
+        grad_qkv[:, heads_width + HEAD_DIM :],
+        grad_out.astype(f32).T,
         gains[1],
         gains[2],
         grad_gate,

time: 853 us -> 757 us (0.89)
  matrix products: 106 us -> 14.4 us
    dot_general x12 -> x5, matrix products: 87.3 us -> 11.8 us  [contract(): lax.dot_general(left_side, right_side, (((left_dim,), (right_dim,)), ((),...]
    dot_general x2 -> x0, matrix products: 16.4 us -> none  [the longest x1 8.94 us: on_device(): gate_lin = jnp.dot(normed_two, gate_full, preferred_element_type=f32)]
    pallas_call x11 -> x8, Pallas kernels: 661 us -> 672 us  [run_tasks(): pl.pallas_call(body, out_shape=[o for t in tasks for o in t.outs], in_spe...]
where the time goes in v3:
time: 757 us; the launch traced here: 748 us
  Pallas kernels  677 us (89%)
  other arithmetic  32.1 us (4%)
  local copies, waits for them, and re-layouts  21.5 us (3%)
  matrix products  14.4 us (2%)
    pallas_call x8, Pallas kernels, run_tasks(): pl.pallas_call(body, out_shape=[o for t in tasks for o in t.outs], in_spe...  672 us
    unnamed x76, local copies, waits for them, and re-layouts  15.2 us

profile of v3, /device:TPU:2, one launch (start us, length us, event | category | flops | bytes accessed | tf_op | source)
XLA Modules:
  0.0 748.3 jit_solution(9932743877425827722)
XLA Ops:
  0.7 1.3 fusion.21
  2.1 1.3 select_reduce_fusion
  4.7 2.0 fusion.77.kinds
  6.7 1.3 reshape.169.refs_2_
  8.0 0.7 broadcast_add_fusion.3
  8.7 0.7 broadcast_add_fusion.2
  9.4 0.7 broadcast_add_fusion
  10.1 0.2 fusion.14.refs_0_
  10.4 1.2 pad_maximum_fusion.refs_1_
  11.6 0.5 copy-done.3
  12.1 1.3 copy-done.5
  13.4 159.0 %shard_map.246 = (bf16[4,128,2304]{2,1,0:T(8,128)(2,1)S(1)}, bf16[4,2,288,1536]{3,2,1,0:T(8,128)(2,1)S(1)}, bf16[4,2,2,144,2304]{4,3,2,1,0:T(8,128)(2,1)}, bf16[...) custom-call(bf16[128,2304]{1,0:T(8,128)(2,1)S(1)} %fusion.14.refs_0_, ...), custom_call_target="tpu_custom_call" | custom-call | bytes 5455872 | tf_op jit(solution)/shard_map/pallas_call | solution.py:1374
  172.4 2.6 fusion.1
  175.0 1.3 fusion.68
  176.6 60.2 %shard_map.247 = (bf16[4,2,512,512]{3,2,1,0:T(8,128)(2,1)S(1)}, bf16[4,2,2,144,2304]{4,3,2,1,0:T(8,128)(2,1)S(1)}) custom-call(bf16[512,512]{1,0:T(8,128)(2,1)S(1)} %pad_maximum_fusion.2.refs_0_, bf16[4,144,1152]{2,1,0:T(8,128)(2,1)S(1)} %get-tuple-element.41.refs_1_), custom_call_target="tpu_custom_call" | custom-call | bytes 1851392 | tf_op jit(solution)/shard_map/pallas_call | solution.py:1374
  236.8 3.9 copy-done
  240.7 2.0 shard_map.248
  242.7 1.4 convolution_convert_fusion.3
  244.2 30.8 %shard_map.249 = f32[128,2304]{1,0:T(8,128)S(1)} custom-call(bf16[4,128,2304]{2,1,0:T(8,128)(2,1)S(1)} %bitcast.59), custom_call_target="tpu_custom_call" | custom-call | bytes 2359296 | tf_op jit(solution)/shard_map/pallas_call | solution.py:1374
  275.0 0.2 multiply_reduce_fusion.6
  275.2 0.9 copy-done.22
  276.1 0.4 multiply_reduce_fusion.5
  276.5 1.0 multiply_convert_fusion.1.refs_0_
  277.5 164.2 %shard_map.250 = (f32[128,2304]{1,0:T(8,128)}, f32[128,2304]{1,0:T(8,128)}, bf16[2304,2304]{1,0:T(8,128)(2,1)}, bf16[2304,2304]{1,0:T(8,128)(2,1)}, bf16[2304,2304]{1,0:T(8,128)(2,1)}) custom-call(bf16[128,2304]{1,0:T(8,128)(2,1)} %multiply_convert_fusion.1.refs_0_, bf16[128,2304]{1,0:T(8,128)(2,1)} %refs_1_.1, f32[1,2304]{1,0:T(1,128)} %reshape.169.refs_2_, ...), custom_call_target="tpu_custom_call" | custom-call | bytes 33034752 | tf_op jit(solution)/shard_map/pallas_call | solution.py:1374
  441.7 1.5 multiply_reduce_fusion.4
  443.3 0.4 multiply_reduce_fusion
  443.7 0.9 copy-done.25
  444.6 0.1 copy-done.27
  444.7 2.2 fusion.13
  447.0 0.3 multiply_convert_fusion.refs_0_
  447.3 0.7 stack.31
  447.9 35.0 %shard_map.251 = bf16[4,128,2304]{2,1,0:T(8,128)(2,1)S(1)} custom-call(bf16[128,2304]{1,0:T(8,128)(2,1)S(1)} %multiply_convert_fusion.refs_0_), custom_call_target="tpu_custom_call" | custom-call | bytes 589824 | tf_op jit(solution)/shard_map/pallas_call | solution.py:1374
  482.9 3.2 fusion.10.up_ref
  486.3 2.9 shard_map.252
  489.2 2.0 copy-done.1
  491.2 1.4 convolution_convert_fusion.2
  492.6 0.7 slice-done.2
  493.4 2.2 copy-done.2
  495.6 67.0 %shard_map.253 = (bf16[512,512]{1,0:T(8,128)(2,1)S(1)}, bf16[288,512]{1,0:T(8,128)(2,1)S(1)}, bf16[4,144,1152]{2,1,0:T(8,128)(2,1)S(1)}) custom-call(bf16[4,2,512,512]{3,2,1,0:T(8,128)(2,1)S(1)} %bitcast.55, bf16[4,2,288,512]{3,2,1,0:T(8,128)(2,1)S(1)} %bitcast.60, bf16[4,2,2,144,2304]{4,3,2,1,0:T(8,128)(2,1)S(1)} %bitcast.52), custom_call_target="tpu_custom_call" | custom-call | bytes 17170432 | tf_op jit(solution)/shard_map/pallas_call | solution.py:1374
  562.6 0.9 convert_bitcast_fusion.1
  563.6 1.2 fusion.76
  564.8 1.2 fusion.75
  566.0 1.2 fusion.74
  567.2 1.2 fusion.73
  568.3 1.2 fusion.72
  569.5 1.2 fusion.71
  570.8 2.9 convolution_convert_fusion.1
  573.7 32.3 %shard_map.254 = (f32[128,2304]{1,0:T(8,128)S(1)}, bf16[2,144,2304]{2,1,0:T(8,128)(2,1)S(1)}) custom-call(bf16[4,128,2304]{2,1,0:T(8,128)(2,1)S(1)} %bitcast.56, bf16[4,144,1152]{2,1,0:T(8,128)(2,1)S(1)} %get-tuple-element.55.refs_1_), custom_call_target="tpu_custom_call" | custom-call | bytes 3686400 | tf_op jit(solution)/shard_map/pallas_call | solution.py:1374
  606.1 0.4 fusion.20
  606.5 0.3 copy-done.30
  606.8 2.6 fusion.19
  609.5 2.9 convolution_convert_fusion
  612.4 123.9 %shard_map.255 = (bf16[288,1024]{1,0:T(8,128)(2,1)S(1)}, bf16[2,144,2304]{2,1,0:T(8,128)(2,1)S(1)}, bf16[2,144,2304]{2,1,0:T(8,128)(2,1)S(1)}, f32[8,1152]{1,0:T(8,128)S(1)}) custom-call(bf16[4,2,288,1024]{3,2,1,0:T(8,128)(2,1)S(1)} %bitcast.54, bf16[4,2,2,144,2304]{4,3,2,1,0:T(8,128)(2,1)} %bitcast.74, bf16[4,2,2,144,2304]{4,3,2,1,0:T(8,128)(2,1)} %bitcast.75, ...), custom_call_target="tpu_custom_call" | custom-call | bytes 25970688 | tf_op jit(solution)/shard_map/pallas_call | solution.py:1374
  736.3 1.1 copy-done.6
  737.3 1.1 copy-done.8
  738.4 0.6 squeeze.23
  739.0 0.6 squeeze.22
  739.6 0.6 squeeze.21
  740.2 0.6 squeeze.20
  740.8 0.9 slice.133
  741.7 0.8 fusion.78
  742.6 1.8 convert_bitcast_fusion
  744.3 1.8 bitcast_convert_fusion.1
  746.1 1.8 bitcast_convert_fusion
  (89 shorter events, 0.9 us)
Async XLA Ops:
  0.6 9.5 %copy-start.21 = (bf16[128,2304]{1,0:T(8,128)(2,1)S(1)}, bf16[128,2304]{1,0:T(8,128)(2,1)}, u32[]{:S(2)}) copy-start(bf16[128,2304]{1,0:T(8,128)(2,1)} %param.15) | copy-start | bytes 1769476
  0.7 9.7 %copy-start.28 = (bf16[512,288]{0,1:T(8,128)(2,1)S(1)}, bf16[512,288]{0,1:T(8,128)(2,1)}, u32[]{:S(2)}) copy-start(bf16[512,288]{0,1:T(8,128)(2,1)} %param.21) | copy-start | bytes 884740
  0.7 9.7 %copy-start.29 = (bf16[288,256]{1,0:T(8,128)(2,1)S(1)}, bf16[288,256]{1,0:T(8,128)(2,1)}, u32[]{:S(2)}) copy-start(bf16[288,256]{1,0:T(8,128)(2,1)} %param.20) | copy-start | bytes 442372
  10.1 1.5 copy-start.4
  10.4 1.7 copy-start.3
  12.1 1.3 copy-start.5
  172.4 2.6 copy-start.13
  172.4 70.3 %copy-start.10 = (bf16[4,2,288,1536]{3,2,1,0:T(8,128)(2,1)}, bf16[4,2,288,1536]{3,2,1,0:T(8,128)(2,1)S(1)}, u32[]{:S(2)}) copy-start(bf16[4,2,288,1536]{3,2,1,0:T(8,128)(2,1)S(1)} %get-tuple-element.40) | copy-start | bytes 21233668
  236.7 3.9 copy-start
  240.7 2.0 copy-start.11
  242.7 1.5 copy-start.15
  242.7 1.5 copy-start.17
  242.7 1.5 copy-start.19
  275.0 1.1 copy-start.22
  441.7 1.6 copy-start.26
  443.3 1.3 copy-start.25
  443.3 1.4 copy-start.27
  447.0 36.0 %copy-start.24 = (f32[128,2304]{1,0:T(8,128)}, f32[128,2304]{1,0:T(8,128)S(1)}, u32[]{:S(2)}) copy-start(f32[128,2304]{1,0:T(8,128)S(1)} %get-tuple-element.84) | copy-start | bytes 3538948
  482.9 3.2 copy-start.12
  482.9 3.2 copy-start.16
  482.9 3.3 copy-start.20
  486.3 4.9 copy-start.18
  486.3 6.3 slice-start
  486.3 6.3 slice-start.1
  486.3 84.5 %slice-start.3 = ((s8[7077888]{0:T(1024)(128)(4,1)}), s8[2883584]{0:T(1024)(128)(4,1)S(1)}, s32[]{:S(2)}) async-start(s8[7077888]{0:T(1024)(128)(4,1)} %bitcast.67), calls=%async_computation.3 | async-start | bytes 5767168
  489.2 2.0 copy-start.1
  491.2 2.2 slice-start.2
  493.4 2.2 copy-start.2
  495.6 75.2 %slice-start.4 = ((s8[7077888]{0:T(1024)(128)(4,1)}), s8[4194304]{0:T(1024)(128)(4,1)S(1)}, s32[]{:S(2)}) async-start(s8[7077888]{0:T(1024)(128)(4,1)} %bitcast.67), calls=%async_computation.4 | async-start | bytes 8388608
  570.8 2.9 copy-start.31
  573.7 32.4 %copy-start.23 = (bf16[128,2304]{1,0:T(8,128)(2,1)S(1)}, bf16[128,2304]{1,0:T(8,128)(2,1)}, u32[]{:S(2)}) copy-start(bf16[128,2304]{1,0:T(8,128)(2,1)} %param.15) | copy-start | bytes 1769476
  606.0 0.7 copy-start.30
  606.8 2.7 copy-start.14
  606.8 2.7 copy-start.32
  736.2 1.1 copy-start.6
  737.3 1.1 copy-start.8
  742.6 1.8 copy-start.9
  744.3 1.8 copy-start.7

commit v4 on v3

--- a/solution.py
+++ b/solution.py
@@ -40,15 +40,6 @@
     scaled = upstream * (1.0 + weight_gain)
     inner = jnp.mean(scaled * unit, axis=-1, keepdims=True)
     return (scaled - unit * inner) * factor, jnp.sum(upstream * unit, axis=0)
-
-
-def rope_tables(positions):
-    half_dim = HEAD_DIM // 2
-    frequency = jnp.exp(
-        jnp.arange(half_dim, dtype=f32) * (-2.0 * math.log(10000.0) / HEAD_DIM)
-    )
-    angles = positions.astype(f32)[:, None] * frequency[None, :]
-    return (jnp.cos(angles), jnp.sin(angles))
 
 
 def rotate(tensor, cosine, sine_table):
@@ -253,17 +244,17 @@
     def split(self, whole):
         return turn(self.at, whole.reshape((self.nz, whole.shape[0] // self.nz) + whole.shape[1:]))
 
-    def start(self, own, attn_shard, gate, up, down):
+    def start(self, own, qkv_shard, gate, up):
         at = self.at
-        attn_full = gather_zx(at, attn_shard).reshape(own.shape[1], -1)
-        weights = [spread_weight(at, w) for w in (gate, up, down)]
-        return [rows_to_block(at, own), attn_full] + weights
-
-    def gather_kv(self, own, down):
-        return gather_zx(self.at, own).reshape((self.blocks,) + own.shape), down
-
-    def scatter_heads(self, partial):
-        return rows_from_block(self.at, partial)
+        qkv_full = gather_zx(at, qkv_shard).reshape(own.shape[1], -1)
+        return rows_to_block(at, own), qkv_full, spread_weight(at, gate), spread_weight(at, up)
+
+    def gather_kv(self, own, out_shard, up):
+        out_full = gather_zx(self.at, out_shard).reshape(-1, out_shard.shape[1])
+        return gather_zx(self.at, own).reshape((self.blocks,) + own.shape), out_full, up
+
+    def scatter_heads(self, partial, down):
+        return rows_from_block(self.at, partial), spread_weight(self.at, down)
 
     def gather_z(self, own):
         whole = unturn(self.at, gather_z(self.at, own))
@@ -369,8 +360,13 @@
         pl.semaphore_wait(barrier, len(found))
 
 
-def add_rows(out, left, right, step=16):
+def row_step(rows):
+    return next(step for step in (48, 32, 16) if rows % step == 0)
+
+
+def add_rows(out, left, right):
     rows = left.shape[0]
+    step = row_step(rows)
 
     @pl.loop(0, rows // step)
     def _(i):
@@ -476,18 +472,20 @@
             for sends, _, copy in self.copies(t):
                 pl.when(sends)(copy.wait_send)
 
-    def total(self, out, step=16):
+    def total(self, out):
         p, last = self.spot, self.spot.nz - 2
         mine = self.parts(p.z)
         inner = (p.z > 0) & (p.z < p.nz - 1)
 
         @pl.when(p.z == 0)
         def _():
-            add_rows(out, mine, self.down.at[last], step)
+            add_rows(out, mine, self.down.at[last])
 
         @pl.when(p.z == p.nz - 1)
         def _():
-            add_rows(out, mine, self.up.at[last], step)
+            add_rows(out, mine, self.up.at[last])
+
+        step = row_step(out.shape[0])
 
         @pl.when(inner)
         def _():
@@ -833,89 +831,94 @@
             rows, units = given.shape
             half, quarter = rows // 2, 2 * units // nz
             self.ins = (given.reshape(2, half, units),)
-        self.quarter = quarter
-        self.outs = (jax.ShapeDtypeStruct((nz, 2, 2, half, 2 * quarter), bf16),)
-        self.scratch = (
-            DMA((nz,)), DMA((nz,)), DMA((nz,)), DMA((nz,)), DMA((nz, 2)), DMA((nz, 2)),
-            DMA((nz, 2)), DMA((nz, 2)),
-        )
+        self.outs = (jax.ShapeDtypeStruct((nz * 4 * half, 2 * quarter), bf16),)
+        self.scratch = copy_sems(nz)
 
     def steps(self, p, ins, outs, scratch):
-        (given,), (full,) = ins, outs
-        d_send, d_recv, f_send, f_recv, s_send, s_recv, x_send, x_recv = scratch
-        nz, quarter = p.nz, self.quarter
-
-        def place(z, x, c, y):
-            columns = pl.ds(pl.multiple_of(y * quarter, 128), quarter)
-            return full.at[z, x, c, :, columns]
-
-        fx, fy = p.x + (1 - 2 * p.x) * (1 - p.c), p.y + (1 - 2 * p.y) * p.c
-        sx, sy = p.x + (1 - 2 * p.x) * p.c, p.y + (1 - 2 * p.y) * (1 - p.c)
-
-        def own(z):
-            return given.at[z] if self.dealt else place(z, p.x, p.c, p.y)
-
-        def first(z):
-            target = p.device(x=fx, y=fy)
-            return remote(own(z), place(z, p.x, p.c, p.y), f_send.at[z], f_recv.at[z], target)
-
-        def second(z, which):
-            x, y = (fx, fy) if which else (p.x, p.y)
-            here = place(z, x, p.c, y)
-            src = here if which else own(z)
-            target = p.device(x=sx, y=sy)
-            return remote(src, here, s_send.at[z, which], s_recv.at[z, which], target)
-
-        def across(z, x):
-            here = full.at[z, x, p.c]
-            return remote(here, here, x_send.at[z, x], x_recv.at[z, x], p.partner())
-
-        def keep(z):
-            return pltpu.make_async_copy(given.at[z], place(z, p.x, p.c, p.y), d_send.at[z])
-
-        order = [exclusive_or(p.z, i) for i in range(nz)]
-        if self.dealt:
-            for z in order:
-                first(z).start()
-                second(z, 0).start()
-                keep(z).start()
-            for z in order:
-                keep(z).wait()
+        return copy_steps(p, ins[0], outs[0], scratch, self.dealt)
+
+
+def copy_sems(nz):
+    one, two = DMA((nz,)), DMA((nz, 2))
+    return (one, one, one, one, two, two, two, two)
+
+
+def copy_steps(p, given, full, sems, dealt):
+    d_send, d_recv, f_send, f_recv, s_send, s_recv, x_send, x_recv = sems
+    nz = p.nz
+    quarter, half = full.shape[1] // 2, full.shape[0] // (4 * nz)
+
+    def strip(z, x, c):
+        return pl.ds(pl.multiple_of(((z * 2 + x) * 2 + c) * half, half), half)
+
+    def place(z, x, c, y):
+        return full.at[strip(z, x, c), pl.ds(pl.multiple_of(y * quarter, 128), quarter)]
+
+    fx, fy = p.x + (1 - 2 * p.x) * (1 - p.c), p.y + (1 - 2 * p.y) * p.c
+    sx, sy = p.x + (1 - 2 * p.x) * p.c, p.y + (1 - 2 * p.y) * (1 - p.c)
+
+    def own(z):
+        return given.at[z] if dealt else place(z, p.x, p.c, p.y)
+
+    def first(z):
+        target = p.device(x=fx, y=fy)
+        return remote(own(z), place(z, p.x, p.c, p.y), f_send.at[z], f_recv.at[z], target)
+
+    def second(z, which):
+        x, y = (fx, fy) if which else (p.x, p.y)
+        here = place(z, x, p.c, y)
+        src = here if which else own(z)
+        target = p.device(x=sx, y=sy)
+        return remote(src, here, s_send.at[z, which], s_recv.at[z, which], target)
+
+    def across(z, x):
+        here = full.at[strip(z, x, p.c)]
+        return remote(here, here, x_send.at[z, x], x_recv.at[z, x], p.partner())
+
+    def keep(z):
+        return pltpu.make_async_copy(given.at[z], place(z, p.x, p.c, p.y), d_send.at[z])
+
+    order = [exclusive_or(p.z, i) for i in range(nz)]
+    if dealt:
+        for z in order:
+            first(z).start()
+            second(z, 0).start()
+            keep(z).start()
+        for z in order:
+            keep(z).wait()
+        yield
+    else:
+        deal = Deal(p, given, lambda z, c: place(z, p.x, c, p.y), quarter, d_send, d_recv)
+        deal.start(True)
+        yield
+        deal.arrive(order[0])
+        first(order[0]).start()
+        second(order[0], 0).start()
+        yield
+        deal.start(False)
+        yield
+        for z in order[1:]:
+            deal.arrive(z)
+            first(z).start()
+            second(z, 0).start()
             yield
-        else:
-            deal = Deal(
-                p, given, lambda z, half: place(z, p.x, half, p.y), quarter, d_send, d_recv
-            )
-            deal.start(True)
-            yield
-            deal.arrive(order[0])
-            first(order[0]).start()
-            second(order[0], 0).start()
-            yield
-            deal.start(False)
-            yield
-            for z in order[1:]:
-                deal.arrive(z)
-                first(z).start()
-                second(z, 0).start()
-                yield
-        for z in order:
-            first(z).wait_recv()
-            second(z, 1).start()
-            yield
-        for z in order:
-            second(z, 0).wait_recv()
-            second(z, 1).wait_recv()
-            across(z, 0).start()
-            across(z, 1).start()
-            yield
-        for z in range(nz):
-            first(z).wait_send()
-            for i in range(2):
-                second(z, i).wait_send()
-                across(z, i).wait()
-        if not self.dealt:
-            deal.finish()
+    for z in order:
+        first(z).wait_recv()
+        second(z, 1).start()
+        yield
+    for z in order:
+        second(z, 0).wait_recv()
+        second(z, 1).wait_recv()
+        across(z, 0).start()
+        across(z, 1).start()
+        yield
+    for z in range(nz):
+        first(z).wait_send()
+        for i in range(2):
+            second(z, i).wait_send()
+            across(z, i).wait()
+    if not dealt:
+        deal.finish()
 
 
 class DealBack:
@@ -1088,11 +1091,11 @@
     vmem_outs = (0, 1)
     spare = 10
 
-    def __init__(self, nz, own, cotangent, gain, gate, up, down):
+    def __init__(self, nz, own, cotangent, gain, gate, up, down_pieces):
         rows, depth = own.shape
         units = gate.shape[1]
         self.rows, self.depth, self.units = rows, depth, units
-        self.ins = (own, cotangent, gain.reshape(1, depth), gate, up, down)
+        self.ins = (own, cotangent, gain.reshape(1, depth), gate, up, down_pieces)
         wide = jax.ShapeDtypeStruct((depth, units), bf16)
         exact = jax.ShapeDtypeStruct((rows, depth), f32)
         self.outs = (exact, exact, wide, wide, wide)
@@ -1102,17 +1105,19 @@
         line = pltpu.VMEM((2, nz - 1, rows // 2, depth), bf16)
         self.scratch = (
             weight, weight, weight, tokens, tokens, inner, inner, inner, tokens, line, line,
-            DMA((8, 2, nz)), DMA((8, 2, nz)), DMA((8,)),
+            DMA((8, 2, nz)), DMA((8, 2, nz)), DMA((8,)), *copy_sems(nz),
         )
 
     def steps(self, p, ins, outs, scratch):
         own, cotangent, gain, gate_in, up_in, down_in = ins
         ff_out, dn_out, grad_gate, grad_up, grad_down = outs
-        gate, up, down, normed, d_ff, hidden, gated, upped, parts, above, below, send, recv, local = scratch
+        gate, up, down, normed, d_ff, hidden, gated, upped, parts, above, below, *sems = scratch
+        send, recv, local, *down_sems = sems
+        copies = copy_steps(p, down_in, down, down_sems, True)
         nz, depth, units = p.nz, self.depth, self.units
         part = self.rows // 2
         half_rows = nz * part
-        tile = 768 if units % 768 == 0 and depth % 768 == 0 else 128
+        tile = units // 3
 
         def entry(buffer, half):
             return lambda z: buffer.at[pl.ds(pl.multiple_of(half * half_rows + z * part, part), part)]
@@ -1130,7 +1135,7 @@
 
         loads = [
             pltpu.make_async_copy(src, dst, local.at[i])
-            for i, (src, dst) in enumerate(((gate_in, gate), (up_in, up), (down_in, down)))
+            for i, (src, dst) in enumerate(((gate_in, gate), (up_in, up)))
         ]
 
         def gelu(v):
@@ -1208,7 +1213,6 @@
             return pltpu.make_async_copy(src, dst, local.at[3 + i])
 
         blocks = depth // 256
-        tiles = units // tile
         one, two, one_back, two_back = gathers
         sum_one, sum_two, sum_one_back, sum_two_back = scatters
         keep = [
@@ -1217,84 +1221,87 @@
         ]
         keep[0].start()
         keep[1].start()
-        for load in loads:
-            load.start()
         keep[0].wait()
         one.start(1)
         keep[1].wait()
-        for s in range(1, nz):
-            one.arrive(s)
-            if s < nz - 1:
-                one.start(s + 1)
-            if s == nz - 2:
-                two.start(1)
+        next(copies)
+        for load in loads:
+            load.start()
+        one.arrive(1)
+        one.start(2)
+        two.start(1)
+        one.arrive(2)
+        one.start(3)
+        for _ in range(nz):
+            next(copies)
+        one.arrive(3)
+        two.arrive(1)
+        two.start(2)
         for load in loads:
             load.wait()
         hide(0, 0, 1)
-        two.arrive(1)
-        two.start(2)
-        hide(0, 1, tiles)
         two.arrive(2)
         two.start(3)
+        hide(0, 1, 3)
+        two.arrive(3)
+        hide(1, 0, 1)
+        for _ in copies:
+            pass
         project(0)
         sum_one.start(1)
-        two.arrive(3)
-        hide(1, 0, 1)
+        hide(1, 1, 3)
         sum_one.arrive(1)
         sum_one.start(2)
-        hide(1, 1, tiles)
+        project(1)
+        sum_two.start(1)
         sum_one.arrive(2)
         sum_one.start(3)
-        project(1)
-        sum_two.start(1)
+        sum_two.arrive(1)
+        sum_two.start(2)
         sum_one.arrive(3)
         sum_one.total(ff_out.at[pl.ds(0, part)])
         turn_back(0)
         one_back.start(1)
-        sum_two.arrive(1)
-        sum_two.start(2)
+        sum_two.arrive(2)
+        sum_two.start(3)
         one_back.arrive(1)
         one_back.start(2)
-        sum_two.arrive(2)
-        sum_two.start(3)
-        one_back.arrive(2)
-        one_back.start(3)
         sum_two.arrive(3)
         sum_two.total(ff_out.at[pl.ds(part, part)])
         turn_back(1)
+        one_back.arrive(2)
+        one_back.start(3)
         two_back.start(1)
         one_back.arrive(3)
-        sum_one.finish()
-        hide_back(0, 0, 1)
+        hide_back(0, 0, 3)
         two_back.arrive(1)
         two_back.start(2)
-        hide_back(0, 1, tiles)
+        sum_one.finish()
+        project_back(0)
+        sum_one_back.start(1)
         two_back.arrive(2)
         two_back.start(3)
-        project_back(0)
-        sum_one_back.start(1)
         two_back.arrive(3)
-        hide_back(1, 0, 1)
+        hide_back(1, 0, 3)
         sum_one_back.arrive(1)
         sum_one_back.start(2)
-        hide_back(1, 1, tiles)
-        sum_one_back.arrive(2)
-        sum_one_back.start(3)
         sum_two.finish()
         project_back(1)
         sum_two_back.start(1)
         weigh(d_ff, hidden, down, 0, blocks)
         store(0, down, grad_down).start()
-        sum_one_back.arrive(3)
+        sum_one_back.arrive(2)
         sum_two_back.arrive(1)
         sum_two_back.start(2)
-        sum_one_back.total(dn_out.at[pl.ds(0, part)])
+        sum_one_back.start(3)
         weigh(normed, gated, gate, 0, blocks)
         store(1, gate, grad_gate).start()
         sum_two_back.arrive(2)
         sum_two_back.start(3)
         weigh(normed, upped, up, 0, blocks)
         store(2, up, grad_up).start()
+        sum_one_back.arrive(3)
+        sum_one_back.total(dn_out.at[pl.ds(0, part)])
         sum_two_back.arrive(3)
         sum_two_back.total(dn_out.at[pl.ds(part, part)])
         for gather in gathers:
@@ -1390,7 +1397,7 @@
     return found[0] if len(tasks) == 1 else [f[0] for f in found]
 
 
-START_ORDER = "10231223" + "132224" + "12222" + "3331" + "2222" + "33333333"
+START_ORDER = "10212" + "23" + "1222" + "12222" + "3" + "12222"
 FINISH_ORDER = "01203111" + "1112" + "03112" + "11220" + "3112" + "2220" + "32222"
 KV_ORDER = "0120" + "12" + "2" + "20" + "12222" + "01" + "222201" + "2222"
 
@@ -1409,26 +1416,27 @@
     def flat(self, whole):
         return whole.reshape(-1, whole.shape[-1])
 
-    def start(self, own, attn_shard, gate, up, down):
+    def start(self, own, qkv_shard, gate, up):
         nz = self.nz
         tasks = [
             PlaneGather(own),
-            PairGather(nz, attn_shard, True),
+            PairGather(nz, qkv_shard, True),
             Copies(nz, gate, False),
-            Copies(nz, up, False),
-            DealTask(nz, down),
+            DealTask(nz, up),
         ]
-        *found, pieces = self.run(tasks, START_ORDER)
-        return [self.flat(w) for w in found] + [pieces]
-
-    def gather_kv(self, own, pieces):
-        whole, down = self.run(
-            [PairGather(self.nz, own, False), Copies(self.nz, pieces, True)], "010011110111"
+        rows, qkv, gate_full, pieces = self.run(tasks, START_ORDER)
+        return self.flat(rows), self.flat(qkv), gate_full, pieces
+
+    def gather_kv(self, own, out_shard, pieces):
+        nz = self.nz
+        whole, out, up = self.run(
+            [PairGather(nz, own, False), PairGather(nz, out_shard, True), Copies(nz, pieces, True)],
+            "1021" + "0101" + "2222" + "01" + "2222",
         )
-        return whole.reshape((self.blocks,) + own.shape), self.flat(down)
-
-    def scatter_heads(self, partial):
-        return self.run([PlaneScatter(partial)])[0]
+        return whole.reshape((self.blocks,) + own.shape), self.flat(out), up
+
+    def scatter_heads(self, partial, down):
+        return self.run([PlaneScatter(partial), DealTask(self.nz, down)], "01")
 
     def feed_forward(self, own, cotangent, gain, gate, up, down):
         task = FeedForward(self.nz, own, cotangent, gain, gate, up, down)
@@ -1447,7 +1455,7 @@
             [PairScatter(nz, given, False), PairScatter(nz, out_given, True), Sums(nz, grad, False)],
             KV_ORDER,
         )
-        return kv.astype(f32), out, sums
+        return kv, out, sums
 
     def scatter_heads_back(self, partial, sums):
         rows, shard = self.run([PlaneScatter(partial), DealBackTask(self.nz, sums)], "01")
@@ -1468,15 +1476,103 @@
         return qkv, self.flat(gate), self.flat(up), total.reshape(gains.shape)
 
 
+def project_kernel(info, normed_ref, weight_ref, q_ref, kv_ref, cos_ref, sin_ref):
+    rows, half = cos_ref.shape
+    dim = 2 * half
+    heads = q_ref.shape[0]
+    blocks = (info.shape[0] - 2) // 2
+    me, prompts = info[2 * blocks], info[2 * blocks + 1]
+    first = jnp.minimum(info[blocks + me], prompts) * rows
+    positions = (lax.broadcasted_iota(jnp.int32, (rows, half), 0) + first).astype(f32)
+    index = lax.broadcasted_iota(jnp.int32, (rows, half), 1).astype(f32)
+    angles = positions * jnp.exp(index * (-2.0 * math.log(10000.0) / dim))
+    cos_ref[...] = jnp.cos(angles)
+    sin_ref[...] = jnp.sin(angles)
+    for i in range(heads + 2):
+        columns = slice(i * dim, (i + 1) * dim)
+        linear = jnp.dot(normed_ref[...], weight_ref[:, columns], preferred_element_type=f32)
+        if i <= heads:
+            linear = rotate(linear, cos_ref[...], sin_ref[...])
+        if i < heads:
+            q_ref[i] = linear.astype(bf16)
+        else:
+            kv_ref[:, (i - heads) * dim : (i - heads + 1) * dim] = linear.astype(bf16)
+
+
+def project(info, normed, weight):
+    rows = normed.shape[0]
+    heads = weight.shape[1] // HEAD_DIM - 2
+    table = jax.ShapeDtypeStruct((rows, HEAD_DIM // 2), f32)
+    return pl.pallas_call(
+        project_kernel,
+        in_specs=[pl.BlockSpec(memory_space=pltpu.SMEM), in_vmem, in_vmem],
+        out_specs=[in_vmem] * 4,
+        out_shape=[
+            jax.ShapeDtypeStruct((heads, rows, HEAD_DIM), bf16),
+            jax.ShapeDtypeStruct((rows, 2 * HEAD_DIM), bf16),
+            table,
+            table,
+        ],
+        compiler_params=pltpu.CompilerParams(vmem_limit_bytes=24 * 2**20),
+        cost_estimate=pl.CostEstimate(
+            flops=2 * rows * weight.size, bytes_accessed=2 * weight.size, transcendentals=0
+        ),
+    )(info, normed, weight)
+
+
+def project_back_kernel(dq_ref, dkv_ref, cos_ref, sin_ref, weight_ref, lin_ref, out_ref):
+    heads, rows, dim = dq_ref.shape
+    cosine, sine = cos_ref[...], -sin_ref[...]
+    for i in range(heads):
+        lin_ref[:, i * dim : (i + 1) * dim] = rotate(dq_ref[i], cosine, sine).astype(bf16)
+    start = heads * dim
+    d_key = rotate(dkv_ref[:, :dim].astype(f32), cosine, sine)
+    lin_ref[:, start : start + dim] = d_key.astype(bf16)
+    lin_ref[:, start + dim :] = dkv_ref[:, dim:].astype(bf16)
+    depth = weight_ref.shape[0]
+    tile = 384
+
+    @pl.loop(0, depth // tile)
+    def _(i):
+        at = pl.ds(pl.multiple_of(i * tile, 128), tile)
+        out_ref[:, at] = contract(lin_ref[...], weight_ref[at, :], 1, 1).astype(bf16)
+
+
+def project_back(d_query, d_kv, cosine, sine_table, weight):
+    rows = d_kv.shape[0]
+    depth, width = weight.shape
+    return pl.pallas_call(
+        project_back_kernel,
+        in_specs=[in_vmem] * 5,
+        out_specs=[in_vmem] * 2,
+        out_shape=[
+            jax.ShapeDtypeStruct((rows, width), bf16),
+            jax.ShapeDtypeStruct((rows, depth), bf16),
+        ],
+        compiler_params=pltpu.CompilerParams(vmem_limit_bytes=24 * 2**20),
+        cost_estimate=pl.CostEstimate(
+            flops=2 * rows * weight.size, bytes_accessed=2 * weight.size, transcendentals=0
+        ),
+    )(d_query, d_kv, cosine, sine_table, weight)
+
+
 def causal_mask(rows):
     shape = (rows, rows)
     return lax.broadcasted_iota(jnp.int32, shape, 1) <= lax.broadcasted_iota(jnp.int32, shape, 0)
 
 
-def forward_kernel(kinds, q_ref, kv_ref, out_ref, exact_ref, inv_ref, acc, total):
+def kind_of(info, step):
+    blocks = pl.num_programs(0)
+    me, prompts = info[2 * blocks], info[2 * blocks + 1]
+    role = info[blocks + step]
+    reads = (info[step] == info[me]) & (role < prompts) & (role < info[blocks + me])
+    return jnp.where(step == me, 2, jnp.where(reads, 1, 0))
+
+
+def forward_kernel(info, q_ref, kv_ref, out_ref, exact_ref, inv_ref, acc, total):
     step, last = pl.program_id(0), pl.num_programs(0) - 1
     heads, rows, dim = q_ref.shape
-    kind = kinds[step]
+    kind = kind_of(info, step)
 
     @pl.when(step == 0)
     def _():
@@ -1510,19 +1606,19 @@
             out_ref[:, head * dim : (head + 1) * dim] = value.astype(bf16)
 
 
-def whole2(step, kinds):
+def whole2(step, info):
     return (0, 0)
 
 
-def whole3(step, kinds):
+def whole3(step, info):
     return (0, 0, 0)
 
 
-def by_step(step, kinds):
+def by_step(step, info):
     return (step, 0, 0)
 
 
-def attend(kinds, queries, all_kv):
+def attend(info, queries, all_kv):
     heads, rows, dim = queries.shape
     return pl.pallas_call(
         forward_kernel,
@@ -1548,19 +1644,19 @@
             jax.ShapeDtypeStruct((rows, heads * dim), f32),
             jax.ShapeDtypeStruct((heads, rows, 1), f32),
         ],
-        compiler_params=pltpu.CompilerParams(vmem_limit_bytes=40 * 2**20),
+        compiler_params=pltpu.CompilerParams(vmem_limit_bytes=24 * 2**20),
         cost_estimate=pl.CostEstimate(
             flops=3 * 4 * heads * rows * rows * dim,
             bytes_accessed=8 * rows * dim * heads,
             transcendentals=6 * heads * rows * rows,
         ),
-    )(kinds, queries, all_kv)
-
-
-def backward_kernel(kinds, q_ref, kv_ref, up_ref, exact_ref, inv_ref, dq_ref, dkv_ref):
+    )(info, queries, all_kv)
+
+
+def backward_kernel(info, q_ref, kv_ref, up_ref, exact_ref, inv_ref, dq_ref, dkv_ref):
     step = pl.program_id(0)
     heads, rows, dim = q_ref.shape
-    kind = kinds[step]
+    kind = kind_of(info, step)
 
     @pl.when(step == 0)
     def _():
@@ -1600,7 +1696,7 @@
         work(True)
 
 
-def attend_back(kinds, queries, all_kv, upstream, exact, inverse):
+def attend_back(info, queries, all_kv, upstream, exact, inverse):
     heads, rows, dim = queries.shape
     blocks = all_kv.shape[0]
     return pl.pallas_call(
@@ -1624,13 +1720,13 @@
             jax.ShapeDtypeStruct((heads, rows, dim), f32),
             jax.ShapeDtypeStruct((blocks, rows, 2 * dim), bf16),
         ],
-        compiler_params=pltpu.CompilerParams(vmem_limit_bytes=40 * 2**20),
+        compiler_params=pltpu.CompilerParams(vmem_limit_bytes=24 * 2**20),
         cost_estimate=pl.CostEstimate(
             flops=3 * 10 * heads * rows * rows * dim,
             bytes_accessed=16 * rows * dim * heads,
             transcendentals=6 * heads * rows * rows,
         ),
-    )(kinds, queries, all_kv, upstream, exact, inverse)
+    )(info, queries, all_kv, upstream, exact, inverse)
 
 
 def on_device(
@@ -1653,50 +1749,31 @@
     at = Place()
     own_rows, depth = tokens.shape
     shard_rows, units = w_gate.shape
-    regular = at.nz == 4 and shard_rows % 32 == 0 and (2 * units // at.nz) % 128 == 0
+    regular = at.nz == 4 and shard_rows % 32 == 0 and units == depth and units % 768 == 0
     comm = Kernels(at) if regular else Permutes(at)
     blocks = at.blocks
-    block_len = own_rows * lax.axis_size("heads")
-    prompt_len = blocks // 4
-    block_ids = jnp.arange(blocks, dtype=jnp.int32)
-    my_group = jnp.sum(jnp.where(block_ids == comm.block, block_group, 0))
-    my_role = jnp.sum(jnp.where(block_ids == comm.block, block_role, 0))
-    positions = jnp.where(
-        my_role < prompt_len, my_role * block_len, prompt_len * block_len
-    ) + jnp.arange(block_len, dtype=jnp.int32)
-    cosine, sine_table = rope_tables(positions)
-    prompt = (block_group == my_group) & (block_role < prompt_len) & (block_role < my_role)
-    kinds = jnp.where(block_ids == comm.block, 2, prompt.astype(jnp.int32)).astype(jnp.int32)
+    info = jnp.concatenate(
+        [block_group, block_role, jnp.stack([comm.block, blocks // 4]).astype(jnp.int32)]
+    )
 
     token_f32 = tokens.astype(f32)
     heads_width = w_query.shape[1]
-    qkv_width = heads_width + 2 * HEAD_DIM
-    attn_shard = jnp.concatenate([w_query, w_key, w_value, w_out.T], axis=1)
-    normed_one, attn_full, gate_full, up_full, down_pieces = comm.start(
-        normalize(token_f32, norm_attn_in).astype(bf16), attn_shard, w_gate, w_up, w_down.T
+    normed_one, qkv_full, gate_full, up_pieces = comm.start(
+        normalize(token_f32, norm_attn_in).astype(bf16),
+        jnp.concatenate([w_query, w_key, w_value], axis=1),
+        w_gate,
+        w_up,
     )
-    qkv_full, out_full = attn_full[:, :qkv_width], attn_full[:, qkv_width:]
-    qkv_lin = jnp.dot(normed_one, qkv_full, preferred_element_type=f32)
-    queries = jnp.stack(
-        [
-            rotate(qkv_lin[:, :HEAD_DIM], cosine, sine_table),
-            rotate(qkv_lin[:, HEAD_DIM:heads_width], cosine, sine_table),
-        ]
-    ).astype(bf16)
-    own_kv = jnp.concatenate(
-        [
-            rotate(qkv_lin[:, heads_width : heads_width + HEAD_DIM], cosine, sine_table),
-            qkv_lin[:, heads_width + HEAD_DIM :],
-        ],
-        axis=1,
-    ).astype(bf16)
-    all_kv, down_full = comm.gather_kv(own_kv, down_pieces)
-    attn_rows, attended, inverse = attend(kinds, queries, all_kv)
-    attn_proj = comm.scatter_heads(contract(attn_rows, out_full, 1, 1).astype(bf16))
+    queries, own_kv, cosine, sine_table = project(info, normed_one, qkv_full)
+    all_kv, out_full, up_full = comm.gather_kv(own_kv, w_out.T, up_pieces)
+    attn_rows, attended, inverse = attend(info, queries, all_kv)
+    attn_proj, down_pieces = comm.scatter_heads(
+        contract(attn_rows, out_full, 1, 1).astype(bf16), w_down.T
+    )
     middle = token_f32 + normalize(attn_proj, norm_attn_out)
 
     ff_proj, d_normed_two, gate_sum, up_sum, down_sum = comm.feed_forward(
-        normalize(middle, norm_ff_in).astype(bf16), cotangent, norm_ff_out, gate_full, up_full, down_full
+        normalize(middle, norm_ff_in).astype(bf16), cotangent, norm_ff_out, gate_full, up_full, down_pieces
     )
     layer_out = middle + normalize(ff_proj, norm_ff_out)
     upstream = cotangent.astype(f32)
@@ -1707,22 +1784,12 @@
     d_proj, grad_attn_out = normalize_back(attn_proj, norm_attn_out, d_middle)
     d_proj_rows = comm.gather_heads(d_proj.astype(bf16))
     d_attended = contract(d_proj_rows, out_full, 1, 0).astype(bf16)
-    d_query, d_kv_parts = attend_back(kinds, queries, all_kv, d_attended, attended, inverse)
+    d_query, d_kv_parts = attend_back(info, queries, all_kv, d_attended, attended, inverse)
     d_kv, grad_out, down_sums = comm.scatter_kv_sums(
         d_kv_parts, contract(d_proj_rows, attn_rows, 0, 0).astype(bf16), down_sum
     )
-    d_qkv_lin = jnp.concatenate(
-        [
-            rotate(d_query[0], cosine, -sine_table),
-            rotate(d_query[1], cosine, -sine_table),
-            rotate(d_kv[:, :HEAD_DIM], cosine, -sine_table),
-            d_kv[:, HEAD_DIM:],
-        ],
-        axis=1,
-    ).astype(bf16)
-    d_normed_one, grad_down = comm.scatter_heads_back(
-        contract(d_qkv_lin, qkv_full, 1, 1).astype(bf16), down_sums
-    )
+    d_qkv_lin, d_partial = project_back(d_query, d_kv, cosine, sine_table, qkv_full)
+    d_normed_one, grad_down = comm.scatter_heads_back(d_partial, down_sums)
     d_token_part, grad_attn_in = normalize_back(token_f32, norm_attn_in, d_normed_one)
     input_grad = (d_middle + d_token_part).astype(bf16)
     grad_qkv, grad_gate, grad_up, gains = comm.finish(

time: 757 us -> 713 us (0.942)
  Pallas kernels: 677 us -> 653 us
  other arithmetic: 32.1 us -> 20.9 us
    pallas_call x8, Pallas kernels: 672 us -> 637 us  [run_tasks(): pl.pallas_call(body, out_shape=[o for t in tasks for o in t.outs], in_spe...]
    pallas_call x0 -> x2, Pallas kernels: none -> 8.6 us  [the longest x1 4.63 us: project_back(): pl.pallas_call(project_back_kernel, in_specs=[in_vmem] * 5, out_specs=[in...]
    unnamed x76 -> x74, local copies, waits for them, and re-layouts: 15.2 us -> 13.9 us
where the time goes in v4:
time: 713 us; the launch traced here: 703 us
  Pallas kernels  653 us (92%)
  other arithmetic  20.9 us (3%)
  local copies, waits for them, and re-layouts  18.8 us (3%)
  matrix products  8.8 us (1%)
    pallas_call x8, Pallas kernels, run_tasks(): pl.pallas_call(body, out_shape=[o for t in tasks for o in t.outs], in_spe...  637 us

profile of v4, /device:TPU:2, one launch (start us, length us, event | category | flops | bytes accessed | tf_op | source)
XLA Modules:
  0.0 703.4 jit_solution(13150373890873490426)
XLA Ops:
  0.7 0.8 pad_add_fusion.info
  1.5 0.7 broadcast_add_fusion.3
  2.2 1.4 fusion.12
  3.6 1.4 fusion.5.refs_0_
  5.0 1.1 pad_maximum_fusion.refs_1_
  6.0 108.9 %shard_map.246 = (bf16[4,128,2304]{2,1,0:T(8,128)(2,1)S(1)}, bf16[4,2,288,1024]{3,2,1,0:T(8,128)(2,1)S(1)}, bf16[2304,2304]{1,0:T(8,128)(2,1)S(1)}, bf16[4,144,1152]{2,1,0:T(8,128)(2,1)S(1)}) custom-call(bf16[128,2304]{1,0:T(8,128)(2,1)S(1)} %fusion.5.refs_0_, bf16[288,1024]{1,0:T(8,128)(2,1)S(1)} %pad_maximum_fusion.refs_1_, ...), custom_call_target="tpu_custom_call" | custom-call | bytes 3833856 | tf_op jit(solution)/shard_map/pallas_call | solution.py:1381
  115.0 4.0 copy-done
  119.0 4.0 shard_map.247
  123.0 0.0 copy-start.16
  123.0 0.7 copy-done.16
  123.7 0.7 copy-done.18
  124.4 66.9 %shard_map.248 = (bf16[4,2,512,512]{3,2,1,0:T(8,128)(2,1)S(1)}, bf16[4,2,288,512]{3,2,1,0:T(8,128)(2,1)S(1)}, bf16[2304,2304]{1,0:T(8,128)(2,1)S(1)}) custom-call(bf16[512,512]{1,0:T(8,128)(2,1)S(1)} %get-tuple-element.50.refs_0_, bf16[288,512]{1,0:T(8,128)(2,1)S(1)} %bitcast.54, bf16[4,144,1152]{2,1,0:T(8,128)(2,1)S(1)} %get-tuple-element.51.refs_2_), custom_call_target="tpu_custom_call" | custom-call | bytes 2146304 | tf_op jit(solution)/shard_map/pallas_call | solution.py:1381
  191.3 4.0 copy-done.1
  195.3 2.9 shard_map.249
  198.2 0.0 copy-start.13
  198.2 0.0 copy-start.3
  198.3 1.4 convolution_convert_fusion.2
  199.7 0.1 copy-done.3
  199.8 30.4 %shard_map.250 = (f32[128,2304]{1,0:T(8,128)S(1)}, bf16[4,144,1152]{2,1,0:T(8,128)(2,1)S(1)}) custom-call(bf16[4,128,2304]{2,1,0:T(8,128)(2,1)S(1)} %bitcast.47, bf16[2,144,2304]{2,1,0:T(8,128)(2,1)S(1)} %bitcast.51), custom_call_target="tpu_custom_call" | custom-call | bytes 3686400 | tf_op jit(solution)/shard_map/pallas_call | solution.py:1381
  230.2 0.0 copy-start.2
  230.2 1.1 copy-done.2
  231.2 0.2 multiply_reduce_fusion.6
  231.4 0.5 copy-done.30
  231.9 0.4 copy-done.22
  232.3 0.4 multiply_reduce_fusion.5
  232.7 0.0 copy-start.29
  232.7 0.3 copy-done.31
  233.0 0.7 copy-done.20
  233.7 1.0 multiply_convert_fusion.1.refs_0_
  234.7 0.6 reshape.154.refs_2_
  235.3 179.6 %shard_map.251 = (f32[128,2304]{1,0:T(8,128)}, f32[128,2304]{1,0:T(8,128)}, bf16[2304,2304]{1,0:T(8,128)(2,1)}, bf16[2304,2304]{1,0:T(8,128)(2,1)}, bf16[2304,2304]{1,0:T(8,128)(2,1)}) custom-call(bf16[128,2304]{1,0:T(8,128)(2,1)} %multiply_convert_fusion.1.refs_0_, bf16[128,2304]{1,0:T(8,128)(2,1)} %refs_1_.1, f32[1,2304]{1,0:T(1,128)} %reshape.154.refs_2_, ...), custom_call_target="tpu_custom_call" | custom-call | bytes 23745024 | tf_op jit(solution)/shard_map/pallas_call | solution.py:1381
  414.9 2.5 multiply_reduce_fusion
  417.5 0.1 copy-done.26
  417.6 0.4 copy-done.27
  418.0 3.3 fusion.4
  421.3 0.3 multiply_convert_fusion.refs_0_
  421.6 0.8 copy-done.24
  422.4 31.2 %shard_map.252 = bf16[4,128,2304]{2,1,0:T(8,128)(2,1)S(1)} custom-call(bf16[128,2304]{1,0:T(8,128)(2,1)S(1)} %multiply_convert_fusion.refs_0_), custom_call_target="tpu_custom_call" | custom-call | bytes 589824 | tf_op jit(solution)/shard_map/pallas_call | solution.py:1381
  453.5 0.0 copy-start.12
  453.6 1.4 convolution_convert_fusion.1
  455.0 0.2 copy-done.12
  455.2 1.4 convolution_convert_fusion.3.up_ref
  456.6 4.9 shard_map.253
  461.6 0.0 copy-start.17
  461.6 0.0 copy-start.19
  461.6 64.7 %shard_map.254 = (bf16[512,512]{1,0:T(8,128)(2,1)S(1)}, bf16[288,512]{1,0:T(8,128)(2,1)S(1)}, bf16[4,144,1152]{2,1,0:T(8,128)(2,1)S(1)}) custom-call(bf16[4,2,512,512]{3,2,1,0:T(8,128)(2,1)S(1)} %bitcast.45, bf16[4,2,288,512]{3,2,1,0:T(8,128)(2,1)S(1)} %bitcast.50, bf16[4,2,2,144,2304]{4,3,2,1,0:T(8,128)(2,1)S(1)} %bitcast.43), custom_call_target="tpu_custom_call" | custom-call | bytes 17170432 | tf_op jit(solution)/shard_map/pallas_call | solution.py:1381
  526.3 4.6 shard_map.255
  530.9 0.0 copy-start.15
  531.0 0.0 copy-start.23
  531.0 33.8 %shard_map.256 = (f32[128,2304]{1,0:T(8,128)S(1)}, bf16[2,144,2304]{2,1,0:T(8,128)(2,1)S(1)}) custom-call(bf16[4,128,2304]{2,1,0:T(8,128)(2,1)S(1)} %bitcast.46, bf16[4,144,1152]{2,1,0:T(8,128)(2,1)S(1)} %get-tuple-element.70.refs_1_), custom_call_target="tpu_custom_call" | custom-call | bytes 3686400 | tf_op jit(solution)/shard_map/pallas_call | solution.py:1381
  564.8 0.4 fusion.11
  565.3 4.6 convolution_convert_fusion
  569.9 121.7 %shard_map.257 = (bf16[288,1024]{1,0:T(8,128)(2,1)S(1)}, bf16[2,144,2304]{2,1,0:T(8,128)(2,1)S(1)}, bf16[2,144,2304]{2,1,0:T(8,128)(2,1)S(1)}, f32[8,1152]{1,0:T(8,128)S(1)}) custom-call(bf16[4,2,288,1024]{3,2,1,0:T(8,128)(2,1)S(1)} %bitcast.44, bf16[4,2,2,144,2304]{4,3,2,1,0:T(8,128)(2,1)} %bitcast.65, bf16[4,2,2,144,2304]{4,3,2,1,0:T(8,128)(2,1)} %bitcast.66, ...), custom_call_target="tpu_custom_call" | custom-call | bytes 25970688 | tf_op jit(solution)/shard_map/pallas_call | solution.py:1381
  691.6 1.8 bitcast_convert_fusion
  693.4 1.8 bitcast_convert_fusion.1
  695.1 0.8 fusion.13
  696.0 0.9 slice.32
  696.9 0.6 squeeze.12
  697.5 0.6 squeeze.13
  698.1 0.6 squeeze.14
  698.7 0.6 squeeze.15
  699.3 1.8 convert_bitcast_fusion
  701.1 1.2 fusion.10
  702.3 0.9 convert_bitcast_fusion.1
  (69 shorter events, 0.3 us)
Async XLA Ops:
  0.6 4.3 copy-start.28
  2.2 3.8 copy-start.5
  3.6 2.5 copy-start.4
  115.0 4.0 copy-start
  119.0 4.0 copy-start.7
  119.0 4.0 copy-start.10
  119.0 5.4 copy-start.6
  123.0 0.7 copy-start.16
  123.7 0.7 copy-start.18
  191.3 4.0 copy-start.1
  195.3 2.9 copy-start.8
  195.3 4.4 copy-start.11
  198.2 1.5 copy-start.13
  198.2 1.5 copy-start.3
  230.2 1.1 copy-start.2
  231.2 0.7 copy-start.30
  231.2 1.1 copy-start.22
  232.3 0.7 copy-start.31
  232.7 1.0 copy-start.20
  232.7 2.0 copy-start.29
  414.9 2.6 copy-start.21
  414.9 2.7 copy-start.26
  414.9 3.0 copy-start.27
  421.3 1.1 copy-start.24
  422.4 31.2 %copy-start.14 = (bf16[512,512]{1,0:T(8,128)(2,1)S(1)}, bf16[512,512]{1,0:T(8,128)(2,1)}, u32[]{:S(2)}) copy-start(bf16[512,512]{1,0:T(8,128)(2,1)} %copy-done.13) | copy-start | bytes 1572868
  453.5 1.7 copy-start.12
  453.6 3.0 copy-start.9
  455.2 6.3 slice-start
  455.2 6.3 slice-start.1
  456.6 4.9 slice-start.2
  456.6 69.6 %slice-start.3 = ((s8[4718592]{0:T(1024)(128)(4,1)}), s8[4194304]{0:T(1024)(128)(4,1)S(1)}, s32[]{:S(2)}) async-start(s8[4718592]{0:T(1024)(128)(4,1)} %bitcast.56), calls=%async_computation.3 | async-start | bytes 8388608
  461.6 64.7 %slice-start.4 = ((s8[4718592]{0:T(1024)(128)(4,1)}), s8[524288]{0:T(1024)(128)(4,1)S(1)}, s32[]{:S(2)}) async-start(s8[4718592]{0:T(1024)(128)(4,1)} %bitcast.56), calls=%async_computation.4 | async-start | bytes 1048576
  461.6 64.7 %copy-start.17 = (f32[512,128]{1,0:T(8,128)S(1)}, f32[512,128]{1,0:T(8,128)}, u32[]{:S(2)}) copy-start(f32[512,128]{1,0:T(8,128)} %copy-done.16) | copy-start | bytes 786436
  461.6 64.7 %copy-start.19 = (f32[512,128]{1,0:T(8,128)S(1)}, f32[512,128]{1,0:T(8,128)}, u32[]{:S(2)}) copy-start(f32[512,128]{1,0:T(8,128)} %copy-done.18) | copy-start | bytes 786436
  530.9 33.8 %copy-start.15 = (bf16[512,1024]{1,0:T(8,128)(2,1)}, bf16[512,1024]{1,0:T(8,128)(2,1)S(1)}, u32[]{:S(2)}) copy-start(bf16[512,1024]{1,0:T(8,128)(2,1)S(1)} %get-tuple-element.72) | copy-start | bytes 3145732
  531.0 33.8 %copy-start.23 = (bf16[128,2304]{1,0:T(8,128)(2,1)S(1)}, bf16[128,2304]{1,0:T(8,128)(2,1)}, u32[]{:S(2)}) copy-start(bf16[128,2304]{1,0:T(8,128)(2,1)} %param.15) | copy-start | bytes 1769476
  699.3 1.8 copy-start.25

commit v5 on v4

--- a/solution.py
+++ b/solution.py
@@ -253,8 +253,10 @@
         out_full = gather_zx(self.at, out_shard).reshape(-1, out_shard.shape[1])
         return gather_zx(self.at, own).reshape((self.blocks,) + own.shape), out_full, up
 
-    def scatter_heads(self, partial, down):
-        return rows_from_block(self.at, partial), spread_weight(self.at, down)
+    def heads_forward(self, partial, tokens, gain_out, gain_in, down):
+        summed = rows_from_block(self.at, partial)
+        middle = tokens.astype(f32) + normalize(summed, gain_out)
+        return summed, normalize(middle, gain_in).astype(bf16), spread_weight(self.at, down)
 
     def gather_z(self, own):
         whole = unturn(self.at, gather_z(self.at, own))
@@ -284,8 +286,13 @@
         ]
         return [ff_proj, d_normed] + grads
 
-    def gather_heads(self, own):
-        return rows_to_block(self.at, own)
+    def heads_backward(self, d_normed, projected, tokens, cotangent, gain_out, gain_in):
+        middle = tokens.astype(f32) + normalize(projected, gain_out)
+        part, by_in = normalize_back(middle, gain_in, d_normed)
+        d_middle = cotangent.astype(f32) + part
+        d_projected, by_out = normalize_back(projected, gain_out, d_middle)
+        rows = rows_to_block(self.at, d_projected.astype(bf16))
+        return rows, d_middle, jnp.stack([by_out, by_in])
 
     def scatter_pairs(self, grad):
         rows = grad.shape[0] // self.blocks
@@ -515,30 +522,78 @@
     def __init__(self, own):
         self.ins = (own,)
         self.outs = (jax.ShapeDtypeStruct((4,) + own.shape, bf16),)
-        self.scratch = (DMA((4,)), DMA((4,)), DMA)
+        self.scratch = (DMA((6,)), DMA((4, 2)), DMA((2,)), DMA)
 
     def steps(self, p, ins, outs, scratch):
-        (own,), (whole,), (send, recv, local) = ins, outs, scratch
-        part = 2 * p.y + p.c
+        (own,), (whole,), (send, recv, on_send, local) = ins, outs, scratch
+        part, half = 2 * p.y + p.c, own.shape[0] // 2
+        same = p.c == p.x
+
+        def rows(of, i):
+            return whole.at[of, pl.ds(i * half, half)]
+
+        def piece(i):
+            return own.at[pl.ds(i * half, half)]
+
+        along = [
+            remote(piece(i), rows(part, i), send.at[2 * k + i], recv.at[part, i], target)
+            for k, target in enumerate((p.device(x=1 - p.x, c=p.x), p.device(y=1 - p.y, c=p.x)))
+            for i in range(2)
+        ]
+        home = [
+            remote(piece(i), rows(part, i), send.at[4 + i], recv.at[part, i], p.device(c=1 - p.c))
+            for i in range(2)
+        ]
         keep = pltpu.make_async_copy(own, whole.at[part], local)
-        copies = []
-        for i, (dx, dy) in enumerate([(1, 0), (0, 1), (1, 1), (0, 0)]):
-            target = p.device(x=flip(p.x, dx), y=flip(p.y, dy), c=p.x)
-            copies.append(remote(own, whole.at[part], send.at[i], recv.at[part], target))
-        *away, home = copies
-        for copy in away:
-            copy.start()
-        pl.when(p.c == p.x)(keep.start)
-        pl.when(p.c != p.x)(home.start)
+
+        def passed(k, by_x):
+            if by_x:
+                here = rows(2 * p.y + k, 0)
+                return remote(here, here, on_send.at[k], recv.at[2 * p.y + k, 0], p.device(y=1 - p.y))
+            here = rows(2 * (1 - p.y) + k, 1)
+            return remote(
+                here, here, on_send.at[k], recv.at[2 * (1 - p.y) + k, 1], p.device(x=1 - p.x)
+            )
+
+        along[0].start()
+        along[3].start()
+        along[1].start()
+        along[2].start()
+        pl.when(same)(keep.start)
+        for copy in home:
+            pl.when(jnp.logical_not(same))(copy.start)
         yield
-        for copy in away:
+        for k in range(2):
+
+            @pl.when(jnp.logical_not(same))
+            def _(k=k):
+                passed(k, True).wait_recv()
+                passed(k, True).start()
+
+            @pl.when(same)
+            def _(k=k):
+                passed(k, False).wait_recv()
+                passed(k, False).start()
+
+        yield
+        for copy in along:
             copy.wait_send()
-        pl.when(p.c == p.x)(keep.wait)
-        pl.when(p.c != p.x)(home.wait_send)
+        pl.when(same)(keep.wait)
+        for copy in home:
+            pl.when(jnp.logical_not(same))(copy.wait_send)
+        for k in range(2):
+            pl.when(jnp.logical_not(same))(passed(k, True).wait_send)
+            pl.when(same)(passed(k, False).wait_send)
         for slot in range(4):
-            came = remote(own, whole.at[slot], send.at[0], recv.at[slot], p.partner())
-            mine = (p.c == p.x) & (part == slot)
-            pl.when(jnp.logical_not(mine))(came.wait_recv)
+            y, c = slot // 2, slot % 2
+            for i in range(2):
+                came = remote(rows(slot, i), rows(slot, i), send.at[0], recv.at[slot, i], p.partner())
+                if i == 0:
+                    waited = jnp.logical_not(same) & (p.y == y)
+                else:
+                    waited = same & (p.y != y)
+                mine = same & (part == slot)
+                pl.when(jnp.logical_not(waited | mine))(came.wait_recv)
 
 
 class PlaneScatter(Task):
@@ -579,6 +634,72 @@
             at = pl.ds(pl.multiple_of(i * 16, 16), 16)
             low = came[0, at, :].astype(f32) + came[1, at, :].astype(f32)
             out[at, :] = low + (came[2, at, :].astype(f32) + came[3, at, :].astype(f32))
+
+
+class HeadsForward(PlaneScatter):
+    vmem_ins = (0, 1, 2, 3)
+    vmem_outs = (0, 1)
+
+    def __init__(self, partial, tokens, gain_out, gain_in):
+        super().__init__(partial)
+        depth = tokens.shape[1]
+        self.ins += (tokens, gain_out.reshape(1, depth), gain_in.reshape(1, depth))
+        self.outs += (jax.ShapeDtypeStruct(tokens.shape, bf16),)
+
+    def steps(self, p, ins, outs, scratch):
+        partial, tokens, gain_out, gain_in = ins
+        summed, normed = outs
+        yield from super().steps(p, (partial,), (summed,), scratch)
+
+        @pl.loop(0, normed.shape[0] // 16)
+        def _(i):
+            at = pl.ds(pl.multiple_of(i * 16, 16), 16)
+            middle = tokens[at, :].astype(f32) + normalize(summed[at, :], gain_out[...])
+            normed[at, :] = normalize(middle, gain_in[...]).astype(bf16)
+
+
+class HeadsBackward(PlaneGather):
+    vmem_ins = (0, 1, 2, 3, 4, 5)
+    vmem_outs = (0, 1, 2)
+
+    def __init__(self, d_normed, projected, tokens, cotangent, gain_out, gain_in):
+        super().__init__(tokens)
+        depth = tokens.shape[1]
+        gains = (gain_out.reshape(1, depth), gain_in.reshape(1, depth))
+        self.ins = (d_normed, projected, tokens, cotangent) + gains
+        self.outs += (
+            jax.ShapeDtypeStruct(tokens.shape, f32),
+            jax.ShapeDtypeStruct((2, 16, depth), f32),
+        )
+        self.scratch += (pltpu.VMEM(tokens.shape, bf16),)
+
+    def steps(self, p, ins, outs, scratch):
+        d_normed, projected, tokens, cotangent, gain_out, gain_in = ins
+        whole, d_middle, sums = outs
+        *sems, own = scratch
+        sums[...] = jnp.zeros_like(sums)
+
+        def back(values, gain, upstream):
+            factor = factor_of(values)
+            unit = values * factor
+            scaled = upstream * (1.0 + gain)
+            inner = jnp.mean(scaled * unit, axis=-1, keepdims=True)
+            return (scaled - unit * inner) * factor, upstream * unit
+
+        @pl.loop(0, own.shape[0] // 16)
+        def _(i):
+            at = pl.ds(pl.multiple_of(i * 16, 16), 16)
+            values = projected[at, :]
+            middle = tokens[at, :].astype(f32) + normalize(values, gain_out[...])
+            part, by_in = back(middle, gain_in[...], d_normed[at, :])
+            total = cotangent[at, :].astype(f32) + part
+            d_middle[at, :] = total
+            d_values, by_out = back(values, gain_out[...], total)
+            own[at, :] = d_values.astype(bf16)
+            sums[0] += by_out
+            sums[1] += by_in
+
+        yield from super().steps(p, (own,), (whole,), sems)
 
 
 class PairGather(Task):
@@ -820,8 +941,6 @@
 
 
 class Copies(Task):
-    vmem_outs = (0,)
-
     def __init__(self, nz, given, dealt):
         self.dealt = dealt
         if dealt:
@@ -832,10 +951,15 @@
             half, quarter = rows // 2, 2 * units // nz
             self.ins = (given.reshape(2, half, units),)
         self.outs = (jax.ShapeDtypeStruct((nz * 4 * half, 2 * quarter), bf16),)
-        self.scratch = copy_sems(nz)
+        self.scratch = (pltpu.VMEM(self.outs[0].shape, bf16), DMA, *copy_sems(nz))
 
     def steps(self, p, ins, outs, scratch):
-        return copy_steps(p, ins[0], outs[0], scratch, self.dealt)
+        full, done, *sems = scratch
+        yield from copy_steps(p, ins[0], full, sems, self.dealt)
+        store = pltpu.make_async_copy(full, outs[0], done)
+        store.start()
+        yield
+        store.wait()
 
 
 def copy_sems(nz):
@@ -1049,33 +1173,42 @@
                 across(z, x).start()
                 bring(z, x).start()
         yield
-        for z in order:
+        def over_core(z):
             for x in range(2):
                 across(z, x).wait_recv()
                 bring(z, x).wait()
                 add_rows(mine.at[z, x], mine.at[z, x], came.at[z, x])
             for which in (1, 0):
                 first(z, which).start()
-            yield
+
+        def over_first(z):
+            for which in (1, 0):
+                at = place(z, sx, sy) if which else place(z, p.x, p.y)
+                first(z, which).wait_recv()
+                add_rows(at, at, first_in.at[z, which])
+                if which:
+                    second(z).start()
+
+        def over_second(z):
+            second(z).wait_recv()
+            at = place(z, p.x, p.y)
+            if self.deal:
+                add_rows(at, at, second_in.at[z])
+                back.start(z)
+            else:
+                add_rows(out.at[z], at, second_in.at[z])
+
+        over_core(order[0])
+        yield
         for i in range(nz + 1):
+            if i + 1 < nz:
+                over_core(order[i + 1])
+                yield
             if i < nz:
-                z = order[i]
-                for which in (1, 0):
-                    at = place(z, sx, sy) if which else place(z, p.x, p.y)
-                    first(z, which).wait_recv()
-                    add_rows(at, at, first_in.at[z, which])
-                    if which:
-                        second(z).start()
+                over_first(order[i])
                 yield
             if i >= 1:
-                z = order[i - 1]
-                second(z).wait_recv()
-                at = place(z, p.x, p.y)
-                if self.deal:
-                    add_rows(at, at, second_in.at[z])
-                    back.start(z)
-                else:
-                    add_rows(out.at[z], at, second_in.at[z])
+                over_second(order[i - 1])
                 yield
         if self.deal:
             back.finish()
@@ -1346,7 +1479,7 @@
                 out[...] = total
 
 
-def run_tasks(nz, number, tasks, order=""):
+def run_tasks(nz, number, tasks, order="", every=False):
     counts = [(len(t.ins), len(t.outs), len(t.scratch)) for t in tasks]
 
     def split(refs, which):
@@ -1394,12 +1527,14 @@
         ),
     )(*[x for t in tasks for x in t.ins])
     found, _ = split(list(results), 1)
+    if every:
+        return found
     return found[0] if len(tasks) == 1 else [f[0] for f in found]
 
 
-START_ORDER = "10212" + "23" + "1222" + "12222" + "3" + "12222"
-FINISH_ORDER = "01203111" + "1112" + "03112" + "11220" + "3112" + "2220" + "32222"
-KV_ORDER = "0120" + "12" + "2" + "20" + "12222" + "01" + "222201" + "2222"
+START_ORDER = "10212" + "230" + "1222" + "12222" + "22223" + "21"
+FINISH_ORDER = "0103111101131101132220113222022322222"
+KV_ORDER = "0120" + "12" + "222" + "021" + "2222" + "01" + "222" + "01" + "2"
 
 
 class Kernels:
@@ -1431,20 +1566,26 @@
         nz = self.nz
         whole, out, up = self.run(
             [PairGather(nz, own, False), PairGather(nz, out_shard, True), Copies(nz, pieces, True)],
-            "1021" + "0101" + "2222" + "01" + "2222",
+            "1021" + "012" + "0222" + "1" + "2222" + "02" + "1",
         )
         return whole.reshape((self.blocks,) + own.shape), self.flat(out), up
 
-    def scatter_heads(self, partial, down):
-        return self.run([PlaneScatter(partial), DealTask(self.nz, down)], "01")
+    def heads_forward(self, partial, tokens, gain_out, gain_in, down):
+        task = HeadsForward(partial, tokens, gain_out, gain_in)
+        self.number += 1
+        (summed, normed), (pieces,) = run_tasks(
+            self.nz, self.number, [task, DealTask(self.nz, down)], "01", True
+        )
+        return summed, normed, pieces
 
     def feed_forward(self, own, cotangent, gain, gate, up, down):
         task = FeedForward(self.nz, own, cotangent, gain, gate, up, down)
         self.number += 1
         return run_tasks(self.nz, self.number, [task])
 
-    def gather_heads(self, own):
-        return self.flat(self.run([PlaneGather(own)])[0])
+    def heads_backward(self, *given):
+        whole, d_middle, sums = self.run([HeadsBackward(*given)])
+        return self.flat(whole), d_middle, jnp.sum(sums, axis=1)
 
     def scatter_kv_sums(self, parts, out_grad, grad):
         nz = self.nz
@@ -1767,22 +1908,21 @@
     queries, own_kv, cosine, sine_table = project(info, normed_one, qkv_full)
     all_kv, out_full, up_full = comm.gather_kv(own_kv, w_out.T, up_pieces)
     attn_rows, attended, inverse = attend(info, queries, all_kv)
-    attn_proj, down_pieces = comm.scatter_heads(
-        contract(attn_rows, out_full, 1, 1).astype(bf16), w_down.T
+    attn_proj, normed_two, down_pieces = comm.heads_forward(
+        contract(attn_rows, out_full, 1, 1).astype(bf16), tokens, norm_attn_out, norm_ff_in, w_down.T
+    )
+
+    ff_proj, d_normed_two, gate_sum, up_sum, down_sum = comm.feed_forward(
+        normed_two, cotangent, norm_ff_out, gate_full, up_full, down_pieces
     )
     middle = token_f32 + normalize(attn_proj, norm_attn_out)
-
-    ff_proj, d_normed_two, gate_sum, up_sum, down_sum = comm.feed_forward(
-        normalize(middle, norm_ff_in).astype(bf16), cotangent, norm_ff_out, gate_full, up_full, down_pieces
-    )
     layer_out = middle + normalize(ff_proj, norm_ff_out)
     upstream = cotangent.astype(f32)
     _, grad_ff_out = normalize_back(ff_proj, norm_ff_out, upstream)
 
-    d_middle_part, grad_ff_in = normalize_back(middle, norm_ff_in, d_normed_two)
-    d_middle = upstream + d_middle_part
-    d_proj, grad_attn_out = normalize_back(attn_proj, norm_attn_out, d_middle)
-    d_proj_rows = comm.gather_heads(d_proj.astype(bf16))
+    d_proj_rows, d_middle, inner_gains = comm.heads_backward(
+        d_normed_two, attn_proj, tokens, cotangent, norm_attn_out, norm_ff_in
+    )
     d_attended = contract(d_proj_rows, out_full, 1, 0).astype(bf16)
     d_query, d_kv_parts = attend_back(info, queries, all_kv, d_attended, attended, inverse)
     d_kv, grad_out, down_sums = comm.scatter_kv_sums(
@@ -1796,7 +1936,7 @@
         contract(normed_one, d_qkv_lin, 0, 0).astype(bf16),
         gate_sum,
         up_sum,
-        jnp.stack([grad_attn_in, grad_attn_out, grad_ff_in, grad_ff_out]),
+        jnp.stack([grad_attn_in, inner_gains[0], inner_gains[1], grad_ff_out]),
     )
     grad_qkv, grad_gate, grad_up = [g.astype(f32) for g in (grad_qkv, grad_gate, grad_up)]
     return (

time: 713 us -> 698 us (0.979)
    pallas_call x8, Pallas kernels: 637 us -> 627 us  [run_tasks(): pl.pallas_call(body, out_shape=[o for t in tasks for o in t.outs], in_spe...]
    unnamed x74 -> x80, local copies, waits for them, and re-layouts: 13.9 us -> 15.6 us
where the time goes in v5:
time: 698 us; the launch traced here: 691 us
  Pallas kernels  646 us (93%)
  local copies, waits for them, and re-layouts  20.5 us (3%)
  other arithmetic  14.2 us (2%)
  matrix products  8.83 us (1%)
    pallas_call x8, Pallas kernels, run_tasks(): pl.pallas_call(body, out_shape=[o for t in tasks for o in t.outs], in_spe...  627 us
    unnamed x80, local copies, waits for them, and re-layouts  15.6 us

profile of v5, /device:TPU:2, one launch (start us, length us, event | category | flops | bytes accessed | tf_op | source)
XLA Modules:
  0.0 690.7 jit_solution(9073800341806080675)
XLA Ops:
  0.6 0.0 copy-start.31
  0.7 0.8 pad_add_fusion.info
  1.5 0.7 broadcast_add_fusion.2
  2.2 1.4 fusion.11
  3.6 1.4 fusion.4.refs_0_
  4.9 0.0 copy-done.31
  5.0 1.1 pad_maximum_fusion.refs_1_
  6.0 101.5 %shard_map.246 = (bf16[4,128,2304]{2,1,0:T(8,128)(2,1)S(1)}, bf16[4,2,288,1024]{3,2,1,0:T(8,128)(2,1)S(1)}, bf16[2304,2304]{1,0:T(8,128)(2,1)S(1)}, bf16[4,144,1152]{2,1,0:T(8,128)(2,1)S(1)}) custom-call(bf16[128,2304]{1,0:T(8,128)(2,1)S(1)} %fusion.4.refs_0_, bf16[288,1024]{1,0:T(8,128)(2,1)S(1)} %pad_maximum_fusion.refs_1_, ...), custom_call_target="tpu_custom_call" | custom-call | bytes 3833856 | tf_op jit(solution)/shard_map/pallas_call | solution.py:1514
  107.5 4.1 copy-done.1
  111.6 4.0 shard_map.247
  115.6 0.0 copy-done.13
  115.6 0.0 copy-done.16
  115.6 0.0 copy-start.26
  115.6 0.7 copy-done.26
  116.3 68.0 %shard_map.248 = (bf16[4,2,512,512]{3,2,1,0:T(8,128)(2,1)S(1)}, bf16[4,2,288,512]{3,2,1,0:T(8,128)(2,1)S(1)}, bf16[2304,2304]{1,0:T(8,128)(2,1)S(1)}) custom-call(bf16[512,512]{1,0:T(8,128)(2,1)S(1)} %get-tuple-element.54.refs_0_, bf16[288,512]{1,0:T(8,128)(2,1)S(1)} %bitcast.52, bf16[4,144,1152]{2,1,0:T(8,128)(2,1)S(1)} %get-tuple-element.55.refs_2_), custom_call_target="tpu_custom_call" | custom-call | bytes 2146304 | tf_op jit(solution)/shard_map/pallas_call | solution.py:1514
  184.3 3.9 copy-done.2
  188.2 3.8 shard_map.249
  192.0 1.0 copy-done.19
  193.0 0.8 copy-done.21
  193.8 0.0 copy-start.9
  193.8 1.5 convolution_convert_fusion.2
  195.4 0.2 copy-done.9
  195.5 31.3 %shard_map.250 = (f32[128,2304]{1,0:T(8,128)S(1)}, bf16[128,2304]{1,0:T(8,128)(2,1)S(1)}, bf16[4,144,1152]{2,1,0:T(8,128)(2,1)S(1)}) custom-call(bf16[4,128,2304]{2,1,0:T(8,128)(2,1)S(1)} %bitcast.47, bf16[128,2304]{1,0:T(8,128)(2,1)S(1)} %copy-done, f32[1,2304]{1,0:T(1,128)S(1)} %reshape.144.refs_2_.refs_4_, f32[1,2304]{1,0:T(1,128)S(1)} %reshape.145.refs_3_.refs_5_, ...), custom_call_target="tpu_custom_call" | custom-call | bytes 4285440 | tf_op jit(solution)/shard_map/pallas_call | solution.py:1514
  226.8 0.0 copy-start.4
  226.8 1.1 copy-done.4
  227.9 0.8 copy-done.11
  228.7 0.6 reshape.147.refs_2_
  229.3 177.9 %shard_map.251 = (f32[128,2304]{1,0:T(8,128)}, f32[128,2304]{1,0:T(8,128)}, bf16[2304,2304]{1,0:T(8,128)(2,1)}, bf16[2304,2304]{1,0:T(8,128)(2,1)}, bf16[2304,2304]{1,0:T(8,128)(2,1)}) custom-call(bf16[128,2304]{1,0:T(8,128)(2,1)} %copy-done.11, bf16[128,2304]{1,0:T(8,128)(2,1)} %refs_3_.1, f32[1,2304]{1,0:T(1,128)} %reshape.147.refs_2_, ...), custom_call_target="tpu_custom_call" | custom-call | bytes 23745024 | tf_op jit(solution)/shard_map/pallas_call | solution.py:1514
  407.2 1.3 copy-done.10
  408.4 29.0 %shard_map.252 = (bf16[4,128,2304]{2,1,0:T(8,128)(2,1)S(1)}, f32[128,2304]{1,0:T(8,128)S(1)}, f32[2,16,2304]{2,1,0:T(8,128)S(1)}) custom-call(f32[128,2304]{1,0:T(8,128)S(1)} %copy-done.10, f32[128,2304]{1,0:T(8,128)S(1)} %get-tuple-element.59.refs_1_, bf16[128,2304]{1,0:T(8,128)(2,1)S(1)} %copy-done, bf16[128,2304]{1,0:T(8,128)(2,1)S(1)} %copy-done.3, ...), custom_call_target="tpu_custom_call" | custom-call | bytes 2368512 | tf_op jit(solution)/shard_map/pallas_call | solution.py:1514
  437.5 0.0 copy-start.18
  437.5 0.0 copy-start.22
  437.5 1.4 convolution_convert_fusion.1
  439.0 0.2 copy-done.18
  439.2 1.4 convolution_convert_fusion.3.up_ref
  440.6 0.1 copy-done.20
  440.6 0.1 copy-done.22
  440.8 6.8 shard_map.253
  447.6 0.0 slice-start.4
  447.6 0.0 copy-start.27
  447.6 0.0 copy-start.29
  447.6 65.1 %shard_map.254 = (bf16[512,512]{1,0:T(8,128)(2,1)S(1)}, bf16[288,512]{1,0:T(8,128)(2,1)S(1)}, bf16[4,144,1152]{2,1,0:T(8,128)(2,1)S(1)}) custom-call(bf16[4,2,512,512]{3,2,1,0:T(8,128)(2,1)S(1)} %bitcast.45, bf16[4,2,288,512]{3,2,1,0:T(8,128)(2,1)S(1)} %bitcast.48, bf16[4,2,2,144,2304]{4,3,2,1,0:T(8,128)(2,1)S(1)} %bitcast.43), custom_call_target="tpu_custom_call" | custom-call | bytes 17170432 | tf_op jit(solution)/shard_map/pallas_call | solution.py:1514
  512.8 4.6 shard_map.255
  517.4 0.0 copy-start.25
  517.4 31.2 %shard_map.256 = (f32[128,2304]{1,0:T(8,128)S(1)}, bf16[2,144,2304]{2,1,0:T(8,128)(2,1)S(1)}) custom-call(bf16[4,128,2304]{2,1,0:T(8,128)(2,1)S(1)} %bitcast.46, bf16[4,144,1152]{2,1,0:T(8,128)(2,1)S(1)} %get-tuple-element.77.refs_1_), custom_call_target="tpu_custom_call" | custom-call | bytes 3686400 | tf_op jit(solution)/shard_map/pallas_call | solution.py:1514
  548.6 0.0 copy-start.5
  548.7 0.4 fusion.10
  549.1 1.3 copy-done.30
  550.4 0.2 multiply_reduce_fusion.1
  550.6 0.2 multiply_reduce_fusion.2
  550.8 1.9 multiply_reduce_fusion
  552.6 0.1 reduce_sum.76
  552.8 4.6 convolution_convert_fusion
  557.4 122.8 %shard_map.257 = (bf16[288,1024]{1,0:T(8,128)(2,1)S(1)}, bf16[2,144,2304]{2,1,0:T(8,128)(2,1)S(1)}, bf16[2,144,2304]{2,1,0:T(8,128)(2,1)S(1)}, f32[8,1152]{1,0:T(8,128)S(1)}) custom-call(bf16[4,2,288,1024]{3,2,1,0:T(8,128)(2,1)S(1)} %bitcast.44, bf16[4,2,2,144,2304]{4,3,2,1,0:T(8,128)(2,1)} %bitcast.65, bf16[4,2,2,144,2304]{4,3,2,1,0:T(8,128)(2,1)} %bitcast.66, ...), custom_call_target="tpu_custom_call" | custom-call | bytes 25970688 | tf_op jit(solution)/shard_map/pallas_call | solution.py:1514
  680.1 1.8 bitcast_convert_fusion
  681.9 1.8 bitcast_convert_fusion.1
  683.7 0.8 fusion.14
  684.5 0.9 slice.35
  685.4 0.6 squeeze.12
  686.0 0.6 squeeze.13
  686.6 0.6 squeeze.14
  687.2 0.6 squeeze.15
  687.8 1.8 convert_bitcast_fusion
  689.6 0.9 convert_bitcast_fusion.1
  (66 shorter events, 0.2 us)
Async XLA Ops:
  0.6 4.3 copy-start.31
  2.2 3.8 copy-start.8
  3.6 2.5 copy-start.7
  107.5 4.1 copy-start.1
  111.6 4.0 copy-start.13
  111.6 4.0 copy-start.16
  111.6 4.7 copy-start.12
  115.6 0.7 copy-start.26
  116.3 71.9 %copy-start.28 = (f32[512,128]{1,0:T(8,128)}, f32[512,128]{1,0:T(8,128)S(1)}, u32[]{:S(2)}) copy-start(f32[512,128]{1,0:T(8,128)S(1)} %get-tuple-element.75.sin_ref) | copy-start | bytes 786436
  184.3 3.9 copy-start.2
  188.2 3.8 copy-start.14
  188.2 7.1 %copy-start.17 = (bf16[4,2,288,512]{3,2,1,0:T(8,128)(2,1)}, bf16[4,2,288,512]{3,2,1,0:T(8,128)(2,1)S(1)}, u32[]{:S(2)}) copy-start(bf16[4,2,288,512]{3,2,1,0:T(8,128)(2,1)S(1)} %get-tuple-element.58) | copy-start | bytes 7077892
  192.0 1.0 copy-start.19
  193.0 0.8 copy-start.21
  193.8 1.5 copy-start.23
  193.8 1.5 copy-start.32
  193.8 1.5 copy-start.34
  193.8 1.6 copy-start
  193.8 1.7 copy-start.9
  195.5 33.2 %copy-start.33 = (f32[2304]{0:T(1024)S(1)}, f32[2304]{0:T(1024)}, u32[]{:S(2)}) copy-start(f32[2304]{0:T(1024)} %param.27) | copy-start | bytes 27652
  226.8 1.1 copy-start.4
  227.9 0.8 copy-start.11
  229.3 177.9 %copy-start.3 = (bf16[128,2304]{1,0:T(8,128)(2,1)S(1)}, bf16[128,2304]{1,0:T(8,128)(2,1)}, u32[]{:S(2)}) copy-start(bf16[128,2304]{1,0:T(8,128)(2,1)} %refs_3_.1) | copy-start | bytes 1769476
  407.2 1.3 copy-start.10
  408.4 29.0 %copy-start.24 = (bf16[512,512]{1,0:T(8,128)(2,1)S(1)}, bf16[512,512]{1,0:T(8,128)(2,1)}, u32[]{:S(2)}) copy-start(bf16[512,512]{1,0:T(8,128)(2,1)} %copy-done.23) | copy-start | bytes 1572868
  437.5 1.7 copy-start.18
  437.5 3.0 copy-start.15
  437.5 3.1 copy-start.20
  437.5 3.2 copy-start.22
  439.2 8.4 %slice-start = ((s8[10616832]{0:T(1024)(128)(4,1)}), s8[4194304]{0:T(1024)(128)(4,1)S(1)}, s32[]{:S(2)}) async-start(s8[10616832]{0:T(1024)(128)(4,1)} %bitcast.41), calls=%async_computation | async-start | bytes 8388608
  439.2 8.4 %slice-start.1 = ((s8[10616832]{0:T(1024)(128)(4,1)}), s8[4194304]{0:T(1024)(128)(4,1)S(1)}, s32[]{:S(2)}) async-start(s8[10616832]{0:T(1024)(128)(4,1)} %bitcast.41), calls=%async_computation.1 | async-start | bytes 8388608
  440.7 6.8 slice-start.2
  440.7 72.0 %slice-start.3 = ((s8[4718592]{0:T(1024)(128)(4,1)}), s8[4194304]{0:T(1024)(128)(4,1)S(1)}, s32[]{:S(2)}) async-start(s8[4718592]{0:T(1024)(128)(4,1)} %bitcast.54), calls=%async_computation.3 | async-start | bytes 8388608
  447.6 65.1 %slice-start.4 = ((s8[4718592]{0:T(1024)(128)(4,1)}), s8[524288]{0:T(1024)(128)(4,1)S(1)}, s32[]{:S(2)}) async-start(s8[4718592]{0:T(1024)(128)(4,1)} %bitcast.54), calls=%async_computation.4 | async-start | bytes 1048576
  447.6 65.1 %copy-start.27 = (f32[512,128]{1,0:T(8,128)S(1)}, f32[512,128]{1,0:T(8,128)}, u32[]{:S(2)}) copy-start(f32[512,128]{1,0:T(8,128)} %copy-done.26) | copy-start | bytes 786436
  447.6 65.1 %copy-start.29 = (f32[512,128]{1,0:T(8,128)S(1)}, f32[512,128]{1,0:T(8,128)}, u32[]{:S(2)}) copy-start(f32[512,128]{1,0:T(8,128)} %copy-done.28) | copy-start | bytes 786436
  517.4 31.2 %copy-start.25 = (bf16[512,1024]{1,0:T(8,128)(2,1)}, bf16[512,1024]{1,0:T(8,128)(2,1)S(1)}, u32[]{:S(2)}) copy-start(bf16[512,1024]{1,0:T(8,128)(2,1)S(1)} %get-tuple-element.79) | copy-start | bytes 3145732
  548.6 1.9 copy-start.5
  548.7 1.8 copy-start.30
  683.7 4.2 copy-start.6

commit v6 on v5

--- a/solution.py
+++ b/solution.py
@@ -1532,9 +1532,9 @@
     return found[0] if len(tasks) == 1 else [f[0] for f in found]
 
 
-START_ORDER = "10212" + "230" + "1222" + "12222" + "22223" + "21"
+START_ORDER = "10222102221222213222222131"
 FINISH_ORDER = "0103111101131101132220113222022322222"
-KV_ORDER = "0120" + "12" + "222" + "021" + "2222" + "01" + "222" + "01" + "2"
+KV_ORDER = "0120122021220221222011222"
 
 
 class Kernels:

time: 698 us -> 689 us (0.987)
  Pallas kernels: 646 us -> 638 us
    pallas_call x8, Pallas kernels: 627 us -> 618 us  [run_tasks(): pl.pallas_call(body, out_shape=[o for t in tasks for o in t.outs], in_spe...]
where the time goes in v6:
time: 689 us; the launch traced here: 683 us
  Pallas kernels  638 us (93%)
  local copies, waits for them, and re-layouts  20.5 us (3%)
  other arithmetic  14.2 us (2%)
  matrix products  8.84 us (1%)
    pallas_call x8, Pallas kernels, run_tasks(): pl.pallas_call(body, out_shape=[o for t in tasks for o in t.outs], in_spe...  618 us
    unnamed x80, local copies, waits for them, and re-layouts  15.6 us

profile of v6, /device:TPU:2, one launch (start us, length us, event | category | flops | bytes accessed | tf_op | source)
XLA Modules:
  0.0 682.5 jit_solution(11602036325193585249)
XLA Ops:
  0.6 0.0 copy-start.31
  0.7 0.8 pad_add_fusion.info
  1.5 0.7 broadcast_add_fusion.2
  2.2 1.4 fusion.11
  3.6 1.4 fusion.4.refs_0_
  4.9 0.0 copy-done.31
  5.0 1.1 pad_maximum_fusion.refs_1_
  6.0 92.4 %shard_map.246 = (bf16[4,128,2304]{2,1,0:T(8,128)(2,1)S(1)}, bf16[4,2,288,1024]{3,2,1,0:T(8,128)(2,1)S(1)}, bf16[2304,2304]{1,0:T(8,128)(2,1)S(1)}, bf16[4,144,1152]{2,1,0:T(8,128)(2,1)S(1)}) custom-call(bf16[128,2304]{1,0:T(8,128)(2,1)S(1)} %fusion.4.refs_0_, bf16[288,1024]{1,0:T(8,128)(2,1)S(1)} %pad_maximum_fusion.refs_1_, ...), custom_call_target="tpu_custom_call" | custom-call | bytes 3833856 | tf_op jit(solution)/shard_map/pallas_call | solution.py:1514
  98.5 4.1 copy-done.1
  102.6 4.0 shard_map.247
  106.5 0.0 copy-done.13
  106.5 0.0 copy-done.16
  106.5 0.0 copy-start.26
  106.6 0.7 copy-done.26
  107.3 69.0 %shard_map.248 = (bf16[4,2,512,512]{3,2,1,0:T(8,128)(2,1)S(1)}, bf16[4,2,288,512]{3,2,1,0:T(8,128)(2,1)S(1)}, bf16[2304,2304]{1,0:T(8,128)(2,1)S(1)}) custom-call(bf16[512,512]{1,0:T(8,128)(2,1)S(1)} %get-tuple-element.54.refs_0_, bf16[288,512]{1,0:T(8,128)(2,1)S(1)} %bitcast.52, bf16[4,144,1152]{2,1,0:T(8,128)(2,1)S(1)} %get-tuple-element.55.refs_2_), custom_call_target="tpu_custom_call" | custom-call | bytes 2146304 | tf_op jit(solution)/shard_map/pallas_call | solution.py:1514
  176.3 3.9 copy-done.2
  180.2 3.8 shard_map.249
  184.0 1.0 copy-done.19
  185.0 0.8 copy-done.21
  185.8 0.0 copy-start.9
  185.9 1.5 convolution_convert_fusion.2
  187.4 0.2 copy-done.9
  187.6 31.0 %shard_map.250 = (f32[128,2304]{1,0:T(8,128)S(1)}, bf16[128,2304]{1,0:T(8,128)(2,1)S(1)}, bf16[4,144,1152]{2,1,0:T(8,128)(2,1)S(1)}) custom-call(bf16[4,128,2304]{2,1,0:T(8,128)(2,1)S(1)} %bitcast.47, bf16[128,2304]{1,0:T(8,128)(2,1)S(1)} %copy-done, f32[1,2304]{1,0:T(1,128)S(1)} %reshape.144.refs_2_.refs_4_, f32[1,2304]{1,0:T(1,128)S(1)} %reshape.145.refs_3_.refs_5_, ...), custom_call_target="tpu_custom_call" | custom-call | bytes 4285440 | tf_op jit(solution)/shard_map/pallas_call | solution.py:1514
  218.6 0.0 copy-start.4
  218.6 1.1 copy-done.4
  219.6 0.8 copy-done.11
  220.4 0.6 reshape.147.refs_2_
  221.0 179.1 %shard_map.251 = (f32[128,2304]{1,0:T(8,128)}, f32[128,2304]{1,0:T(8,128)}, bf16[2304,2304]{1,0:T(8,128)(2,1)}, bf16[2304,2304]{1,0:T(8,128)(2,1)}, bf16[2304,2304]{1,0:T(8,128)(2,1)}) custom-call(bf16[128,2304]{1,0:T(8,128)(2,1)} %copy-done.11, bf16[128,2304]{1,0:T(8,128)(2,1)} %refs_3_.1, f32[1,2304]{1,0:T(1,128)} %reshape.147.refs_2_, ...), custom_call_target="tpu_custom_call" | custom-call | bytes 23745024 | tf_op jit(solution)/shard_map/pallas_call | solution.py:1514
  400.2 1.3 copy-done.10
  401.5 27.3 %shard_map.252 = (bf16[4,128,2304]{2,1,0:T(8,128)(2,1)S(1)}, f32[128,2304]{1,0:T(8,128)S(1)}, f32[2,16,2304]{2,1,0:T(8,128)S(1)}) custom-call(f32[128,2304]{1,0:T(8,128)S(1)} %copy-done.10, f32[128,2304]{1,0:T(8,128)S(1)} %get-tuple-element.59.refs_1_, bf16[128,2304]{1,0:T(8,128)(2,1)S(1)} %copy-done, bf16[128,2304]{1,0:T(8,128)(2,1)S(1)} %copy-done.3, ...), custom_call_target="tpu_custom_call" | custom-call | bytes 2368512 | tf_op jit(solution)/shard_map/pallas_call | solution.py:1514
  428.8 0.0 copy-start.18
  428.8 0.0 copy-start.22
  428.8 1.4 convolution_convert_fusion.1
  430.3 0.2 copy-done.18
  430.5 1.4 convolution_convert_fusion.3.up_ref
  431.9 0.1 copy-done.20
  431.9 0.1 copy-done.22
  432.0 6.8 shard_map.253
  438.9 0.0 slice-start.4
  438.9 0.0 copy-start.27
  438.9 0.0 copy-start.29
  438.9 62.4 %shard_map.254 = (bf16[512,512]{1,0:T(8,128)(2,1)S(1)}, bf16[288,512]{1,0:T(8,128)(2,1)S(1)}, bf16[4,144,1152]{2,1,0:T(8,128)(2,1)S(1)}) custom-call(bf16[4,2,512,512]{3,2,1,0:T(8,128)(2,1)S(1)} %bitcast.45, bf16[4,2,288,512]{3,2,1,0:T(8,128)(2,1)S(1)} %bitcast.48, bf16[4,2,2,144,2304]{4,3,2,1,0:T(8,128)(2,1)S(1)} %bitcast.43), custom_call_target="tpu_custom_call" | custom-call | bytes 17170432 | tf_op jit(solution)/shard_map/pallas_call | solution.py:1514
  501.3 4.6 shard_map.255
  506.0 0.0 copy-start.25
  506.0 33.8 %shard_map.256 = (f32[128,2304]{1,0:T(8,128)S(1)}, bf16[2,144,2304]{2,1,0:T(8,128)(2,1)S(1)}) custom-call(bf16[4,128,2304]{2,1,0:T(8,128)(2,1)S(1)} %bitcast.46, bf16[4,144,1152]{2,1,0:T(8,128)(2,1)S(1)} %get-tuple-element.77.refs_1_), custom_call_target="tpu_custom_call" | custom-call | bytes 3686400 | tf_op jit(solution)/shard_map/pallas_call | solution.py:1514
  539.8 0.0 copy-start.5
  539.8 0.4 fusion.10
  540.2 1.3 copy-done.30
  541.5 0.2 multiply_reduce_fusion.1
  541.7 0.2 multiply_reduce_fusion.2
  541.9 1.9 multiply_reduce_fusion
  543.8 0.1 reduce_sum.76
  543.9 4.6 convolution_convert_fusion
  548.5 123.5 %shard_map.257 = (bf16[288,1024]{1,0:T(8,128)(2,1)S(1)}, bf16[2,144,2304]{2,1,0:T(8,128)(2,1)S(1)}, bf16[2,144,2304]{2,1,0:T(8,128)(2,1)S(1)}, f32[8,1152]{1,0:T(8,128)S(1)}) custom-call(bf16[4,2,288,1024]{3,2,1,0:T(8,128)(2,1)S(1)} %bitcast.44, bf16[4,2,2,144,2304]{4,3,2,1,0:T(8,128)(2,1)} %bitcast.65, bf16[4,2,2,144,2304]{4,3,2,1,0:T(8,128)(2,1)} %bitcast.66, ...), custom_call_target="tpu_custom_call" | custom-call | bytes 25970688 | tf_op jit(solution)/shard_map/pallas_call | solution.py:1514
  672.0 1.8 bitcast_convert_fusion
  673.7 1.8 bitcast_convert_fusion.1
  675.5 0.8 fusion.14
  676.3 0.9 slice.35
  677.2 0.6 squeeze.12
  677.8 0.6 squeeze.13
  678.5 0.6 squeeze.14
  679.1 0.6 squeeze.15
  679.7 1.8 convert_bitcast_fusion
  681.4 0.9 convert_bitcast_fusion.1
  (66 shorter events, 0.2 us)
Async XLA Ops:
  0.6 4.3 copy-start.31
  2.2 3.8 copy-start.8
  3.6 2.5 copy-start.7
  98.5 4.1 copy-start.1
  102.6 4.0 copy-start.13
  102.6 4.0 copy-start.16
  102.6 4.7 copy-start.12
  106.5 0.7 copy-start.26
  107.3 73.0 %copy-start.28 = (f32[512,128]{1,0:T(8,128)}, f32[512,128]{1,0:T(8,128)S(1)}, u32[]{:S(2)}) copy-start(f32[512,128]{1,0:T(8,128)S(1)} %get-tuple-element.75.sin_ref) | copy-start | bytes 786436
  176.3 3.9 copy-start.2
  180.2 3.8 copy-start.14
  180.2 7.1 %copy-start.17 = (bf16[4,2,288,512]{3,2,1,0:T(8,128)(2,1)}, bf16[4,2,288,512]{3,2,1,0:T(8,128)(2,1)S(1)}, u32[]{:S(2)}) copy-start(bf16[4,2,288,512]{3,2,1,0:T(8,128)(2,1)S(1)} %get-tuple-element.58) | copy-start | bytes 7077892
  184.0 1.0 copy-start.19
  185.0 0.8 copy-start.21
  185.8 1.5 copy-start.23
  185.8 1.5 copy-start.32
  185.8 1.5 copy-start.34
  185.8 1.6 copy-start
  185.8 1.7 copy-start.9
  187.6 32.9 %copy-start.33 = (f32[2304]{0:T(1024)S(1)}, f32[2304]{0:T(1024)}, u32[]{:S(2)}) copy-start(f32[2304]{0:T(1024)} %param.27) | copy-start | bytes 27652
  218.6 1.1 copy-start.4
  219.6 0.8 copy-start.11
  221.0 179.1 %copy-start.3 = (bf16[128,2304]{1,0:T(8,128)(2,1)S(1)}, bf16[128,2304]{1,0:T(8,128)(2,1)}, u32[]{:S(2)}) copy-start(bf16[128,2304]{1,0:T(8,128)(2,1)} %refs_3_.1) | copy-start | bytes 1769476
  400.2 1.3 copy-start.10
  401.5 27.3 %copy-start.24 = (bf16[512,512]{1,0:T(8,128)(2,1)S(1)}, bf16[512,512]{1,0:T(8,128)(2,1)}, u32[]{:S(2)}) copy-start(bf16[512,512]{1,0:T(8,128)(2,1)} %copy-done.23) | copy-start | bytes 1572868
  428.8 1.7 copy-start.18
  428.8 3.0 copy-start.15
  428.8 3.1 copy-start.20
  428.8 3.2 copy-start.22
  430.5 8.4 %slice-start = ((s8[10616832]{0:T(1024)(128)(4,1)}), s8[4194304]{0:T(1024)(128)(4,1)S(1)}, s32[]{:S(2)}) async-start(s8[10616832]{0:T(1024)(128)(4,1)} %bitcast.41), calls=%async_computation | async-start | bytes 8388608
  430.5 8.4 %slice-start.1 = ((s8[10616832]{0:T(1024)(128)(4,1)}), s8[4194304]{0:T(1024)(128)(4,1)S(1)}, s32[]{:S(2)}) async-start(s8[10616832]{0:T(1024)(128)(4,1)} %bitcast.41), calls=%async_computation.1 | async-start | bytes 8388608
  432.0 6.8 %slice-start.2 = ((s8[10616832]{0:T(1024)(128)(4,1)}), s8[2228224]{0:T(1024)(128)(4,1)S(1)}, s32[]{:S(2)}) async-start(s8[10616832]{0:T(1024)(128)(4,1)} %bitcast.41), calls=%async_computation.2 | async-start | bytes 4456448
  432.0 69.3 %slice-start.3 = ((s8[4718592]{0:T(1024)(128)(4,1)}), s8[4194304]{0:T(1024)(128)(4,1)S(1)}, s32[]{:S(2)}) async-start(s8[4718592]{0:T(1024)(128)(4,1)} %bitcast.54), calls=%async_computation.3 | async-start | bytes 8388608
  438.9 62.4 %slice-start.4 = ((s8[4718592]{0:T(1024)(128)(4,1)}), s8[524288]{0:T(1024)(128)(4,1)S(1)}, s32[]{:S(2)}) async-start(s8[4718592]{0:T(1024)(128)(4,1)} %bitcast.54), calls=%async_computation.4 | async-start | bytes 1048576
  438.9 62.4 %copy-start.27 = (f32[512,128]{1,0:T(8,128)S(1)}, f32[512,128]{1,0:T(8,128)}, u32[]{:S(2)}) copy-start(f32[512,128]{1,0:T(8,128)} %copy-done.26) | copy-start | bytes 786436
  438.9 62.4 %copy-start.29 = (f32[512,128]{1,0:T(8,128)S(1)}, f32[512,128]{1,0:T(8,128)}, u32[]{:S(2)}) copy-start(f32[512,128]{1,0:T(8,128)} %copy-done.28) | copy-start | bytes 786436
  506.0 33.8 %copy-start.25 = (bf16[512,1024]{1,0:T(8,128)(2,1)}, bf16[512,1024]{1,0:T(8,128)(2,1)S(1)}, u32[]{:S(2)}) copy-start(bf16[512,1024]{1,0:T(8,128)(2,1)S(1)} %get-tuple-element.79) | copy-start | bytes 3145732
  539.8 1.9 copy-start.5
  539.8 1.8 copy-start.30
  675.5 4.2 copy-start.6

commit v7 on v6

--- a/solution.py
+++ b/solution.py
@@ -1360,31 +1360,32 @@
         next(copies)
         for load in loads:
             load.start()
+        two.start(1)
         one.arrive(1)
         one.start(2)
-        two.start(1)
+        two.arrive(1)
         one.arrive(2)
+        two.start(2)
         one.start(3)
         for _ in range(nz):
             next(copies)
         one.arrive(3)
-        two.arrive(1)
-        two.start(2)
         for load in loads:
             load.wait()
         hide(0, 0, 1)
         two.arrive(2)
+        hide(0, 1, 2)
         two.start(3)
-        hide(0, 1, 3)
         two.arrive(3)
-        hide(1, 0, 1)
+        hide(0, 2, 3)
         for _ in copies:
             pass
         project(0)
         sum_one.start(1)
-        hide(1, 1, 3)
+        hide(1, 0, 2)
         sum_one.arrive(1)
         sum_one.start(2)
+        hide(1, 2, 3)
         project(1)
         sum_two.start(1)
         sum_one.arrive(2)
@@ -1400,10 +1401,10 @@
         one_back.arrive(1)
         one_back.start(2)
         sum_two.arrive(3)
+        one_back.arrive(2)
+        one_back.start(3)
         sum_two.total(ff_out.at[pl.ds(part, part)])
         turn_back(1)
-        one_back.arrive(2)
-        one_back.start(3)
         two_back.start(1)
         one_back.arrive(3)
         hide_back(0, 0, 3)
@@ -1411,9 +1412,9 @@
         two_back.start(2)
         sum_one.finish()
         project_back(0)
-        sum_one_back.start(1)
         two_back.arrive(2)
         two_back.start(3)
+        sum_one_back.start(1)
         two_back.arrive(3)
         hide_back(1, 0, 3)
         sum_one_back.arrive(1)

time: 689 us -> 686 us (level)
  no operation moved by 1% of the time
where the time goes in v7:
time: 686 us; the launch traced here: 679 us
  Pallas kernels  634 us (92%)
  local copies, waits for them, and re-layouts  20.5 us (3%)
  other arithmetic  14.2 us (2%)
  matrix products  8.83 us (1%)
    pallas_call x8, Pallas kernels, run_tasks(): pl.pallas_call(body, out_shape=[o for t in tasks for o in t.outs], in_spe...  615 us
    unnamed x80, local copies, waits for them, and re-layouts  15.6 us

profile of v7, /device:TPU:2, one launch (start us, length us, event | category | flops | bytes accessed | tf_op | source)
XLA Modules:
  0.0 679.4 jit_solution(1649242039914602043)
XLA Ops:
  0.6 0.0 copy-start.31
  0.7 0.8 pad_add_fusion.info
  1.5 0.7 broadcast_add_fusion.2
  2.2 1.4 fusion.11
  3.6 1.4 fusion.4.refs_0_
  4.9 0.0 copy-done.31
  5.0 1.1 pad_maximum_fusion.refs_1_
  6.0 92.4 %shard_map.246 = (bf16[4,128,2304]{2,1,0:T(8,128)(2,1)S(1)}, bf16[4,2,288,1024]{3,2,1,0:T(8,128)(2,1)S(1)}, bf16[2304,2304]{1,0:T(8,128)(2,1)S(1)}, bf16[4,144,1152]{2,1,0:T(8,128)(2,1)S(1)}) custom-call(bf16[128,2304]{1,0:T(8,128)(2,1)S(1)} %fusion.4.refs_0_, bf16[288,1024]{1,0:T(8,128)(2,1)S(1)} %pad_maximum_fusion.refs_1_, ...), custom_call_target="tpu_custom_call" | custom-call | bytes 3833856 | tf_op jit(solution)/shard_map/pallas_call | solution.py:1515
  98.5 4.1 copy-done.1
  102.6 4.0 shard_map.247
  106.6 0.0 copy-start.26
  106.6 0.7 copy-done.26
  107.3 69.0 %shard_map.248 = (bf16[4,2,512,512]{3,2,1,0:T(8,128)(2,1)S(1)}, bf16[4,2,288,512]{3,2,1,0:T(8,128)(2,1)S(1)}, bf16[2304,2304]{1,0:T(8,128)(2,1)S(1)}) custom-call(bf16[512,512]{1,0:T(8,128)(2,1)S(1)} %get-tuple-element.54.refs_0_, bf16[288,512]{1,0:T(8,128)(2,1)S(1)} %bitcast.52, bf16[4,144,1152]{2,1,0:T(8,128)(2,1)S(1)} %get-tuple-element.55.refs_2_), custom_call_target="tpu_custom_call" | custom-call | bytes 2146304 | tf_op jit(solution)/shard_map/pallas_call | solution.py:1515
  176.3 3.9 copy-done.2
  180.2 3.8 shard_map.249
  184.0 1.0 copy-done.19
  185.0 0.8 copy-done.21
  185.8 0.0 copy-start.9
  185.9 1.5 convolution_convert_fusion.2
  187.4 0.0 copy-done
  187.4 0.2 copy-done.9
  187.6 31.2 %shard_map.250 = (f32[128,2304]{1,0:T(8,128)S(1)}, bf16[128,2304]{1,0:T(8,128)(2,1)S(1)}, bf16[4,144,1152]{2,1,0:T(8,128)(2,1)S(1)}) custom-call(bf16[4,128,2304]{2,1,0:T(8,128)(2,1)S(1)} %bitcast.47, bf16[128,2304]{1,0:T(8,128)(2,1)S(1)} %copy-done, f32[1,2304]{1,0:T(1,128)S(1)} %reshape.144.refs_2_.refs_4_, f32[1,2304]{1,0:T(1,128)S(1)} %reshape.145.refs_3_.refs_5_, ...), custom_call_target="tpu_custom_call" | custom-call | bytes 4285440 | tf_op jit(solution)/shard_map/pallas_call | solution.py:1515
  218.8 0.0 copy-start.4
  218.8 1.1 copy-done.4
  219.8 0.8 copy-done.11
  220.7 0.6 reshape.147.refs_2_
  221.3 175.7 %shard_map.251 = (f32[128,2304]{1,0:T(8,128)}, f32[128,2304]{1,0:T(8,128)}, bf16[2304,2304]{1,0:T(8,128)(2,1)}, bf16[2304,2304]{1,0:T(8,128)(2,1)}, bf16[2304,2304]{1,0:T(8,128)(2,1)}) custom-call(bf16[128,2304]{1,0:T(8,128)(2,1)} %copy-done.11, bf16[128,2304]{1,0:T(8,128)(2,1)} %refs_3_.1, f32[1,2304]{1,0:T(1,128)} %reshape.147.refs_2_, ...), custom_call_target="tpu_custom_call" | custom-call | bytes 23745024 | tf_op jit(solution)/shard_map/pallas_call | solution.py:1515
  397.0 0.0 copy-done.3
  397.0 1.3 copy-done.10
  398.3 28.2 %shard_map.252 = (bf16[4,128,2304]{2,1,0:T(8,128)(2,1)S(1)}, f32[128,2304]{1,0:T(8,128)S(1)}, f32[2,16,2304]{2,1,0:T(8,128)S(1)}) custom-call(f32[128,2304]{1,0:T(8,128)S(1)} %copy-done.10, f32[128,2304]{1,0:T(8,128)S(1)} %get-tuple-element.59.refs_1_, bf16[128,2304]{1,0:T(8,128)(2,1)S(1)} %copy-done, bf16[128,2304]{1,0:T(8,128)(2,1)S(1)} %copy-done.3, ...), custom_call_target="tpu_custom_call" | custom-call | bytes 2368512 | tf_op jit(solution)/shard_map/pallas_call | solution.py:1515
  426.5 0.0 copy-start.18
  426.6 0.0 copy-start.22
  426.6 1.4 convolution_convert_fusion.1
  428.0 0.2 copy-done.18
  428.2 1.4 convolution_convert_fusion.3.up_ref
  429.6 0.1 copy-done.20
  429.7 0.1 copy-done.22
  429.8 6.8 %shard_map.253 = (f32[2,512,256]{2,1,0:T(8,128)S(1)}, bf16[8,512,512]{2,1,0:T(8,128)(2,1)S(1)}) custom-call(s32[18]{0:T(128)S(1)} %pad_add_fusion.info, bf16[2,512,256]{2,1,0:T(8,128)(2,1)S(1)} %get-tuple-element.53.q_ref, bf16[8,512,512]{2,1,0:T(8,128)(2,1)S(1)} %bitcast.58, bf16[512,512]{1,0:T(8,128)(2,1)S(1)} %convolution_convert_fusion.3.up_ref, ...), custom_call_target="tpu_custom_call" | custom-call | flops 4026531840 | bytes 4194304 | tf_op jit(solution)/shard_map/pallas_call | solution.py:1844
  436.6 0.0 slice-start.4
  436.7 0.0 copy-start.27
  436.7 0.0 copy-start.29
  436.7 61.7 %shard_map.254 = (bf16[512,512]{1,0:T(8,128)(2,1)S(1)}, bf16[288,512]{1,0:T(8,128)(2,1)S(1)}, bf16[4,144,1152]{2,1,0:T(8,128)(2,1)S(1)}) custom-call(bf16[4,2,512,512]{3,2,1,0:T(8,128)(2,1)S(1)} %bitcast.45, bf16[4,2,288,512]{3,2,1,0:T(8,128)(2,1)S(1)} %bitcast.48, bf16[4,2,2,144,2304]{4,3,2,1,0:T(8,128)(2,1)S(1)} %bitcast.43), custom_call_target="tpu_custom_call" | custom-call | bytes 17170432 | tf_op jit(solution)/shard_map/pallas_call | solution.py:1515
  498.4 4.6 shard_map.255
  503.1 0.0 copy-start.25
  503.1 33.4 %shard_map.256 = (f32[128,2304]{1,0:T(8,128)S(1)}, bf16[2,144,2304]{2,1,0:T(8,128)(2,1)S(1)}) custom-call(bf16[4,128,2304]{2,1,0:T(8,128)(2,1)S(1)} %bitcast.46, bf16[4,144,1152]{2,1,0:T(8,128)(2,1)S(1)} %get-tuple-element.77.refs_1_), custom_call_target="tpu_custom_call" | custom-call | bytes 3686400 | tf_op jit(solution)/shard_map/pallas_call | solution.py:1515
  536.5 0.0 copy-start.5
  536.6 0.4 fusion.10
  537.0 1.3 copy-done.30
  538.3 0.2 multiply_reduce_fusion.1
  538.5 0.2 multiply_reduce_fusion.2
  538.6 1.9 multiply_reduce_fusion
  540.5 0.1 reduce_sum.76
  540.7 4.6 convolution_convert_fusion
  545.2 123.4 %shard_map.257 = (bf16[288,1024]{1,0:T(8,128)(2,1)S(1)}, bf16[2,144,2304]{2,1,0:T(8,128)(2,1)S(1)}, bf16[2,144,2304]{2,1,0:T(8,128)(2,1)S(1)}, f32[8,1152]{1,0:T(8,128)S(1)}) custom-call(bf16[4,2,288,1024]{3,2,1,0:T(8,128)(2,1)S(1)} %bitcast.44, bf16[4,2,2,144,2304]{4,3,2,1,0:T(8,128)(2,1)} %bitcast.65, bf16[4,2,2,144,2304]{4,3,2,1,0:T(8,128)(2,1)} %bitcast.66, ...), custom_call_target="tpu_custom_call" | custom-call | bytes 25970688 | tf_op jit(solution)/shard_map/pallas_call | solution.py:1515
  668.7 1.8 bitcast_convert_fusion
  670.4 1.8 bitcast_convert_fusion.1
  672.2 0.8 fusion.14
  673.0 0.9 slice.35
  673.9 0.6 squeeze.12
  674.5 0.6 squeeze.13
  675.1 0.6 squeeze.14
  675.7 0.6 squeeze.15
  676.4 1.8 convert_bitcast_fusion
  678.1 0.9 convert_bitcast_fusion.1
  (66 shorter events, 0.2 us)
Async XLA Ops:
  0.6 4.3 copy-start.31
  2.2 3.8 copy-start.8
  3.6 2.5 copy-start.7
  98.5 4.1 copy-start.1
  102.6 4.0 copy-start.13
  102.6 4.0 copy-start.16
  102.6 4.7 copy-start.12
  106.6 0.7 copy-start.26
  107.3 73.0 %copy-start.28 = (f32[512,128]{1,0:T(8,128)}, f32[512,128]{1,0:T(8,128)S(1)}, u32[]{:S(2)}) copy-start(f32[512,128]{1,0:T(8,128)S(1)} %get-tuple-element.75.sin_ref) | copy-start | bytes 786436
  176.3 3.9 copy-start.2
  180.2 3.8 copy-start.14
  180.2 7.1 %copy-start.17 = (bf16[4,2,288,512]{3,2,1,0:T(8,128)(2,1)}, bf16[4,2,288,512]{3,2,1,0:T(8,128)(2,1)S(1)}, u32[]{:S(2)}) copy-start(bf16[4,2,288,512]{3,2,1,0:T(8,128)(2,1)S(1)} %get-tuple-element.58) | copy-start | bytes 7077892
  184.0 1.0 copy-start.19
  185.0 0.8 copy-start.21
  185.8 1.5 copy-start.23
  185.8 1.5 copy-start.32
  185.8 1.5 copy-start.34
  185.8 1.5 copy-start
  185.8 1.7 copy-start.9
  187.6 33.1 %copy-start.33 = (f32[2304]{0:T(1024)S(1)}, f32[2304]{0:T(1024)}, u32[]{:S(2)}) copy-start(f32[2304]{0:T(1024)} %param.27) | copy-start | bytes 27652
  218.8 1.1 copy-start.4
  219.8 0.8 copy-start.11
  221.3 175.8 %copy-start.3 = (bf16[128,2304]{1,0:T(8,128)(2,1)S(1)}, bf16[128,2304]{1,0:T(8,128)(2,1)}, u32[]{:S(2)}) copy-start(bf16[128,2304]{1,0:T(8,128)(2,1)} %refs_3_.1) | copy-start | bytes 1769476
  397.0 1.3 copy-start.10
  398.3 28.2 %copy-start.24 = (bf16[512,512]{1,0:T(8,128)(2,1)S(1)}, bf16[512,512]{1,0:T(8,128)(2,1)}, u32[]{:S(2)}) copy-start(bf16[512,512]{1,0:T(8,128)(2,1)} %copy-done.23) | copy-start | bytes 1572868
  426.5 1.7 copy-start.18
  426.5 3.0 copy-start.15
  426.6 3.1 copy-start.20
  426.6 3.2 copy-start.22
  428.2 8.4 %slice-start = ((s8[10616832]{0:T(1024)(128)(4,1)}), s8[4194304]{0:T(1024)(128)(4,1)S(1)}, s32[]{:S(2)}) async-start(s8[10616832]{0:T(1024)(128)(4,1)} %bitcast.41), calls=%async_computation | async-start | bytes 8388608
  428.2 8.4 %slice-start.1 = ((s8[10616832]{0:T(1024)(128)(4,1)}), s8[4194304]{0:T(1024)(128)(4,1)S(1)}, s32[]{:S(2)}) async-start(s8[10616832]{0:T(1024)(128)(4,1)} %bitcast.41), calls=%async_computation.1 | async-start | bytes 8388608
  429.8 6.8 %slice-start.2 = ((s8[10616832]{0:T(1024)(128)(4,1)}), s8[2228224]{0:T(1024)(128)(4,1)S(1)}, s32[]{:S(2)}) async-start(s8[10616832]{0:T(1024)(128)(4,1)} %bitcast.41), calls=%async_computation.2 | async-start | bytes 4456448
  429.8 68.6 %slice-start.3 = ((s8[4718592]{0:T(1024)(128)(4,1)}), s8[4194304]{0:T(1024)(128)(4,1)S(1)}, s32[]{:S(2)}) async-start(s8[4718592]{0:T(1024)(128)(4,1)} %bitcast.54), calls=%async_computation.3 | async-start | bytes 8388608
  436.6 61.7 %slice-start.4 = ((s8[4718592]{0:T(1024)(128)(4,1)}), s8[524288]{0:T(1024)(128)(4,1)S(1)}, s32[]{:S(2)}) async-start(s8[4718592]{0:T(1024)(128)(4,1)} %bitcast.54), calls=%async_computation.4 | async-start | bytes 1048576
  436.7 61.7 %copy-start.27 = (f32[512,128]{1,0:T(8,128)S(1)}, f32[512,128]{1,0:T(8,128)}, u32[]{:S(2)}) copy-start(f32[512,128]{1,0:T(8,128)} %copy-done.26) | copy-start | bytes 786436
  436.7 61.7 %copy-start.29 = (f32[512,128]{1,0:T(8,128)S(1)}, f32[512,128]{1,0:T(8,128)}, u32[]{:S(2)}) copy-start(f32[512,128]{1,0:T(8,128)} %copy-done.28) | copy-start | bytes 786436
  503.1 33.5 %copy-start.25 = (bf16[512,1024]{1,0:T(8,128)(2,1)}, bf16[512,1024]{1,0:T(8,128)(2,1)S(1)}, u32[]{:S(2)}) copy-start(bf16[512,1024]{1,0:T(8,128)(2,1)S(1)} %get-tuple-element.79) | copy-start | bytes 3145732
  536.5 1.9 copy-start.5
  536.5 1.8 copy-start.30
  672.2 4.2 copy-start.6
